TPU v7x, 32 devices: a whole 2x2x4 slice. The times are simulated.
32 devices in a mesh: seq: 8 (over z, y), head: 4 (over x, core).
Axes of the slice: x: 2, y: 2, z: 4, core: 2. Of those that a mesh axis runs over, the one named last changes fastest.
Arguments:
- tokens: bfloat16 [8192, 2048], P('seq'), may hold values from -6 to 6
- w_query: bfloat16 [2048, 2048], P(None, 'head'), may hold values from -0.125 to 0.125
- w_key: bfloat16 [2048, 2048], P(None, 'head'), may hold values from -0.125 to 0.125
- w_value: bfloat16 [2048, 2048], P(None, 'head'), may hold values from -0.125 to 0.125
- omega: float32 [128, 256], replicated, may hold values from -5 to 5
- w_out: bfloat16 [2048, 2048], P('head'), may hold values from -0.125 to 0.125
Outputs:
- mixed: bfloat16 [8192, 2048], P(('seq', 'head'))
All inputs are finite; a program needn't handle non-finite values.
Results may differ from a plain program's by a relative error of at most 0.0063.
Values may be sent and summed in bfloat16 or wider, within the bound.
No kernel may reach another device: no remote copies, remote signals or barrier semaphores. Data moves between devices by JAX's collectives and lax.ppermute only.
A program may use at most 128 MiB of HBM per device.

v0:
```python
import math

import jax
import jax.numpy as jnp
from jax import lax
from jax.sharding import PartitionSpec as P

BLOCK = 512


highest_precision = lax.Precision.HIGHEST
stabilizer = 0.001


def prefix(value, axis, join, neutral):
    count, mine = (lax.axis_size(axis), lax.axis_index(axis))
    pieces = jax.tree.map(lambda part: lax.all_gather(part, axis), value)
    so_far = jax.tree.map(
        lambda part, zero: jnp.full_like(part, 0) + jnp.asarray(zero, part.dtype), value, neutral
    )

    def turn(position, so_far):
        longer = join(so_far, jax.tree.map(lambda part: part[position], pieces))
        return jax.tree.map(lambda new, old: jnp.where(position < mine, new, old), longer, so_far)

    return lax.fori_loop(0, count - 1, turn, so_far)


def feature_map(values, omega):
    head_size = omega.shape[0]
    scaled = values * head_size ** (-0.25)
    projected = jnp.einsum("thd,dm->thm", scaled, omega, precision=highest_precision)
    half_square = 0.5 * jnp.sum(scaled * scaled, axis=-1, keepdims=True)
    return ((jnp.exp(projected - half_square) + stabilizer) / math.sqrt(omega.shape[1])).astype(
        jnp.bfloat16
    )


def add_pair(earlier, later):
    return (earlier[0] + later[0], earlier[1] + later[1])


def shards(tokens, w_query, w_key, w_value, omega, w_out):
    tok_rows = tokens.shape[0]
    head_size = omega.shape[0]
    local_heads = w_query.shape[1] // head_size
    query = jnp.dot(tokens, w_query, preferred_element_type=jnp.float32).reshape(
        tok_rows, local_heads, head_size
    )
    key = jnp.dot(tokens, w_key, preferred_element_type=jnp.float32).reshape(
        tok_rows, local_heads, head_size
    )
    value = (
        jnp.dot(tokens, w_value, preferred_element_type=jnp.float32)
        .astype(jnp.bfloat16)
        .reshape(tok_rows, local_heads, head_size)
    )
    query_feat = feature_map(query, omega)
    key_feat = feature_map(key, omega)
    block_count = tok_rows // BLOCK
    block_states = []
    block_norms = []
    for block_index in range(block_count):
        block_keys = key_feat[block_index * BLOCK : (block_index + 1) * BLOCK]
        block_values = value[block_index * BLOCK : (block_index + 1) * BLOCK]
        block_states.append(
            jnp.einsum("xtv,xte->tve", block_keys, block_values, preferred_element_type=jnp.float32)
        )
        block_norms.append(jnp.sum(block_keys, axis=0, dtype=jnp.float32))
    state_total = block_states[0]
    norm_total = block_norms[0]
    block_index = 1
    state_total = state_total + block_states[block_index]
    norm_total = norm_total + block_norms[block_index]
    zero_state = jnp.zeros_like(state_total)
    zero_norm = jnp.zeros_like(norm_total)
    state_prefix, norm_prefix = prefix(
        (state_total, norm_total), "seq", add_pair, (zero_state, zero_norm)
    )
    causal = jnp.arange(BLOCK)[:, None] >= jnp.arange(BLOCK)[None, :]
    cumulative_state = state_prefix
    running_norm = norm_prefix
    outputs = []
    for block_index in range(block_count):
        query_block = query_feat[block_index * BLOCK : (block_index + 1) * BLOCK]
        block_keys = key_feat[block_index * BLOCK : (block_index + 1) * BLOCK]
        block_values = value[block_index * BLOCK : (block_index + 1) * BLOCK]
        scores = jnp.einsum(
            "thm,shm->hts", query_block, block_keys, preferred_element_type=jnp.float32
        )
        scores = jnp.where(causal[None], scores, jnp.float32(0.0))
        query_features = query_block.astype(jnp.float32)
        denom = jnp.sum(scores, axis=-1).T + jnp.einsum(
            "thm,hm->th", query_features, running_norm, precision=highest_precision
        )
        weights = scores.astype(jnp.bfloat16)
        numerator = jnp.einsum(
            "hts,shd->thd", weights, block_values, preferred_element_type=jnp.float32
        )
        numerator = numerator + jnp.einsum(
            "crx,rxs->crs", query_features, cumulative_state, precision=highest_precision
        )
        outputs.append((numerator / denom[..., None]).astype(jnp.bfloat16))
        cumulative_state = cumulative_state + block_states[block_index]
        running_norm = running_norm + block_norms[block_index]
    attention = jnp.concatenate(outputs, axis=0).reshape(tok_rows, local_heads * head_size)
    mixed = lax.psum_scatter(
        jnp.dot(attention, w_out, preferred_element_type=jnp.float32),
        "head",
        scatter_dimension=0,
        tiled=True,
    )
    return mixed.astype(jnp.bfloat16)


def solution(mesh):
    placed = (
        P("seq", None),
        P(None, "head"),
        P(None, "head"),
        P(None, "head"),
        P(),
        P("head", None),
    )
    return jax.shard_map(
        shards, mesh=mesh, in_specs=placed, out_specs=P(("seq", "head"), None), check_vma=False
    )
```

profile of v0, /device:TPU:0, one launch (start us, length us, event | category | flops | bytes accessed | tf_op | source)
XLA Modules:
  0.0 201.5 jit_solution(3377981324147290222)
XLA Ops:
  6.5 5.4 %multiply_reduce_fusion = (f32[1024,4]{0,1:T(4,128)S(1)}, f32[1024,512]{0,1:T(8,128)S(1)}) fusion(bf16[1024,2048]{1,0:T(8,128)(2,1)} %param.8, bf16[2048,512]{1,0:T(8,128)(2,1)} %param.10), kind=kOutput, calls=%fused_computation.14 | convolution fusion | flops 2149052416 | bytes 8404992 | tf_op jit(solution)/shard_map/dot_general | solution.py:50
  12.0 2.4 %convolution_convert_fusion = bf16[1024,512]{0,1:T(8,128)(2,1)S(1)} fusion(bf16[1024,2048]{1,0:T(8,128)(2,1)S(1)} %copy-done.11, bf16[2048,512]{1,0:T(8,128)(2,1)S(1)} %copy-done.12), kind=kOutput, calls=%fused_computation.20 | convolution fusion | flops 2148007936 | bytes 7340032 | tf_op jit(solution)/shard_map/dot_general | solution.py:54
  14.5 0.8 copy-done.14
  15.3 4.7 %multiply_convert_fusion = bf16[1024,4,256]{2,0,1:T(8,128)(2,1)S(1)} fusion(f32[1024,4,128]{0,2,1:T(8,128)S(1)} %bitcast.72, f32[1024,4]{0,1:T(4,128)S(1)} %broadcast_multiply_fusion, f32[128,256]{1,0:T(8,128)S(1)} %copy-done.14), kind=kOutput, calls=%fused_computation.2 | convolution fusion | flops 1614807040 | bytes 4341760 | tf_op jit(solution)/shard_map/thd,dm->thm/dot_general | solution.py:32
  20.6 0.8 copy-done.3
  21.3 1.3 convolution_add_fusion
  22.7 2.0 convert_reduce_fusion
  24.7 32.4 %all-gather.2 = f32[8,4,256]{2,1,0:T(4,128)S(1)} all-gather(f32[1,4,256]{2,1,0:T(4,128)S(1)} %add_bitcast_fusion.1), channel_id=3, replica_groups=mesh['seq'=8,'head'=4] {'seq'}, dimensions={0}, use_global_device_ids=true | all-gather | bytes 36864 | tf_op jit(solution)/shard_map/all_gather | solution.py:17
  57.3 4.7 %multiply_reduce_fusion.1 = (f32[1024,4]{0,1:T(4,128)S(1)}, f32[1024,512]{0,1:T(8,128)S(1)}) fusion(bf16[1024,2048]{1,0:T(8,128)(2,1)} %param.8, bf16[2048,512]{1,0:T(8,128)(2,1)S(1)} %copy-done.13), kind=kOutput, calls=%fused_computation.15 | convolution fusion | flops 2149052416 | bytes 8404992 | tf_op jit(solution)/shard_map/dot_general | solution.py:47
  62.0 4.9 %multiply_convert_fusion.1 = bf16[1024,4,256]{2,0,1:T(8,128)(2,1)S(1)} fusion(f32[1024,4,128]{0,2,1:T(8,128)S(1)} %bitcast.73, f32[1024,4]{0,1:T(4,128)S(1)} %broadcast_multiply_fusion.1, f32[128,256]{1,0:T(8,128)S(1)} %copy-done.15), kind=kOutput, calls=%fused_computation.3 | convolution fusion | flops 1614807040 | bytes 4341760 | tf_op jit(solution)/shard_map/thd,dm->thm/dot_general | solution.py:32
  66.9 0.7 fusion.18
  67.7 0.6 copy-done.1
  68.2 2.0 copy-done.5
  70.2 2.5 %select_reduce_fusion.1 = (f32[4,512]{1,0:T(4,128)S(1)}, f32[4,512]{1,0:T(4,128)S(1)}, bf16[4,512,512]{1,2,0:T(8,128)(2,1)}) fusion(pred[512,512]{0,1:T(8,128)(4,1)S(1)} %iota_compare_fusion, f32[4,512,512]{1,2,0:T(8,128)S(1)} %fusion.18, bf16[1024,4,256]{2,0,1:T(8,128)(2,1)S(1)} %copy-done.4, bf16[1024,4,256]{2,0,1:T(8,128)(2,1)S(1)} %multiply_convert_fusion.1), kind=kOutput, calls=%fused_computation.6 | convolution fusion | flops 542109696 | bytes 8667136 | tf_op jit(solution)/shard_map/thm,shm->hts/dot_general | solution.py:88
  72.7 26.4 %all-gather.5.cloned.1.call-done = f32[32,256,128]{2,1,0:T(8,128)} async-done(((f32[4,256,128]{2,1,0:T(8,128)}), f32[32,256,128]{2,1,0:T(8,128)}) %all-gather.5.cloned.1.call-update) | async-done | bytes 4194320 | tf_op jit(solution)/shard_map/all_gather | solution.py:17
  99.1 8.8 %while.16 = (s32[]{:T(128)}, f32[4,256,128]{2,1,0:T(8,128)S(1)}, f32[4,256]{1,0:T(4,128)S(1)}, s32[]{:T(128)}, f32[8,4,256,128]{3,2,1,0:T(8,128)}, /*index=5*/f32[8,4,256]{2,1,0:T(4,128)S(1)}, s32[]{:T(128)}, s32[]{:T(128)}) while((s32[]{:T(128)}, f32[4,256,128]{2,1,0:T(8,128)S(1)}, f32[4,256]{1,0:T(4,128)S(1)}, s32[]{:T(128)}, ...), condition=%wide.region_5.6_spmd.clone, body=%wide.region_4.5_spmd.clone.sunk | while | flops 396292 | bytes 1585267 | solution.py:26
  99.1 1.2 add_select_fusion.4
  100.3 1.2 add_select_fusion.4
  101.6 1.2 add_select_fusion.4
  102.9 1.2 add_select_fusion.4
  104.1 1.2 add_select_fusion.4
  105.4 1.2 add_select_fusion.4
  106.7 1.2 add_select_fusion.4
  107.9 2.6 %fusion.28 = f32[4,128,512]{2,1,0:T(8,128)S(1)} fusion(f32[4,256,128]{2,1,0:T(8,128)S(1)} %get-tuple-element.115, bf16[1024,4,256]{2,0,1:T(8,128)(2,1)} %copy-done.1), kind=kOutput, calls=%fused_computation.46 | convolution fusion | flops 805306368 | bytes 2621440 | tf_op jit(solution)/shard_map/crx,rxs->crs/dot_general | solution.py:100
  110.6 1.2 fusion.16
  111.8 0.9 fusion.14
  112.7 0.9 fusion.26
  113.7 0.6 fusion.13
  114.7 0.7 copy-done.16
  116.1 5.6 %fusion.41 = f32[1024,2048]{1,0:T(8,128)} fusion(bf16[1024,512]{0,1:T(8,128)(2,1)S(1)} %bitcast.70, bf16[512,2048]{1,0:T(8,128)(2,1)S(1)} %copy-done), kind=kOutput, calls=%fused_computation.65 | convolution fusion | flops 2147483648 | bytes 11534336 | tf_op jit(solution)/shard_map/dot_general | solution.py:108
  121.8 70.1 %reduce-scatter.2.cloned.1.call-done = f32[256,2048]{1,0:T(8,128)} async-done(((f32[1024,2048]{1,0:T(8,128)}), f32[256,2048]{1,0:T(8,128)}) %reduce-scatter.2.cloned.1.call-update) | async-done | bytes 2097168 | tf_op jit(solution)/shard_map/reduce_scatter | solution.py:107
  191.9 2.7 %convert_element_type.41 = bf16[256,2048]{1,0:T(8,128)(2,1)} convert(f32[256,2048]{1,0:T(8,128)} %reduce-scatter.2.cloned.1.call-done) | non-fusion elementwise | flops 524288 | bytes 3145728 | tf_op jit(solution)/shard_map/convert_element_type | solution.py:113
  (52 shorter events, 2.0 us)
Async XLA Ops:
  6.5 109.6 %copy-start = (bf16[512,2048]{1,0:T(8,128)(2,1)S(1)}, bf16[512,2048]{1,0:T(8,128)(2,1)}, u32[]{:S(2)}) copy-start(bf16[512,2048]{1,0:T(8,128)(2,1)} %param.13) | copy-start | bytes 6291460
  6.5 92.6 %all-gather.5.cloned.1.call-start = ((), (), s32[]{:S(2)}) async-start(), calls=%async_computation.2 | async-start | bytes 4718592 | tf_op jit(solution)/shard_map/all_gather | solution.py:17
  6.5 5.4 %copy-start.11 = (bf16[1024,2048]{1,0:T(8,128)(2,1)S(1)}, bf16[1024,2048]{1,0:T(8,128)(2,1)}, u32[]{:S(2)}) copy-start(bf16[1024,2048]{1,0:T(8,128)(2,1)} %param.8) | copy-start | bytes 12582916
  6.5 5.4 %copy-start.12 = (bf16[2048,512]{1,0:T(8,128)(2,1)S(1)}, bf16[2048,512]{1,0:T(8,128)(2,1)}, u32[]{:S(2)}) copy-start(bf16[2048,512]{1,0:T(8,128)(2,1)} %param.11) | copy-start | bytes 6291460
  14.4 0.9 copy-start.14
  14.5 5.5 %copy-start.9 = (bf16[512,512]{0,1:T(8,128)(2,1)}, bf16[512,512]{0,1:T(8,128)(2,1)S(1)}, u32[]{:S(2)}) copy-start(bf16[512,512]{0,1:T(8,128)(2,1)S(1)} %get-tuple-element.155) | copy-start | bytes 1572868
  14.5 6.0 %copy-start.7 = (bf16[512,512]{0,1:T(8,128)(2,1)}, bf16[512,512]{0,1:T(8,128)(2,1)S(1)}, u32[]{:S(2)}) copy-start(bf16[512,512]{0,1:T(8,128)(2,1)S(1)} %get-tuple-element.154) | copy-start | bytes 1572868
  20.0 1.3 copy-start.3
  22.7 169.3 %reduce-scatter.2.cloned.1.call-start = ((), (), s32[]{:S(2)}) async-start(), calls=%async_computation.1 | async-start | bytes 10485760 | tf_op jit(solution)/shard_map/reduce_scatter | solution.py:107
  22.7 34.5 %copy-start.13 = (bf16[2048,512]{1,0:T(8,128)(2,1)S(1)}, bf16[2048,512]{1,0:T(8,128)(2,1)}, u32[]{:S(2)}) copy-start(bf16[2048,512]{1,0:T(8,128)(2,1)} %param.9) | copy-start | bytes 6291460
  57.3 4.7 %copy-start.15 = (f32[128,256]{1,0:T(8,128)S(1)}, f32[128,256]{1,0:T(8,128)}, u32[]{:S(2)}) copy-start(f32[128,256]{1,0:T(8,128)} %param.12) | copy-start | bytes 393220
  62.0 4.9 %copy-start.4 = (bf16[1024,4,256]{2,0,1:T(8,128)(2,1)S(1)}, bf16[1024,4,256]{2,0,1:T(8,128)(2,1)}, u32[]{:S(2)}) copy-start(bf16[1024,4,256]{2,0,1:T(8,128)(2,1)} %copy-done.3) | copy-start | bytes 6291460
  66.9 1.3 copy-start.1
  68.2 2.0 copy-start.5
  107.9 2.6 %copy-start.2 = (bf16[1024,4,256]{2,0,1:T(8,128)(2,1)S(1)}, bf16[1024,4,256]{2,0,1:T(8,128)(2,1)}, u32[]{:S(2)}) copy-start(bf16[1024,4,256]{2,0,1:T(8,128)(2,1)} %copy-done.1) | copy-start | bytes 6291460
  110.5 3.2 %copy-start.6 = (f32[4,512,512]{1,2,0:T(8,128)S(1)}, f32[4,512,512]{1,2,0:T(8,128)}, u32[]{:S(2)}) copy-start(f32[4,512,512]{1,2,0:T(8,128)} %copy-done.5) | copy-start | bytes 12582916
  110.5 3.2 %copy-start.8 = (bf16[512,512]{0,1:T(8,128)(2,1)S(1)}, bf16[512,512]{0,1:T(8,128)(2,1)}, u32[]{:S(2)}) copy-start(bf16[512,512]{0,1:T(8,128)(2,1)} %copy-done.7) | copy-start | bytes 1572868
  113.7 1.0 copy-start.10
  113.7 1.8 copy-start.16
Sparse Core Ops, SparseCore 0:
  22.8 76.2 all-gather.4
  121.9 69.9 reduce-scatter.1
where the time goes:
time: 202 us; the launch traced here: 201 us
  waiting for transfers between devices  96.6 us (48%)
  matrix products  39.5 us (20%)
  blocking collectives  32.4 us (16%)
  between operations  13.8 us (7%)
  other arithmetic  13.6 us (7%)
  local copies, waits for them, and re-layouts  5.41 us (3%)
    reduce_scatter x1, waiting for transfers between devices, shards(): lax.psum_scatter(jnp.dot(attention, w_out, preferred_element_type=jnp.flo...  70.1 us
    all_gather x1, blocking collectives, prefix(): pieces = jax.tree.map(lambda part: lax.all_gather(part, axis), value)  32.4 us
    all_gather x1, waiting for transfers between devices, prefix(): pieces = jax.tree.map(lambda part: lax.all_gather(part, axis), value)  26.4 us
    dot_general x2, matrix products, feature_map(): jnp.einsum('thd,dm->thm', scaled, omega, precision=highest_precision)  9.57 us
    select_n x14, other arithmetic, turn(): jnp.where(position < mine, new, old)  8.64 us
    dot_general x1, matrix products, shards(): jnp.dot(attention, w_out, preferred_element_type=jnp.float32)  5.62 us
    dot_general x1, matrix products, shards(): jnp.dot(tokens, w_key, preferred_element_type=jnp.float32)  5.39 us
    unnamed x34, local copies, waits for them, and re-layouts  5.33 us
  transfers between devices with their start and end apart: 2, of which 2 were waited for; matrix products, arithmetic and copies ran while one was open for 7% of the time, Pallas kernels for 0%

commit v1 on v0

v1 whole, which is shorter than its diff:
```python
import functools
import math

import jax
import jax.numpy as jnp
from jax import lax
from jax.experimental import pallas as pl
from jax.experimental.pallas import tpu as pltpu
from jax.sharding import PartitionSpec as P

BLOCK = 512
TAIL = 16
STABILIZER = 0.001
BF16 = jnp.bfloat16
F32 = jnp.float32


def params(mib):
    return pltpu.CompilerParams(vmem_limit_bytes=mib * 2**20)


def dot(a, b):
    return lax.dot_general(a, b, (((1,), (0,)), ((), ())), preferred_element_type=F32)


def dot_nt(a, b):
    return lax.dot_general(a, b, (((1,), (1,)), ((), ())), preferred_element_type=F32)


def dot_tn(a, b):
    return lax.dot_general(a, b, (((0,), (0,)), ((), ())), preferred_element_type=F32)


def halves(value):
    high = value.astype(BF16)
    return high, (value - high.astype(F32)).astype(BF16)


def feature_weights(omega):
    size, features = omega.shape
    high, low = halves(omega * size ** (-0.25))
    minus = jnp.full((2 * size, features), -1.0, BF16)
    return jnp.concatenate([high, high, low, low, minus], axis=0)


def features(rows, weights):
    size = rows.shape[1]
    high, low = halves(rows)
    square_high, square_low = halves(rows * rows * (0.5 * size ** (-0.5)))
    left = jnp.concatenate([high, low, high, low, square_high, square_low], axis=1)
    exponent = dot(left, weights)
    return ((jnp.exp(exponent) + STABILIZER) * (1.0 / math.sqrt(weights.shape[1]))).astype(BF16)


def key_kernel(tok, wk, wv, omega, feat, value, state, message, local):
    block = pl.program_id(1)
    size = omega.shape[0]
    weights = feature_weights(omega[...])
    keys = dot(tok[...], wk[...])
    values = dot(tok[...], wv[...]).astype(BF16)
    value[...] = values
    for j in range(feat.shape[0]):
        f = features(keys[:, j * size : (j + 1) * size], weights)
        feat[j] = f
        outer = dot_tn(values[:, j * size : (j + 1) * size], f)
        norm = jnp.sum(f.astype(F32), axis=0, keepdims=True)
        added = jnp.concatenate([outer, norm, jnp.zeros((TAIL - 1, f.shape[1]), F32)], axis=0)

        @pl.when(block == 0)
        def _():
            state[j] = added

        @pl.when(block > 0)
        def _():
            state[j] += added

        total = state[j]
        norm = total[size : size + 1]
        high, low = halves(norm)
        message[j] = jnp.concatenate(
            [total[:size].astype(BF16), high, low, jnp.zeros((TAIL - 2, f.shape[1]), BF16)], axis=0
        )
        local[0, j] = jnp.concatenate(
            [total[:size].astype(BF16), jnp.broadcast_to(high, (size, f.shape[1]))], axis=0
        )


def query_kernel(tok, wq, omega, feat, value, local, qfeat, result):
    block = pl.program_id(1)
    size = omega.shape[0]
    rows = tok.shape[0]
    half = rows // 2
    weights = feature_weights(omega[...])
    query = dot(tok[...], wq[...])
    causal = lax.broadcasted_iota(jnp.int32, (half, half), 0) >= lax.broadcasted_iota(
        jnp.int32, (half, half), 1
    )
    for j in range(qfeat.shape[0]):
        f = features(query[:, j * size : (j + 1) * size], weights)
        qfeat[j] = f
        k = feat[j]
        v = jnp.concatenate([value[:, j * size : (j + 1) * size], jnp.ones((rows, size), BF16)], axis=1)
        top = jnp.where(causal, dot_nt(f[:half], k[:half]), 0.0).astype(BF16)
        left = dot_nt(f[half:], k[:half]).astype(BF16)
        right = jnp.where(causal, dot_nt(f[half:], k[half:]), 0.0).astype(BF16)
        upper = dot(top, v[:half])
        lower = dot(jnp.concatenate([left, right], axis=1), v)
        out = jnp.concatenate([upper, lower], axis=0)
        columns = slice(j * 2 * size, (j + 1) * 2 * size)

        @pl.when(block == 0)
        def _():
            result[:, columns] = out

        @pl.when(block > 0)
        def _():
            result[:, columns] = out + dot_nt(f, local[0, j])


def finish_kernel(qfeat, result, prefix, attention):
    size = attention.shape[1] // qfeat.shape[0]
    for j in range(qfeat.shape[0]):
        p = prefix[j]
        norm = p[size : size + 1].astype(F32) + p[size + 1 : size + 2].astype(F32)
        right = jnp.concatenate([p[:size], jnp.broadcast_to(norm.astype(BF16), (size, p.shape[1]))], axis=0)
        r = result[:, j * 2 * size : (j + 1) * 2 * size] + dot_nt(qfeat[j], right)
        attention[:, j * size : (j + 1) * size] = (r[:, :size] / r[:, size:]).astype(BF16)


def out_kernel(count, *refs):
    total = None
    for a, w in zip(refs[:count], refs[count : 2 * count]):
        term = dot(a[...], w[...])
        total = term if total is None else total + term
    if len(refs) == 2 * count + 2:
        total = total + refs[2 * count][...]
    refs[-1][...] = total.astype(refs[-1].dtype)


def out_product(lefts, rights, partial, dtype):
    count = len(lefts)
    rows, columns = lefts[0].shape[0], rights[0].shape[1]
    width = min(512, columns)
    specs = [pl.BlockSpec(a.shape, lambda i: (0, 0)) for a in lefts]
    specs += [pl.BlockSpec((w.shape[0], width), lambda i: (0, i)) for w in rights]
    operands = list(lefts) + list(rights)
    if partial is not None:
        specs.append(pl.BlockSpec((rows, width), lambda i: (0, i)))
        operands.append(partial)
    depth = sum(a.shape[1] for a in lefts)
    return pl.pallas_call(
        functools.partial(out_kernel, count),
        grid=(columns // width,),
        in_specs=specs,
        out_specs=pl.BlockSpec((rows, width), lambda i: (0, i)),
        out_shape=jax.ShapeDtypeStruct((rows, columns), dtype),
        compiler_params=params(32),
        cost_estimate=pl.CostEstimate(
            flops=2 * rows * columns * depth, bytes_accessed=2 * columns * depth, transcendentals=0
        ),
    )(*operands)


def swap(value, axis, bit):
    count = lax.axis_size(axis)
    return lax.ppermute(value, axis, [(i, i ^ bit) for i in range(count)])


def pack(total, size):
    high = lax.reduce_precision(total, 8, 7)
    low = total[:, size : size + 1] - high[:, size : size + 1]
    return jnp.concatenate(
        [high[:, : size + 1], low, jnp.zeros_like(total[:, : TAIL - 2])], axis=1
    ).astype(BF16)


def unpack(message, size):
    wide = message.astype(F32)
    return jnp.concatenate(
        [wide[:, :size], wide[:, size : size + 1] + wide[:, size + 1 : size + 2], jnp.zeros_like(wide[:, : TAIL - 1])],
        axis=1,
    )


def prefix(total, message, size):
    count = lax.axis_size("seq")
    mine = lax.axis_index("seq")
    side = mine % 2
    group = total.shape[0] // 2
    own = lax.dynamic_slice_in_dim(total, side * group, group, 0)
    other = lax.dynamic_slice_in_dim(message, (1 - side) * group, group, 0)
    received = unpack(swap(other, "seq", 1), size)
    pair = own + received
    earlier = jnp.zeros_like(pair)
    step = 2
    while step < count:
        sent = pack(pair + earlier, size)
        earlier = earlier + unpack(
            lax.ppermute(sent, "seq", [(i, i + step) for i in range(count - step)]), size
        )
        step *= 2
    even = side == 0
    kept = pack(earlier + jnp.where(even, 0.0, received), size)
    handed = swap(pack(earlier + jnp.where(even, own, 0.0), size), "seq", 1)
    return jnp.concatenate([jnp.where(even, kept, handed), jnp.where(even, handed, kept)], axis=0)


def shards(tokens, w_query, w_key, w_value, omega, w_out):
    rows, width = tokens.shape
    size, feats = omega.shape
    heads = w_query.shape[1] // size
    blocks = rows // BLOCK
    pairs = heads // 2
    seq_side = lax.axis_index("seq") % 2
    head_at = lax.axis_index("head")

    half = w_out.shape[0] // 2
    piece = half // 2
    w_core = swap(w_out, "head", 1)
    near, far = [], []
    for i in range(2):
        sent = lax.dynamic_slice_in_dim(w_out, seq_side * half + i * piece, piece, 0)
        near.append(swap(sent, "head", 2))
    for i in range(2):
        far.append(swap(near[i], "seq", 1))

    row_spec = pl.BlockSpec((BLOCK, width), lambda p, b: (b, 0))
    weight_spec = pl.BlockSpec((width, 2 * size), lambda p, b: (0, p))
    omega_spec = pl.BlockSpec((size, feats), lambda p, b: (0, 0))
    feat_spec = pl.BlockSpec((2, BLOCK, feats), lambda p, b: (p, b, 0))
    value_spec = pl.BlockSpec((BLOCK, 2 * size), lambda p, b: (b, p))
    state_spec = pl.BlockSpec((2, size + TAIL, feats), lambda p, b: (p, 0, 0))
    key_feat, value, total, message, local = pl.pallas_call(
        key_kernel,
        grid=(pairs, blocks),
        in_specs=[row_spec, weight_spec, weight_spec, omega_spec],
        out_specs=[
            feat_spec,
            value_spec,
            state_spec,
            state_spec,
            pl.BlockSpec((1, 2, 2 * size, feats), lambda p, b: (b, p, 0, 0)),
        ],
        out_shape=[
            jax.ShapeDtypeStruct((heads, rows, feats), BF16),
            jax.ShapeDtypeStruct((rows, heads * size), BF16),
            jax.ShapeDtypeStruct((heads, size + TAIL, feats), F32),
            jax.ShapeDtypeStruct((heads, size + TAIL, feats), BF16),
            jax.ShapeDtypeStruct((blocks, heads, 2 * size, feats), BF16),
        ],
        compiler_params=params(40),
        cost_estimate=pl.CostEstimate(
            flops=6 * 10**9, bytes_accessed=12 * 2**20, transcendentals=heads * rows * feats
        ),
        name="keys",
    )(tokens, w_key, w_value, omega)

    query_feat, result = pl.pallas_call(
        query_kernel,
        grid=(pairs, blocks),
        in_specs=[
            row_spec,
            weight_spec,
            omega_spec,
            feat_spec,
            value_spec,
            pl.BlockSpec((1, 2, 2 * size, feats), lambda p, b: (jnp.maximum(b - 1, 0), p, 0, 0)),
        ],
        out_specs=[feat_spec, pl.BlockSpec((BLOCK, 4 * size), lambda p, b: (b, p))],
        out_shape=[
            jax.ShapeDtypeStruct((heads, rows, feats), BF16),
            jax.ShapeDtypeStruct((rows, heads * 2 * size), F32),
        ],
        compiler_params=params(40),
        cost_estimate=pl.CostEstimate(
            flops=6 * 10**9, bytes_accessed=12 * 2**20, transcendentals=heads * rows * feats
        ),
        name="queries",
    )(tokens, w_query, omega, key_feat, value, local)

    earlier = prefix(total, message, size)

    attention = pl.pallas_call(
        finish_kernel,
        grid=(pairs, blocks),
        in_specs=[
            feat_spec,
            pl.BlockSpec((BLOCK, 4 * size), lambda p, b: (b, p)),
            state_spec,
        ],
        out_specs=value_spec,
        out_shape=jax.ShapeDtypeStruct((rows, heads * size), BF16),
        compiler_params=params(32),
        cost_estimate=pl.CostEstimate(
            flops=4 * rows * heads * size * feats, bytes_accessed=7 * 2**20, transcendentals=0
        ),
        name="finish",
    )(query_feat, result, earlier)

    share = rows // lax.axis_size("head")

    def part(bit):
        return lax.dynamic_slice_in_dim(attention, (head_at ^ bit) * share, share, 0)

    from_x = swap(part(2), "head", 2)
    from_diagonal = swap(swap(part(3), "head", 2), "head", 1)
    from_core = swap(part(1), "head", 1)
    near = jnp.concatenate(near, axis=0)
    far = jnp.concatenate(far, axis=0)
    core_near = swap(near, "head", 1)
    core_far = swap(far, "head", 1)

    first = out_product([part(0), from_core], [w_out, w_core], None, F32)

    def columns(value, side):
        return lax.dynamic_slice_in_dim(value, side * half, half, 1)

    return out_product(
        [
            columns(from_x, seq_side),
            columns(from_x, 1 - seq_side),
            columns(from_diagonal, seq_side),
            columns(from_diagonal, 1 - seq_side),
        ],
        [near, far, core_near, core_far],
        first,
        BF16,
    )


def solution(mesh):
    placed = (
        P("seq", None),
        P(None, "head"),
        P(None, "head"),
        P(None, "head"),
        P(),
        P("head", None),
    )
    return jax.shard_map(
        shards, mesh=mesh, in_specs=placed, out_specs=P(("seq", "head"), None), check_vma=False
    )
```

time: 202 us -> 114 us (0.56)
  waiting for transfers between devices: 96.6 us -> 34.7 us
  matrix products: 39.5 us -> 0 us
  Pallas kernels: 0 us -> 36.1 us
  blocking collectives: 32.4 us -> 0 us
  starting transfers between devices: 0.04 us -> 19.8 us
  local copies, waits for them, and re-layouts: 5.41 us -> 21.8 us
  between operations: 13.8 us -> 0.45 us
  other arithmetic: 13.6 us -> 0.93 us
    reduce_scatter x1 -> x0, waiting for transfers between devices: 70.1 us -> none  [shards(): lax.psum_scatter(jnp.dot(attention, w_out, preferred_element_type=jnp.flo...]
    dot_general x16 -> x0, matrix products: 39.5 us -> none  [the longest x2 9.57 us: feature_map(): jnp.einsum('thd,dm->thm', scaled, omega, precision=highest_precision)]
    pallas_call x0 -> x5, Pallas kernels: none -> 36.1 us  [the longest x1 14.9 us: shards(): pl.pallas_call(query_kernel, grid=(pairs, blocks), in_specs=[row_spec, we...]
    ppermute x0 -> x15, waiting for transfers between devices: none -> 34.7 us  [the longest x13 34.7 us: swap(): return lax.ppermute(value, axis, [(i, i ^ bit) for i in range(count)])]
    all_gather x1 -> x0, blocking collectives: 32.4 us -> none  [prefix(): pieces = jax.tree.map(lambda part: lax.all_gather(part, axis), value)]
    all_gather x1 -> x0, waiting for transfers between devices: 26.4 us -> none  [prefix(): pieces = jax.tree.map(lambda part: lax.all_gather(part, axis), value)]
    ppermute x0 -> x15, starting transfers between devices: none -> 19.8 us  [the longest x13 10.9 us: swap(): return lax.ppermute(value, axis, [(i, i ^ bit) for i in range(count)])]
    unnamed x34 -> x38, local copies, waits for them, and re-layouts: 5.33 us -> 15.7 us
  transfers between devices with their start and end apart: 2 -> 15, of which waited for: 2 -> 6; matrix products, arithmetic and copies ran while one was open for 7% -> 8% of each run, Pallas kernels for 0% -> 18%
where the time goes in v1:
time: 114 us
  Pallas kernels  36.1 us (32%)
  waiting for transfers between devices  34.7 us (30%)
  local copies, waits for them, and re-layouts  21.8 us (19%)
  starting transfers between devices  19.8 us (17%)
    ppermute x13, waiting for transfers between devices, swap(): return lax.ppermute(value, axis, [(i, i ^ bit) for i in range(count)])  34.7 us
    unnamed x38, local copies, waits for them, and re-layouts  15.7 us
    pallas_call x1, Pallas kernels, shards(): pl.pallas_call(query_kernel, grid=(pairs, blocks), in_specs=[row_spec, we...  14.9 us
    ppermute x13, starting transfers between devices, swap(): return lax.ppermute(value, axis, [(i, i ^ bit) for i in range(count)])  10.9 us
    pallas_call x1, Pallas kernels, shards(): pl.pallas_call(key_kernel, grid=(pairs, blocks), in_specs=[row_spec, weig...  10.9 us
    ppermute x2, starting transfers between devices, prefix(): lax.ppermute(sent, 'seq', [(i, i + step) for i in range(count - step)])  8.89 us
    pallas_call x2, Pallas kernels, out_product(): pl.pallas_call(functools.partial(out_kernel, count), grid=(columns // wid...  8.4 us
  transfers between devices with their start and end apart: 15, of which 6 were waited for; matrix products, arithmetic and copies ran while one was open for 8% of the time, Pallas kernels for 18%

profile of v1, /device:TPU:0, one launch (start us, length us, event | category | flops | bytes accessed | tf_op | source)
XLA Modules:
  0.0 113.8 jit_solution(3581740658814597393)
XLA Ops:
  0.0 2.2 %copy-done.5 = bf16[1024,2048]{1,0:T(8,128)(2,1)S(1)} copy-done((bf16[1024,2048]{1,0:T(8,128)(2,1)S(1)}, bf16[1024,2048]{1,0:T(8,128)(2,1)}, u32[]{:S(2)}) %copy-start.5) | copy-done | bytes 4194328
  2.2 1.6 %copy-done.6 = bf16[2048,512]{1,0:T(8,128)(2,1)S(1)} copy-done((bf16[2048,512]{1,0:T(8,128)(2,1)S(1)}, bf16[2048,512]{1,0:T(8,128)(2,1)}, u32[]{:S(2)}) %copy-start.6) | copy-done | bytes 2097176
  3.8 1.6 %copy-done.7 = bf16[2048,512]{1,0:T(8,128)(2,1)S(1)} copy-done((bf16[2048,512]{1,0:T(8,128)(2,1)S(1)}, bf16[2048,512]{1,0:T(8,128)(2,1)}, u32[]{:S(2)}) %copy-start.7) | copy-done | bytes 2097176
  5.4 0.9 copy-done.9
  6.3 10.9 %keys.1 = (bf16[4,1024,256]{2,1,0:T(8,128)(2,1)S(1)}, bf16[1024,512]{1,0:T(8,128)(2,1)S(1)}, f32[4,144,256]{2,1,0:T(8,128)S(1)}, bf16[4,144,256]{2,1,0:T(8,128)(2,1)S(1)}, bf16[2,4,256,256]{3,2,1,0:T(8,128)(2,1)S(1)}) custom-call(bf16[1024,2048]{1,0:T(8,128)(2,1)S(1)} %copy-done.5, bf16[2048,512]{1,0:T(8,128)(2,1)S(1)} %copy-done.6, ...), custom_call_target="tpu_custom_call" | custom-call | flops 6000000000 | bytes 12582912 | tf_op jit(solution)/shard_map/keys/pallas_call | solution.py:233
  17.2 1.4 %copy-done.11 = bf16[4,1024,256]{2,1,0:T(8,128)(2,1)} copy-done((bf16[4,1024,256]{2,1,0:T(8,128)(2,1)}, bf16[4,1024,256]{2,1,0:T(8,128)(2,1)S(1)}, u32[]{:S(2)}) %copy-start.11) | copy-done | bytes 2097176
  18.5 1.0 copy-done.13
  19.5 1.0 copy-done.15
  20.5 3.0 %collective-permute-start = (bf16[2,144,256]{2,1,0:T(8,128)(2,1)S(1)}, bf16[2,144,256]{2,1,0:T(8,128)(2,1)S(1)}, u32[]{:S(2)}, u32[]{:S(2)}) collective-permute-start(bf16[2,144,256]{2,1,0:T(8,128)(2,1)S(1)} %constant_dynamic-slice_fusion.10), channel_id=1, source_target_pairs={{0,4},{4,0},{8,12},{12,8},{16,20},{20,16},{24,28},{28,24},{1,5},{5... | collective-permute-start | bytes 442376 | tf_op jit(solution)/shard_map/ppermute | solution.py:166
  23.7 3.7 %collective-permute-done = bf16[2,144,256]{2,1,0:T(8,128)(2,1)S(1)} collective-permute-done((bf16[2,144,256]{2,1,0:T(8,128)(2,1)S(1)}, bf16[2,144,256]{2,1,0:T(8,128)(2,1)S(1)}, u32[]{:S(2)}, u32[]{:S(2)}) %collective-permute-start) | collective-permute-done | bytes 147488 | tf_op jit(solution)/shard_map/ppermute | solution.py:166
  27.8 4.0 %collective-permute-start.1 = (bf16[2,144,256]{2,1,0:T(8,128)(2,1)S(1)}, bf16[2,144,256]{2,1,0:T(8,128)(2,1)S(1)}, u32[]{:S(2)}, u32[]{:S(2)}) collective-permute-start(bf16[2,144,256]{2,1,0:T(8,128)(2,1)S(1)} %maximum_maximum_fusion.2), channel_id=1, source_target_pairs={{0,8},{4,12},{8,16},{12,20},{16,24},{20,28},{1,9},{5,13},{9,17},{1... | collective-permute-start | bytes 442376 | tf_op jit(solution)/shard_map/ppermute | solution.py:199
  31.7 1.1 constant_dynamic-slice_fusion.2
  32.8 1.5 %collective-permute-start.7 = (bf16[128,2048]{1,0:T(8,128)(2,1)}, bf16[128,2048]{1,0:T(8,128)(2,1)}, u32[]{:S(2)}, u32[]{:S(2)}) collective-permute-start(bf16[128,2048]{1,0:T(8,128)(2,1)} %get-tuple-element.28), channel_id=1, source_target_pairs={{0,2},{1,3},{2,0},{3,1},{4,6},{5,7},{6,4},{7,5},{8,10},{9,11},{10,... | collective-permute-start | bytes 1572872 | tf_op jit(solution)/shard_map/ppermute | solution.py:166
  35.2 4.9 %collective-permute-start.2 = (bf16[2,144,256]{2,1,0:T(8,128)(2,1)S(1)}, bf16[2,144,256]{2,1,0:T(8,128)(2,1)S(1)}, u32[]{:S(2)}, u32[]{:S(2)}) collective-permute-start(bf16[2,144,256]{2,1,0:T(8,128)(2,1)S(1)} %maximum_maximum_fusion.3), channel_id=1, source_target_pairs={{0,16},{4,20},{8,24},{12,28},{1,17},{5,21},{9,25},{13,29},{2,18},{... | collective-permute-start | bytes 442376 | tf_op jit(solution)/shard_map/ppermute | solution.py:199
  40.2 14.9 %queries.1 = (bf16[4,1024,256]{2,1,0:T(8,128)(2,1)S(1)}, f32[1024,1024]{1,0:T(8,128)S(1)}) custom-call(bf16[1024,2048]{1,0:T(8,128)(2,1)} %tok.3, bf16[2048,512]{1,0:T(8,128)(2,1)S(1)} %copy-done.8, f32[128,256]{1,0:T(8,128)S(1)} %copy-done.10, bf16[4,1024,256]{2,1,0:T(8,128)(2,1)S(1)} %copy-done.12, bf16[1024,512]{1,0:T(8,128)(2,1)S(1)} %copy-done.14, ...), custom_call_target="tpu_custom_call" | custom-call | flops 6000000000 | bytes 12582912 | tf_op jit(solution)/shard_map/queries/pallas_call | solution.py:258
  55.1 2.0 %copy-done.1 = f32[1024,1024]{1,0:T(8,128)} copy-done((f32[1024,1024]{1,0:T(8,128)}, f32[1024,1024]{1,0:T(8,128)S(1)}, u32[]{:S(2)}) %copy-start.1) | copy-done | bytes 4194328
  57.0 1.4 %copy-done.3 = bf16[4,1024,256]{2,1,0:T(8,128)(2,1)} copy-done((bf16[4,1024,256]{2,1,0:T(8,128)(2,1)}, bf16[4,1024,256]{2,1,0:T(8,128)(2,1)S(1)}, u32[]{:S(2)}) %copy-start.3) | copy-done | bytes 2097176
  58.8 1.6 %collective-permute-start.3 = (bf16[2,144,256]{2,1,0:T(8,128)(2,1)S(1)}, bf16[2,144,256]{2,1,0:T(8,128)(2,1)S(1)}, u32[]{:S(2)}, u32[]{:S(2)}) collective-permute-start(bf16[2,144,256]{2,1,0:T(8,128)(2,1)S(1)} %maximum_maximum_fusion.5), channel_id=1, source_target_pairs={{0,4},{4,0},{8,12},{12,8},{16,20},{20,16},{24,28},{28,24},{1,5},{5... | collective-permute-start | bytes 442376 | tf_op jit(solution)/shard_map/ppermute | solution.py:166
  61.0 1.1 constant_dynamic-update-slice_fusion.1
  62.2 1.6 %collective-permute-start.10 = (bf16[128,2048]{1,0:T(8,128)(2,1)}, bf16[128,2048]{1,0:T(8,128)(2,1)S(1)}, u32[]{:S(2)}, u32[]{:S(2)}) collective-permute-start(bf16[128,2048]{1,0:T(8,128)(2,1)} %collective-permute-done.8), channel_id=1, source_target_pairs={{0,4},{4,0},{8,12},{12,8},{16,20},{20,16},{24,28},{28,24},{1,5},{5... | collective-permute-start | bytes 1572872 | tf_op jit(solution)/shard_map/ppermute | solution.py:166
  63.8 1.1 constant_dynamic-update-slice_fusion.refs_4_
  65.8 11.1 %collective-permute-done.9 = bf16[128,2048]{1,0:T(8,128)(2,1)S(1)} collective-permute-done((bf16[128,2048]{1,0:T(8,128)(2,1)}, bf16[128,2048]{1,0:T(8,128)(2,1)S(1)}, u32[]{:S(2)}, u32[]{:S(2)}) %collective-permute-start.9) | collective-permute-done | bytes 524320 | tf_op jit(solution)/shard_map/ppermute | solution.py:166
  76.9 0.8 constant_dynamic-update-slice_fusion.3
  77.8 6.9 %collective-permute-done.10 = bf16[128,2048]{1,0:T(8,128)(2,1)S(1)} collective-permute-done((bf16[128,2048]{1,0:T(8,128)(2,1)}, bf16[128,2048]{1,0:T(8,128)(2,1)S(1)}, u32[]{:S(2)}, u32[]{:S(2)}) %collective-permute-start.10) | collective-permute-done | bytes 524320 | tf_op jit(solution)/shard_map/ppermute | solution.py:166
  85.5 1.9 %finish.1 = bf16[1024,512]{1,0:T(8,128)(2,1)S(1)} custom-call(bf16[4,1024,256]{2,1,0:T(8,128)(2,1)S(1)} %copy-done.4, f32[1024,1024]{1,0:T(8,128)S(1)} %copy-done.2, bf16[4,144,256]{2,1,0:T(8,128)(2,1)S(1)} %pad_maximum_fusion.prefix), custom_call_target="tpu_custom_call" | custom-call | flops 536870912 | bytes 7340032 | tf_op jit(solution)/shard_map/finish/pallas_call | solution.py:283
  88.3 1.5 %collective-permute-start.5 = (bf16[256,512]{1,0:T(8,128)(2,1)S(1)}, bf16[256,512]{1,0:T(8,128)(2,1)}, u32[]{:S(2)}, u32[]{:S(2)}) collective-permute-start(bf16[256,512]{1,0:T(8,128)(2,1)S(1)} %get-tuple-element.31), channel_id=1, source_target_pairs={{0,2},{1,3},{2,0},{3,1},{4,6},{5,7},{6,4},{7,5},{8,10},{9,11},{10,... | collective-permute-start | bytes 786440 | tf_op jit(solution)/shard_map/ppermute | solution.py:166
  90.3 7.2 %collective-permute-done.5 = bf16[256,512]{1,0:T(8,128)(2,1)} collective-permute-done((bf16[256,512]{1,0:T(8,128)(2,1)S(1)}, bf16[256,512]{1,0:T(8,128)(2,1)}, u32[]{:S(2)}, u32[]{:S(2)}) %collective-permute-start.5) | collective-permute-done | bytes 262176 | tf_op jit(solution)/shard_map/ppermute | solution.py:166
  97.5 5.1 %collective-permute-done.4 = bf16[256,512]{1,0:T(8,128)(2,1)S(1)} collective-permute-done((bf16[256,512]{1,0:T(8,128)(2,1)S(1)}, bf16[256,512]{1,0:T(8,128)(2,1)S(1)}, u32[]{:S(2)}, u32[]{:S(2)}) %collective-permute-start.4) | collective-permute-done | bytes 262176 | tf_op jit(solution)/shard_map/ppermute | solution.py:166
  103.4 1.0 constant_dynamic-slice_fusion.7
  104.4 1.0 constant_dynamic-slice_fusion.4
  105.4 3.8 %shard_map.64.refs_8_ = f32[256,2048]{1,0:T(8,128)S(1)} custom-call(bf16[256,512]{1,0:T(8,128)(2,1)S(1)} %get-tuple-element.30.refs_0_, bf16[256,512]{1,0:T(8,128)(2,1)} %collective-permute-done.13.refs_1_, bf16[512,2048]{1,0:T(8,128)(2,1)S(1)} %copy-done, bf16[512,2048]{1,0:T(8,128)(2,1)} %collective-permute-done.14.refs_3_), custom_call_target="tpu_custom_call" | custom-call | flops 1073741824 | bytes 4194304 | tf_op jit(solution)/shard_map/pallas_call | solution.py:151
  109.2 4.6 %shard_map.65 = bf16[256,2048]{1,0:T(8,128)(2,1)} custom-call(bf16[256,256]{1,0:T(8,128)(2,1)S(1)} %get-tuple-element.40.refs_0_, bf16[256,256]{1,0:T(8,128)(2,1)S(1)} %get-tuple-element.39.refs_1_, bf16[256,256]{1,0:T(8,128)(2,1)S(1)} %get-tuple-element.38.refs_2_, bf16[256,256]{1,0:T(8,128)(2,1)S(1)} %get-tuple-element.37.refs_3_, ...), custom_call_target="tpu_custom_call" | custom-call | flops 1073741824 | bytes 4194304 | tf_op jit(solution)/shard_map/pallas_call | solution.py:151
  (77 shorter events, 6.1 us)
Async XLA Ops:
  0.0 2.2 %copy-start.5 = (bf16[1024,2048]{1,0:T(8,128)(2,1)S(1)}, bf16[1024,2048]{1,0:T(8,128)(2,1)}, u32[]{:S(2)}) copy-start(bf16[1024,2048]{1,0:T(8,128)(2,1)} %tok.3) | copy-start | bytes 12582916
  2.2 1.6 %copy-start.6 = (bf16[2048,512]{1,0:T(8,128)(2,1)S(1)}, bf16[2048,512]{1,0:T(8,128)(2,1)}, u32[]{:S(2)}) copy-start(bf16[2048,512]{1,0:T(8,128)(2,1)} %wk.1) | copy-start | bytes 6291460
  3.8 1.6 %copy-start.7 = (bf16[2048,512]{1,0:T(8,128)(2,1)S(1)}, bf16[2048,512]{1,0:T(8,128)(2,1)}, u32[]{:S(2)}) copy-start(bf16[2048,512]{1,0:T(8,128)(2,1)} %wv.1) | copy-start | bytes 6291460
  5.4 0.9 copy-start.9
  6.3 17.3 %copy-start = (bf16[512,2048]{1,0:T(8,128)(2,1)S(1)}, bf16[512,2048]{1,0:T(8,128)(2,1)}, u32[]{:S(2)}) copy-start(bf16[512,2048]{1,0:T(8,128)(2,1)} %refs_2_.1) | copy-start | bytes 6291460
  17.2 1.4 %copy-start.11 = (bf16[4,1024,256]{2,1,0:T(8,128)(2,1)}, bf16[4,1024,256]{2,1,0:T(8,128)(2,1)S(1)}, u32[]{:S(2)}) copy-start(bf16[4,1024,256]{2,1,0:T(8,128)(2,1)S(1)} %get-tuple-element.12.feat) | copy-start | bytes 6291460
  18.5 1.0 copy-start.13
  19.5 1.0 copy-start.15
  20.5 6.9 %collective-permute-start = (bf16[2,144,256]{2,1,0:T(8,128)(2,1)S(1)}, bf16[2,144,256]{2,1,0:T(8,128)(2,1)S(1)}, u32[]{:S(2)}, u32[]{:S(2)}) collective-permute-start(bf16[2,144,256]{2,1,0:T(8,128)(2,1)S(1)} %constant_dynamic-slice_fusion.10), channel_id=1, source_target_pairs={{0,4},{4,0},{8,12},{12,8},{16,20},{20,16},{24,28},{28,24},{1,5},{5... | collective-permute-start | bytes 442376 | tf_op jit(solution)/shard_map/ppermute | solution.py:166
  23.5 81.8 %collective-permute-start.14 = (bf16[512,2048]{1,0:T(8,128)(2,1)S(1)}, bf16[512,2048]{1,0:T(8,128)(2,1)}, u32[]{:S(2)}, u32[]{:S(2)}) collective-permute-start(bf16[512,2048]{1,0:T(8,128)(2,1)S(1)} %copy-done), channel_id=1, source_target_pairs={{0,1},{1,0},{2,3},{3,2},{4,5},{5,4},{6,7},{7,6},{8,9},{9,8},{10,11... | collective-permute-start | bytes 6291464 | tf_op jit(solution)/shard_map/ppermute | solution.py:166
  27.4 12.7 %copy-start.16 = (bf16[2,4,256,256]{3,2,1,0:T(8,128)(2,1)S(1)}, bf16[2,4,256,256]{3,2,1,0:T(8,128)(2,1)}, u32[]{:S(2)}) copy-start(bf16[2,4,256,256]{3,2,1,0:T(8,128)(2,1)} %copy-done.15) | copy-start | bytes 3145732
  27.6 12.5 %copy-start.14 = (bf16[1024,512]{1,0:T(8,128)(2,1)S(1)}, bf16[1024,512]{1,0:T(8,128)(2,1)}, u32[]{:S(2)}) copy-start(bf16[1024,512]{1,0:T(8,128)(2,1)} %copy-done.13) | copy-start | bytes 3145732
  27.7 12.4 %copy-start.8 = (bf16[2048,512]{1,0:T(8,128)(2,1)S(1)}, bf16[2048,512]{1,0:T(8,128)(2,1)}, u32[]{:S(2)}) copy-start(bf16[2048,512]{1,0:T(8,128)(2,1)} %wq.1) | copy-start | bytes 6291460
  27.7 12.4 %copy-start.10 = (f32[128,256]{1,0:T(8,128)S(1)}, f32[128,256]{1,0:T(8,128)}, u32[]{:S(2)}) copy-start(f32[128,256]{1,0:T(8,128)} %omega.3) | copy-start | bytes 393220
  27.7 12.4 %copy-start.12 = (bf16[4,1024,256]{2,1,0:T(8,128)(2,1)S(1)}, bf16[4,1024,256]{2,1,0:T(8,128)(2,1)}, u32[]{:S(2)}) copy-start(bf16[4,1024,256]{2,1,0:T(8,128)(2,1)} %copy-done.11) | copy-start | bytes 6291460
  27.8 7.1 %collective-permute-start.1 = (bf16[2,144,256]{2,1,0:T(8,128)(2,1)S(1)}, bf16[2,144,256]{2,1,0:T(8,128)(2,1)S(1)}, u32[]{:S(2)}, u32[]{:S(2)}) collective-permute-start(bf16[2,144,256]{2,1,0:T(8,128)(2,1)S(1)} %maximum_maximum_fusion.2), channel_id=1, source_target_pairs={{0,8},{4,12},{8,16},{12,20},{16,24},{20,28},{1,9},{5,13},{9,17},{1... | collective-permute-start | bytes 442376 | tf_op jit(solution)/shard_map/ppermute | solution.py:199
  32.8 27.6 %collective-permute-start.7 = (bf16[128,2048]{1,0:T(8,128)(2,1)}, bf16[128,2048]{1,0:T(8,128)(2,1)}, u32[]{:S(2)}, u32[]{:S(2)}) collective-permute-start(bf16[128,2048]{1,0:T(8,128)(2,1)} %get-tuple-element.28), channel_id=1, source_target_pairs={{0,2},{1,3},{2,0},{3,1},{4,6},{5,7},{6,4},{7,5},{8,10},{9,11},{10,... | collective-permute-start | bytes 1572872 | tf_op jit(solution)/shard_map/ppermute | solution.py:166
  34.3 27.8 %collective-permute-start.8 = (bf16[128,2048]{1,0:T(8,128)(2,1)}, bf16[128,2048]{1,0:T(8,128)(2,1)}, u32[]{:S(2)}, u32[]{:S(2)}) collective-permute-start(bf16[128,2048]{1,0:T(8,128)(2,1)} %get-tuple-element.27), channel_id=1, source_target_pairs={{0,2},{1,3},{2,0},{3,1},{4,6},{5,7},{6,4},{7,5},{8,10},{9,11},{10,... | collective-permute-start | bytes 1572872 | tf_op jit(solution)/shard_map/ppermute | solution.py:166
  35.2 23.3 %collective-permute-start.2 = (bf16[2,144,256]{2,1,0:T(8,128)(2,1)S(1)}, bf16[2,144,256]{2,1,0:T(8,128)(2,1)S(1)}, u32[]{:S(2)}, u32[]{:S(2)}) collective-permute-start(bf16[2,144,256]{2,1,0:T(8,128)(2,1)S(1)} %maximum_maximum_fusion.3), channel_id=1, source_target_pairs={{0,16},{4,20},{8,24},{12,28},{1,17},{5,21},{9,25},{13,29},{2,18},{... | collective-permute-start | bytes 442376 | tf_op jit(solution)/shard_map/ppermute | solution.py:199
  55.0 2.0 %copy-start.1 = (f32[1024,1024]{1,0:T(8,128)}, f32[1024,1024]{1,0:T(8,128)S(1)}, u32[]{:S(2)}) copy-start(f32[1024,1024]{1,0:T(8,128)S(1)} %get-tuple-element.16.result) | copy-start | bytes 12582916
  57.0 1.4 %copy-start.3 = (bf16[4,1024,256]{2,1,0:T(8,128)(2,1)}, bf16[4,1024,256]{2,1,0:T(8,128)(2,1)S(1)}, u32[]{:S(2)}) copy-start(bf16[4,1024,256]{2,1,0:T(8,128)(2,1)S(1)} %get-tuple-element.15.qfeat) | copy-start | bytes 6291460
  58.5 27.0 %copy-start.4 = (bf16[4,1024,256]{2,1,0:T(8,128)(2,1)S(1)}, bf16[4,1024,256]{2,1,0:T(8,128)(2,1)}, u32[]{:S(2)}) copy-start(bf16[4,1024,256]{2,1,0:T(8,128)(2,1)} %copy-done.3) | copy-start | bytes 6291460
  58.8 6.9 %collective-permute-start.3 = (bf16[2,144,256]{2,1,0:T(8,128)(2,1)S(1)}, bf16[2,144,256]{2,1,0:T(8,128)(2,1)S(1)}, u32[]{:S(2)}, u32[]{:S(2)}) collective-permute-start(bf16[2,144,256]{2,1,0:T(8,128)(2,1)S(1)} %maximum_maximum_fusion.5), channel_id=1, source_target_pairs={{0,4},{4,0},{8,12},{12,8},{16,20},{20,16},{24,28},{28,24},{1,5},{5... | collective-permute-start | bytes 442376 | tf_op jit(solution)/shard_map/ppermute | solution.py:166
  60.5 16.5 %collective-permute-start.9 = (bf16[128,2048]{1,0:T(8,128)(2,1)}, bf16[128,2048]{1,0:T(8,128)(2,1)S(1)}, u32[]{:S(2)}, u32[]{:S(2)}) collective-permute-start(bf16[128,2048]{1,0:T(8,128)(2,1)} %collective-permute-done.7), channel_id=1, source_target_pairs={{0,4},{4,0},{8,12},{12,8},{16,20},{20,16},{24,28},{28,24},{1,5},{5... | collective-permute-start | bytes 1572872 | tf_op jit(solution)/shard_map/ppermute | solution.py:166
  62.2 23.4 %copy-start.2 = (f32[1024,1024]{1,0:T(8,128)S(1)}, f32[1024,1024]{1,0:T(8,128)}, u32[]{:S(2)}) copy-start(f32[1024,1024]{1,0:T(8,128)} %copy-done.1) | copy-start | bytes 12582916
  62.2 22.5 %collective-permute-start.10 = (bf16[128,2048]{1,0:T(8,128)(2,1)}, bf16[128,2048]{1,0:T(8,128)(2,1)S(1)}, u32[]{:S(2)}, u32[]{:S(2)}) collective-permute-start(bf16[128,2048]{1,0:T(8,128)(2,1)} %collective-permute-done.8), channel_id=1, source_target_pairs={{0,4},{4,0},{8,12},{12,8},{16,20},{20,16},{24,28},{28,24},{1,5},{5... | collective-permute-start | bytes 1572872 | tf_op jit(solution)/shard_map/ppermute | solution.py:166
  64.9 44.3 %collective-permute-start.11 = (bf16[256,2048]{1,0:T(8,128)(2,1)S(1)}, bf16[256,2048]{1,0:T(8,128)(2,1)}, u32[]{:S(2)}, u32[]{:S(2)}) collective-permute-start(bf16[256,2048]{1,0:T(8,128)(2,1)S(1)} %constant_dynamic-update-slice_fusion.refs_4_), channel_id=1, source_target_pairs={{0,1},{1,0},{2,3},{3,2},{4,5},{5,4},{6,7},{7,6},{8,9},{9,8},{10,11... | collective-permute-start | bytes 3145736 | tf_op jit(solution)/shard_map/ppermute | solution.py:166
  85.5 23.7 %collective-permute-start.12 = (bf16[256,2048]{1,0:T(8,128)(2,1)}, bf16[256,2048]{1,0:T(8,128)(2,1)}, u32[]{:S(2)}, u32[]{:S(2)}) collective-permute-start(bf16[256,2048]{1,0:T(8,128)(2,1)} %constant_dynamic-update-slice_fusion.2.refs_5_), channel_id=1, source_target_pairs={{0,1},{1,0},{2,3},{3,2},{4,5},{5,4},{6,7},{7,6},{8,9},{9,8},{10,11... | collective-permute-start | bytes 3145736 | tf_op jit(solution)/shard_map/ppermute | solution.py:166
  88.3 9.2 %collective-permute-start.5 = (bf16[256,512]{1,0:T(8,128)(2,1)S(1)}, bf16[256,512]{1,0:T(8,128)(2,1)}, u32[]{:S(2)}, u32[]{:S(2)}) collective-permute-start(bf16[256,512]{1,0:T(8,128)(2,1)S(1)} %get-tuple-element.31), channel_id=1, source_target_pairs={{0,2},{1,3},{2,0},{3,1},{4,6},{5,7},{6,4},{7,5},{8,10},{9,11},{10,... | collective-permute-start | bytes 786440 | tf_op jit(solution)/shard_map/ppermute | solution.py:166
  89.8 12.8 %collective-permute-start.4 = (bf16[256,512]{1,0:T(8,128)(2,1)S(1)}, bf16[256,512]{1,0:T(8,128)(2,1)S(1)}, u32[]{:S(2)}, u32[]{:S(2)}) collective-permute-start(bf16[256,512]{1,0:T(8,128)(2,1)S(1)} %get-tuple-element.32), channel_id=1, source_target_pairs={{0,2},{1,3},{2,0},{3,1},{4,6},{5,7},{6,4},{7,5},{8,10},{9,11},{10,... | collective-permute-start | bytes 786440 | tf_op jit(solution)/shard_map/ppermute | solution.py:166
  97.5 6.8 %collective-permute-start.6 = (bf16[256,512]{1,0:T(8,128)(2,1)}, bf16[256,512]{1,0:T(8,128)(2,1)}, u32[]{:S(2)}, u32[]{:S(2)}) collective-permute-start(bf16[256,512]{1,0:T(8,128)(2,1)} %collective-permute-done.5), channel_id=1, source_target_pairs={{0,1},{1,0},{2,3},{3,2},{4,5},{5,4},{6,7},{7,6},{8,9},{9,8},{10,11... | collective-permute-start | bytes 786440 | tf_op jit(solution)/shard_map/ppermute | solution.py:166
  103.4 2.0 %collective-permute-start.13 = (bf16[256,512]{1,0:T(8,128)(2,1)}, bf16[256,512]{1,0:T(8,128)(2,1)}, u32[]{:S(2)}, u32[]{:S(2)}) collective-permute-start(bf16[256,512]{1,0:T(8,128)(2,1)} %get-tuple-element.29), channel_id=1, source_target_pairs={{0,1},{1,0},{2,3},{3,2},{4,5},{5,4},{6,7},{7,6},{8,9},{9,8},{10,11... | collective-permute-start | bytes 786440 | tf_op jit(solution)/shard_map/ppermute | solution.py:166
  (1 other events, 0.7 us)

commit v2 on v0

v2 whole, which is shorter than its diff:
```python
import functools
import math

import jax
import jax.numpy as jnp
from jax import lax
from jax.experimental import pallas as pl
from jax.experimental.pallas import tpu as pltpu
from jax.sharding import PartitionSpec as P

BLOCK = 512
PART = 128
COST = 1000
QUAD = 4
TILE = 512
TAIL = 16
STABILIZER = 0.001
BF16 = jnp.bfloat16
F32 = jnp.float32


def params(mib):
    return pltpu.CompilerParams(vmem_limit_bytes=mib * 2**20)


def dot(a, b):
    return lax.dot_general(a, b, (((1,), (0,)), ((), ())), preferred_element_type=F32)


def dot_nt(a, b):
    return lax.dot_general(a, b, (((1,), (1,)), ((), ())), preferred_element_type=F32)


def dot_tn(a, b):
    return lax.dot_general(a, b, (((0,), (0,)), ((), ())), preferred_element_type=F32)


def halves(value):
    high = value.astype(BF16)
    return high, (value - high.astype(F32)).astype(BF16)


def feature_weights(omega):
    size, features = omega.shape
    high, low = halves(omega * size ** (-0.25))
    minus = jnp.full((2 * size, features), -1.0, BF16)
    return jnp.concatenate([high, high, low, low, minus], axis=0)


def features(rows, weights):
    size = rows.shape[1]
    high, low = halves(rows)
    square_high, square_low = halves(rows * rows * (0.5 * size ** (-0.5)))
    left = jnp.concatenate([high, low, high, low, square_high, square_low], axis=1)
    exponent = dot(left, weights)
    return ((jnp.exp(exponent) + STABILIZER) * (1.0 / math.sqrt(weights.shape[1]))).astype(BF16)


VMEM = pl.BlockSpec(memory_space=pltpu.VMEM)
SMEM = pl.BlockSpec(memory_space=pltpu.SMEM)
HBM = pl.BlockSpec(memory_space=pltpu.HBM)
ANY = pl.BlockSpec(memory_space=pl.ANY)
ROWS = 8


def narrow(state):
    size = state.shape[0] - ROWS
    norm = state[size:]
    high = norm.astype(BF16).astype(F32)
    return jnp.concatenate([state[:size], high, norm - high], axis=0).astype(BF16)


def widen(message):
    size = message.shape[0] - 2 * ROWS
    wide = message.astype(F32)
    return jnp.concatenate([wide[:size], wide[size : size + ROWS] + wide[size + ROWS :]], axis=0)


def cut_kernel(place, whole, part, sem):
    depth = part.shape[0]
    start = pl.multiple_of(place[0] * depth, depth)
    copy = pltpu.make_async_copy(whole.at[pl.ds(start, depth)], part, sem)
    copy.start()
    copy.wait()


def key_kernel(
    place, tok, wk, wv, omega, wq, wo, _, tok_out, wq_out, feat, value, own, sent_1, sent_2, sent_3, local, rest, wk_in, wv_in, om_in, keys, sem
):
    rows = tok.shape[0]
    size = omega.shape[0]
    chunk = rows // 4
    member = place[2]
    copies = []

    def fetch(source, target):
        copy = pltpu.make_async_copy(source, target, sem.at[len(copies)])
        copy.start()
        copies.append(copy)
        return copy

    def token_chunk(i):
        part = pl.ds(i * chunk, chunk)
        return fetch(tok.at[part], tok_out.at[part])

    wk_copy = fetch(wk, wk_in)
    token_copies = [token_chunk(0), token_chunk(1)]
    om_copy = fetch(omega, om_in)
    token_copies += [token_chunk(2), token_chunk(3)]
    wv_copy = fetch(wv, wv_in)
    wq_copy = fetch(wq, wq_out)
    rest_copy = fetch(wo.at[pl.ds(wo.shape[0] - rest.shape[0], rest.shape[0])], rest)

    wk_copy.wait()
    for i, copy in enumerate(token_copies):
        copy.wait()
        part = slice(i * chunk, (i + 1) * chunk)
        keys[part] = dot(tok_out[part], wk_in[...])
    wv_copy.wait()
    for start in range(0, rows, BLOCK):
        part = slice(start, start + BLOCK)
        value[part] = dot(tok_out[part], wv_in[...]).astype(BF16)
    om_copy.wait()
    weights = feature_weights(om_in[...])
    ones = jnp.ones((BLOCK, TAIL), BF16)
    heads = feat.shape[0]
    for h in range(heads):
        columns = slice(h * size, (h + 1) * size)
        for start in range(0, rows, PART):
            part = slice(start, start + PART)
            feat[h, part] = features(keys[part, columns], weights)
    for h in range(heads):
        columns = slice(h * size, (h + 1) * size)
        total = None
        for block in range(rows // BLOCK):
            part = slice(block * BLOCK, (block + 1) * BLOCK)
            if block > 0:
                norm = jnp.broadcast_to(total[size : size + 1], (size, total.shape[1]))
                local[block - 1, h] = jnp.concatenate([total[:size], norm], axis=0).astype(BF16)
            added = dot_tn(jnp.concatenate([value[part, columns], ones], axis=1), feat[h, part])[: size + ROWS]
            total = added if total is None else total + added
        group = heads // QUAD

        @pl.when(member == h // group)
        def _():
            own[h % group] = total

        @pl.when(member != h // group)
        def _():
            thin = narrow(total)
            for k, sent in ((1, sent_1), (2, sent_2), (3, sent_3)):

                @pl.when(member ^ k == h // group)
                def _():
                    sent[h % group] = thin

    wq_copy.wait()
    rest_copy.wait()


def query_kernel(first, count, tok, wq, omega, feat, value, local, *rest):
    qfeat, result, query = rest[-3:]
    rows = tok.shape[0]
    size = omega.shape[0]
    half = BLOCK // 2
    weights = feature_weights(omega[...])
    causal = lax.broadcasted_iota(jnp.int32, (half, half), 0) >= lax.broadcasted_iota(
        jnp.int32, (half, half), 1
    )
    for start in range(0, rows, BLOCK):
        part = slice(start, start + BLOCK)
        query[part] = dot(tok[part], wq[:, first * size : (first + count) * size])
    for h in range(count):
        for start in range(0, rows, PART):
            part = slice(start, start + PART)
            qfeat[h, part] = features(query[part, h * size : (h + 1) * size], weights)
    for h in range(count):
        for block in range(rows // BLOCK):
            part = slice(block * BLOCK, (block + 1) * BLOCK)
            f = qfeat[h, part]
            k = feat[first + h, part]
            v = value[part, (first + h) * size : (first + h + 1) * size]
            v = jnp.concatenate([v, jnp.ones((BLOCK, size), BF16)], axis=1)
            top = jnp.where(causal, dot_nt(f[:half], k[:half]), 0.0).astype(BF16)
            left = dot_nt(f[half:], k[:half]).astype(BF16)
            right = jnp.where(causal, dot_nt(f[half:], k[half:]), 0.0).astype(BF16)
            upper = dot(top, v[:half])
            lower = dot(jnp.concatenate([left, right], axis=1), v)
            out = jnp.concatenate([upper, lower], axis=0)
            if block > 0:
                out = out + dot_nt(f, local[block - 1, first + h])
            result[part, h * 2 * size : (h + 1) * 2 * size] = out


def group_kernel(own, one, two, three, _, sent):
    for j in range(own.shape[0]):
        sent[j] = narrow(own[j] + widen(one[j]) + widen(two[j]) + widen(three[j]))


def scan_kernel(count, message, received, *rest):
    before, (earlier, sent) = rest[:count], rest[-2:]
    for j in range(message.shape[0]):
        total = widen(received[j])
        if before:
            total = total + before[0][j]
        earlier[j] = total
        sent[j] = narrow(widen(message[j]) + total)


def last_kernel(count, place, own, one, two, three, late, *rest):
    before, outs = rest[:count], rest[-QUAD:]
    member = place[2]
    for j in range(own.shape[0]):
        total = widen(late[j])
        if before:
            total = total + before[0][j]
        states = [own[j], widen(one[j]), widen(two[j]), widen(three[j])]
        for k, out in enumerate(outs):
            value = total
            for i, state in enumerate(states):
                if i != k:
                    value = value + jnp.where((member ^ i) < (member ^ k), state, 0.0)
            out[j] = narrow(value)


def finish_kernel(bits, count, place, *refs):
    prefixes, partials, outs = refs[:QUAD], refs[QUAD:], refs[-len(bits) :]
    group = prefixes[0].shape[0]
    heads = QUAD * group
    size = outs[0].shape[1] // heads
    share = outs[0].shape[0]
    for h in range(heads):
        qfeat, result = partials[2 * (h // count)], partials[2 * (h // count) + 1]
        j = h % count
        p = prefixes[0][h % group].astype(F32)
        for k in range(1, QUAD):
            p = jnp.where(place[2] ^ k == h // group, prefixes[k][h % group].astype(F32), p)
        norm = p[size : size + 1] + p[size + ROWS : size + ROWS + 1]
        right = jnp.concatenate([p[:size], jnp.broadcast_to(norm, (size, p.shape[1]))], axis=0).astype(BF16)
        for bit, out in zip(bits, outs):
            part = pl.ds(pl.multiple_of((place[1] ^ bit) * share, share), share)
            r = result[part, j * 2 * size : (j + 1) * 2 * size] + dot_nt(qfeat[j, part, :], right)
            out[:, h * size : (h + 1) * size] = (r[:, :size] / r[:, size:]).astype(BF16)


def out_kernel(count, place, *refs):
    lefts = refs[: 2]
    rights, others = refs[2 : 2 + 2 * count], refs[2 + 2 * count :]
    streamed = len(others) > 2
    if streamed:
        before, out, tiles, sem = others
    else:
        (out,) = others
        before = None
    width = min(TILE, out.shape[1])
    copies = []
    for tile in range(out.shape[1] // width):
        here = slice(tile * width, (tile + 1) * width)
        total = before[:, here] if streamed else None
        for i, left in enumerate(lefts):
            if count == 1:
                right = rights[i][:, here]
            else:
                near, far, rest = [ref[:, here] for ref in rights[3 * i : 3 * i + 3]]
                even = place[0] == 0
                right = jnp.concatenate([jnp.where(even, near, far), jnp.where(even, far, near), rest], axis=0)
            term = dot(left[...], right)
            total = term if total is None else total + term
        if streamed:
            tiles[:, here] = total.astype(out.dtype)
            part = pl.ds(tile * width, width)
            copies.append(pltpu.make_async_copy(tiles.at[:, part], out.at[:, part], sem.at[tile]))
            copies[-1].start()
        else:
            out[:, here] = total
    for copy in copies:
        copy.wait()


def out_product(place, lefts, rights, partial, dtype):
    rows, width = lefts[0].shape[0], rights[0].shape[1]
    operands = [place] + list(lefts) + [pltpu.with_memory_space_constraint(w, pltpu.VMEM) for w in rights]
    if partial is not None:
        operands.append(partial)
    streamed = dtype == BF16
    return pl.pallas_call(
        functools.partial(out_kernel, len(rights) // 2),
        in_specs=[SMEM] + [VMEM] * (len(operands) - 1),
        out_specs=HBM if streamed else VMEM,
        out_shape=jax.ShapeDtypeStruct((rows, width), dtype) if streamed else pltpu.VMEM((rows, width), dtype),
        scratch_shapes=[pltpu.VMEM((rows, width), dtype), pltpu.SemaphoreType.DMA((width // TILE,))] if streamed else [],
        compiler_params=params(8),
        cost_estimate=pl.CostEstimate(flops=COST, bytes_accessed=COST, transcendentals=0),
        name="out",
    )(*operands)


def swap(value, axis, bit):
    count = lax.axis_size(axis)
    return lax.ppermute(value, axis, [(i, i ^ bit) for i in range(count)])


def nothing(*_):
    pass


def after(value, earlier):
    return pl.pallas_call(
        nothing,
        in_specs=[pl.BlockSpec(memory_space=pl.ANY)] * 2,
        out_specs=pl.BlockSpec(memory_space=pl.ANY),
        out_shape=jax.ShapeDtypeStruct(value.shape, value.dtype),
        input_output_aliases={0: 0},
        compiler_params=params(1),
        cost_estimate=pl.CostEstimate(flops=COST, bytes_accessed=COST, transcendentals=0),
        name="after",
    )(value, earlier)


def local_call(kernel, name, operands, specs, outs, **kwargs):
    return pl.pallas_call(
        kernel,
        in_specs=specs,
        out_specs=[VMEM] * len(outs),
        out_shape=[pltpu.VMEM(shape, dtype) for shape, dtype in outs],
        cost_estimate=pl.CostEstimate(flops=FLOPS.get(name, COST), bytes_accessed=COST, transcendentals=0),
        compiler_params=params(VMEM_MIB[name]),
        name=name,
        **kwargs,
    )(*operands)


FLOPS = dict(keys=10**10, queries=10**9)
VMEM_MIB = dict(cut=4, keys=12, queries=12, group=8, scan=8, last=8, finish=8)


def prefix(place, own, received, message, others):
    count = lax.axis_size("seq")
    wide, thin = (own.shape, F32), (message.shape, BF16)
    step = QUAD
    before = []
    while True:
        late = lax.ppermute(message, "seq", [(i, i + step) for i in range(count - step)])
        step *= 2
        if step >= count:
            break
        earlier, message = local_call(
            functools.partial(scan_kernel, len(before)),
            "scan",
            [message, late] + before,
            [VMEM] * (2 + len(before)),
            [wide, thin],
        )
        before = [earlier]
    return local_call(
        functools.partial(last_kernel, len(before)),
        "last",
        [place, own] + received + [late] + before + others,
        [SMEM] + [VMEM] * (QUAD + 1 + len(before)) + [ANY] * len(others),
        [thin] * QUAD,
    )


def shards(tokens, w_query, w_key, w_value, omega, w_out):
    rows, width = tokens.shape
    size, feats = omega.shape
    heads = w_query.shape[1] // size
    blocks = rows // BLOCK
    seq_side = lax.axis_index("seq") % 2
    head_at = lax.axis_index("head")
    place = jnp.stack([seq_side, head_at, lax.axis_index("seq") % QUAD]).astype(jnp.int32)

    depth = w_out.shape[0] * 7 // 32
    (part,) = local_call(
        cut_kernel,
        "cut",
        [place, pltpu.with_memory_space_constraint(w_out, pltpu.HBM)],
        [SMEM, HBM],
        [((depth, w_out.shape[1]), BF16)],
        scratch_shapes=[pltpu.SemaphoreType.DMA],
    )
    near_part = swap(part, "head", 2)
    w_core = swap(w_out, "head", 1)

    group = heads // QUAD
    tok, wq, key_feat, value, own, *sent, local, rest = local_call(
        key_kernel,
        "keys",
        [place] + [pltpu.with_memory_space_constraint(v, pltpu.HBM) for v in (tokens, w_key, w_value, omega, w_query, w_out)] + [part],
        [SMEM] + [HBM] * 6 + [ANY],
        [
            ((rows, width), BF16),
            (w_query.shape, BF16),
            ((heads, rows, feats), BF16),
            ((rows, heads * size), BF16),
            ((group, size + ROWS, feats), F32),
            ((group, size + 2 * ROWS, feats), BF16),
            ((group, size + 2 * ROWS, feats), BF16),
            ((group, size + 2 * ROWS, feats), BF16),
            ((max(blocks - 1, 1), heads, 2 * size, feats), BF16),
            ((w_out.shape[0] - 2 * depth, w_out.shape[1]), BF16),
        ],
        scratch_shapes=[
            pltpu.VMEM(w_key.shape, BF16),
            pltpu.VMEM(w_value.shape, BF16),
            pltpu.VMEM(omega.shape, F32),
            pltpu.VMEM((rows, heads * size), F32),
            pltpu.SemaphoreType.DMA((9,)),
        ],
    )

    count = heads // 2

    def queries(first, others):
        return local_call(
            functools.partial(query_kernel, first, count),
            "queries",
            [tok, wq, omega, key_feat, value, local] + others,
            [VMEM] * 6 + [ANY] * len(others),
            [((count, rows, feats), BF16), ((rows, count * 2 * size), F32)],
            scratch_shapes=[pltpu.VMEM((rows, count * size), F32)],
        )

    received = [swap(v, "seq", k) for k, v in enumerate(sent, 1)]
    near_rest = swap(rest, "head", 2)
    partials = queries(0, [near_part, w_core])
    (message,) = local_call(
        group_kernel, "group", [own] + received + [partials[0]], [VMEM] * QUAD + [ANY], [(sent[0].shape, BF16)]
    )
    near_part = after(near_part, message)
    core_part = swap(near_part, "head", 1)
    partials = list(partials) + list(queries(count, [message]))
    far_part = swap(near_part, "seq", 1)
    kept, *handed = prefix(place, own, received, message, [partials[2], core_part, far_part])
    prefixes = [kept] + [swap(v, "seq", k) for k, v in enumerate(handed, 1)]
    far_part = after(far_part, kept)
    core_far = swap(far_part, "head", 1)

    share = rows // lax.axis_size("head")
    bits = (2, 3, 1, 0)
    to_x, to_diagonal, to_core, mine = local_call(
        functools.partial(finish_kernel, bits, count),
        "finish",
        [place] + prefixes + partials + [near_rest, core_far],
        [SMEM] + [VMEM] * (QUAD + len(partials)) + [ANY] * 2,
        [((share, heads * size), BF16)] * len(bits),
    )
    from_x = swap(to_x, "head", 2)
    from_diagonal = swap(to_diagonal, "head", 3)
    from_core = swap(to_core, "head", 1)

    total = out_product(place, [mine, from_core], [w_out, w_core], None, F32)
    near_rest = after(near_rest, to_x)
    core_rest = swap(near_rest, "head", 1)
    rights = [near_part, far_part, near_rest, core_part, core_far, core_rest]
    return out_product(place, [from_x, from_diagonal], rights, total, BF16)


def solution(mesh):
    placed = (
        P("seq", None),
        P(None, "head"),
        P(None, "head"),
        P(None, "head"),
        P(),
        P("head", None),
    )
    return jax.shard_map(
        shards, mesh=mesh, in_specs=placed, out_specs=P(("seq", "head"), None), check_vma=False
    )
```

time: 202 us -> 62.6 us (0.31)
  waiting for transfers between devices: 96.6 us -> 18.9 us
  matrix products: 39.5 us -> 0 us
  blocking collectives: 32.4 us -> 0 us
  Pallas kernels: 0 us -> 25.3 us
  starting transfers between devices: 0.04 us -> 17.9 us
  other arithmetic: 13.6 us -> 0.08 us
  between operations: 13.8 us -> 0.31 us
  local copies, waits for them, and re-layouts: 5.41 us -> 0.01 us
    reduce_scatter x1 -> x0, waiting for transfers between devices: 70.1 us -> none  [shards(): lax.psum_scatter(jnp.dot(attention, w_out, preferred_element_type=jnp.flo...]
    dot_general x16 -> x0, matrix products: 39.5 us -> none  [the longest x2 9.57 us: feature_map(): jnp.einsum('thd,dm->thm', scaled, omega, precision=highest_precision)]
    all_gather x1 -> x0, blocking collectives: 32.4 us -> none  [prefix(): pieces = jax.tree.map(lambda part: lax.all_gather(part, axis), value)]
    all_gather x1 -> x0, waiting for transfers between devices: 26.4 us -> none  [prefix(): pieces = jax.tree.map(lambda part: lax.all_gather(part, axis), value)]
    pallas_call x0 -> x12, Pallas kernels: none -> 25.3 us  [the longest x7 20.9 us: local_call(): pl.pallas_call(kernel, in_specs=specs, out_specs=[VMEM] * len(outs), out_...]
    ppermute x0 -> x17, waiting for transfers between devices: none -> 18.9 us  [the longest x16 18.9 us: swap(): return lax.ppermute(value, axis, [(i, i ^ bit) for i in range(count)])]
    ppermute x0 -> x17, starting transfers between devices: none -> 17.9 us  [the longest x16 13.2 us: swap(): return lax.ppermute(value, axis, [(i, i ^ bit) for i in range(count)])]
    select_n x14 -> x0, other arithmetic: 8.64 us -> none  [turn(): jnp.where(position < mine, new, old)]
  transfers between devices with their start and end apart: 2 -> 17, of which waited for: 2 -> 8; matrix products, arithmetic and copies ran while one was open for 7% -> 0% of each run, Pallas kernels for 0% -> 34%
where the time goes in v2:
time: 62.6 us; the launch traced here: 62.4 us
  Pallas kernels  25.3 us (40%)
  waiting for transfers between devices  18.9 us (30%)
  starting transfers between devices  17.9 us (29%)
    pallas_call x7, Pallas kernels, local_call(): pl.pallas_call(kernel, in_specs=specs, out_specs=[VMEM] * len(outs), out_...  20.9 us
    ppermute x16, waiting for transfers between devices, swap(): return lax.ppermute(value, axis, [(i, i ^ bit) for i in range(count)])  18.9 us
    ppermute x16, starting transfers between devices, swap(): return lax.ppermute(value, axis, [(i, i ^ bit) for i in range(count)])  13.2 us
    ppermute x1, starting transfers between devices, prefix(): lax.ppermute(message, 'seq', [(i, i + step) for i in range(count - step)])  4.67 us
    pallas_call x2, Pallas kernels, out_product(): pl.pallas_call(functools.partial(out_kernel, len(rights) // 2), in_specs=...  4.37 us
  transfers between devices with their start and end apart: 17, of which 8 were waited for; matrix products, arithmetic and copies ran while one was open for 0% of the time, Pallas kernels for 34%

profile of v2, /device:TPU:0, one launch (start us, length us, event | category | flops | bytes accessed | tf_op | source)
XLA Modules:
  0.0 62.4 jit_solution(10853384951111871859)
XLA Ops:
  0.0 0.5 collective-permute-start.4
  0.5 0.1 pad_add_fusion.place
  0.5 1.6 %cut.1._ = bf16[112,2048]{1,0:T(8,128)(2,1)S(1)} custom-call(s32[3]{0:T(128)S(1)} %pad_add_fusion.place, bf16[512,2048]{1,0:T(8,128)(2,1)} %refs_2_.1), custom_call_target="tpu_custom_call" | custom-call | flops 1000 | bytes 1000 | tf_op jit(solution)/shard_map/cut/pallas_call | solution.py:321
  2.1 2.6 %collective-permute-start.3 = (bf16[112,2048]{1,0:T(8,128)(2,1)S(1)}, bf16[112,2048]{1,0:T(8,128)(2,1)S(1)}, u32[]{:S(2)}, u32[]{:S(2)}) collective-permute-start(bf16[112,2048]{1,0:T(8,128)(2,1)S(1)} %cut.1._), channel_id=1, source_target_pairs={{0,2},{1,3},{2,0},{3,1},{4,6},{5,7},{6,4},{7,5},{8,10},{9,11},{10,... | collective-permute-start | bytes 1376264 | tf_op jit(solution)/shard_map/ppermute | solution.py:300
  4.7 10.4 %keys.1 = (bf16[1024,2048]{1,0:T(8,128)(2,1)S(1)}, bf16[2048,512]{1,0:T(8,128)(2,1)S(1)}, bf16[4,1024,256]{2,1,0:T(8,128)(2,1)S(1)}, bf16[1024,512]{1,0:T(8,128)...) custom-call(s32[3]{0:T(128)S(1)} %pad_add_fusion.place, ...), custom_call_target="tpu_custom_call" | custom-call | flops 10000000000 | bytes 1000 | tf_op jit(solution)/shard_map/keys/pallas_call | solution.py:321
  15.1 0.1 collective-permute-start.11
  15.2 2.0 %collective-permute-start = (bf16[1,144,256]{2,1,0:T(8,128)(2,1)S(1)}, bf16[1,144,256]{2,1,0:T(8,128)(2,1)S(1)}, u32[]{:S(2)}, u32[]{:S(2)}) collective-permute-start(bf16[1,144,256]{2,1,0:T(8,128)(2,1)S(1)} %get-tuple-element.28), channel_id=1, source_target_pairs={{0,4},{4,0},{8,12},{12,8},{16,20},{20,16},{24,28},{28,24},{1,5},{5... | collective-permute-start | bytes 221192 | tf_op jit(solution)/shard_map/ppermute | solution.py:300
  17.3 1.6 %collective-permute-start.1 = (bf16[1,144,256]{2,1,0:T(8,128)(2,1)S(1)}, bf16[1,144,256]{2,1,0:T(8,128)(2,1)S(1)}, u32[]{:S(2)}, u32[]{:S(2)}) collective-permute-start(bf16[1,144,256]{2,1,0:T(8,128)(2,1)S(1)} %get-tuple-element.29), channel_id=1, source_target_pairs={{0,8},{4,12},{8,0},{12,4},{16,24},{20,28},{24,16},{28,20},{1,9},{5... | collective-permute-start | bytes 221192 | tf_op jit(solution)/shard_map/ppermute | solution.py:300
  18.9 3.4 %queries.2 = (bf16[2,1024,256]{2,1,0:T(8,128)(2,1)S(1)}, f32[1024,512]{1,0:T(8,128)S(1)}) custom-call(bf16[1024,2048]{1,0:T(8,128)(2,1)S(1)} %get-tuple-element.31.tok, bf16[2048,512]{1,0:T(8,128)(2,1)S(1)} %get-tuple-element.32.wq, f32[128,256]{1,0:T(8,128)S(1)} %copy-done.1, bf16[4,1024,256]{2,1,0:T(8,128)(2,1)S(1)} %get-tuple-element.33.feat, ...), custom_call_target="tpu_custom_call" | custom-call | flops 1000000000 | bytes 1000 | tf_op jit(solution)/shard_map/queries/pallas_call | solution.py:321
  22.2 0.1 collective-permute-done.1.two
  22.3 1.8 %collective-permute-done.2.three = bf16[1,144,256]{2,1,0:T(8,128)(2,1)S(1)} collective-permute-done((bf16[1,144,256]{2,1,0:T(8,128)(2,1)S(1)}, bf16[1,144,256]{2,1,0:T(8,128)(2,1)S(1)}, u32[]{:S(2)}, u32[]{:S(2)}) %collective-permute-start.2) | collective-permute-done | bytes 73760 | tf_op jit(solution)/shard_map/ppermute | solution.py:300
  24.1 0.6 collective-permute-start.7
  24.7 4.7 %collective-permute-start.5 = (bf16[1,144,256]{2,1,0:T(8,128)(2,1)S(1)}, bf16[1,144,256]{2,1,0:T(8,128)(2,1)S(1)}, u32[]{:S(2)}, u32[]{:S(2)}) collective-permute-start(bf16[1,144,256]{2,1,0:T(8,128)(2,1)S(1)} %group.1.rest_0_.__1_), channel_id=1, source_target_pairs={{0,16},{4,20},{8,24},{12,28},{1,17},{5,21},{9,25},{13,29},{2,18},{... | collective-permute-start | bytes 221192 | tf_op jit(solution)/shard_map/ppermute | solution.py:343
  29.4 3.4 %queries.3 = (bf16[2,1024,256]{2,1,0:T(8,128)(2,1)S(1)}, f32[1024,512]{1,0:T(8,128)S(1)}) custom-call(bf16[1024,2048]{1,0:T(8,128)(2,1)S(1)} %get-tuple-element.31.tok, bf16[2048,512]{1,0:T(8,128)(2,1)S(1)} %get-tuple-element.32.wq, f32[128,256]{1,0:T(8,128)S(1)} %copy-done.1, bf16[4,1024,256]{2,1,0:T(8,128)(2,1)S(1)} %get-tuple-element.33.feat, ...), custom_call_target="tpu_custom_call" | custom-call | flops 1000000000 | bytes 1000 | tf_op jit(solution)/shard_map/queries/pallas_call | solution.py:321
  32.8 2.1 %collective-permute-done.7.rest_2_.__0_ = bf16[112,2048]{1,0:T(8,128)(2,1)S(1)} collective-permute-done((bf16[112,2048]{1,0:T(8,128)(2,1)S(1)}, bf16[112,2048]{1,0:T(8,128)(2,1)S(1)}, u32[]{:S(2)}, u32[]{:S(2)}) %collective-permute-start.7) | collective-permute-done | bytes 458784 | tf_op jit(solution)/shard_map/ppermute | solution.py:300
  34.9 0.7 %last.1 = (bf16[1,144,256]{2,1,0:T(8,128)(2,1)S(1)}, bf16[1,144,256]{2,1,0:T(8,128)(2,1)S(1)}, bf16[1,144,256]{2,1,0:T(8,128)(2,1)S(1)}, bf16[1,144,256]{2,1,0:T(8,128)(2,1)S(1)}) custom-call(s32[3]{0:T(128)S(1)} %pad_add_fusion.place, f32[1,136,256]{2,1,0:T(8,128)S(1)} %get-tuple-element.27.own, bf16[1,144,256]{2,1,0:T(8,128)(2,1)S(1)} %collective-permute-done.one, ...), custom_call_target="tpu_custom_call" | custom-call | flops 1000 | bytes 1000 | tf_op jit(solution)/shard_map/last/pallas_call | solution.py:321
  35.6 0.1 collective-permute-start.12
  35.7 1.3 %collective-permute-start.8 = (bf16[1,144,256]{2,1,0:T(8,128)(2,1)S(1)}, bf16[1,144,256]{2,1,0:T(8,128)(2,1)S(1)}, u32[]{:S(2)}, u32[]{:S(2)}) collective-permute-start(bf16[1,144,256]{2,1,0:T(8,128)(2,1)S(1)} %get-tuple-element.39), channel_id=1, source_target_pairs={{0,4},{4,0},{8,12},{12,8},{16,20},{20,16},{24,28},{28,24},{1,5},{5... | collective-permute-start | bytes 221192 | tf_op jit(solution)/shard_map/ppermute | solution.py:300
  37.0 1.3 %collective-permute-start.9 = (bf16[1,144,256]{2,1,0:T(8,128)(2,1)S(1)}, bf16[1,144,256]{2,1,0:T(8,128)(2,1)S(1)}, u32[]{:S(2)}, u32[]{:S(2)}) collective-permute-start(bf16[1,144,256]{2,1,0:T(8,128)(2,1)S(1)} %get-tuple-element.40), channel_id=1, source_target_pairs={{0,8},{4,12},{8,0},{12,4},{16,24},{20,28},{24,16},{28,20},{1,9},{5... | collective-permute-start | bytes 221192 | tf_op jit(solution)/shard_map/ppermute | solution.py:300
  38.3 1.0 %collective-permute-start.10 = (bf16[1,144,256]{2,1,0:T(8,128)(2,1)S(1)}, bf16[1,144,256]{2,1,0:T(8,128)(2,1)S(1)}, u32[]{:S(2)}, u32[]{:S(2)}) collective-permute-start(bf16[1,144,256]{2,1,0:T(8,128)(2,1)S(1)} %get-tuple-element.41), channel_id=1, source_target_pairs={{0,12},{4,8},{8,4},{12,0},{16,28},{20,24},{24,20},{28,16},{1,13},{... | collective-permute-start | bytes 221192 | tf_op jit(solution)/shard_map/ppermute | solution.py:300
  39.2 4.1 %collective-permute-done.11.refs_8_.__0_ = bf16[288,2048]{1,0:T(8,128)(2,1)S(1)} collective-permute-done((bf16[288,2048]{1,0:T(8,128)(2,1)S(1)}, bf16[288,2048]{1,0:T(8,128)(2,1)S(1)}, u32[]{:S(2)}, u32[]{:S(2)}) %collective-permute-start.11) | collective-permute-done | bytes 1179680 | tf_op jit(solution)/shard_map/ppermute | solution.py:300
  43.3 0.2 collective-permute-done.10.refs_3_
  43.5 1.4 %finish.1 = (bf16[256,512]{1,0:T(8,128)(2,1)S(1)}, bf16[256,512]{1,0:T(8,128)(2,1)S(1)}, bf16[256,512]{1,0:T(8,128)(2,1)S(1)}, bf16[256,512]{1,0:T(8,128)(2,1)S(1)}) custom-call(s32[3]{0:T(128)S(1)} %pad_add_fusion.place, bf16[1,144,256]{2,1,0:T(8,128)(2,1)S(1)} %get-tuple-element.38.__1_.refs_0_, bf16[1,144,256]{2,1,0:T(8,128)(2,1)S(1)} %collective-permute-done.8.refs_1_, ...), custom_call_target="tpu_custom_call" | custom-call | flops 1000 | bytes 1000 | tf_op jit(solution)/shard_map/finish/pallas_call | solution.py:321
  44.9 0.1 collective-permute-start.15
  45.0 0.5 collective-permute-start.16
  45.5 1.2 %collective-permute-start.14 = (bf16[256,512]{1,0:T(8,128)(2,1)S(1)}, bf16[256,512]{1,0:T(8,128)(2,1)S(1)}, u32[]{:S(2)}, u32[]{:S(2)}) collective-permute-start(bf16[256,512]{1,0:T(8,128)(2,1)S(1)} %get-tuple-element.46), channel_id=1, source_target_pairs={{0,3},{1,2},{2,1},{3,0},{4,7},{5,6},{6,5},{7,4},{8,11},{9,10},{10,... | collective-permute-start | bytes 786440 | tf_op jit(solution)/shard_map/ppermute | solution.py:300
  46.7 0.5 collective-permute-start.13
  47.2 1.0 %collective-permute-done.16.refs_1_ = bf16[256,512]{1,0:T(8,128)(2,1)S(1)} collective-permute-done((bf16[256,512]{1,0:T(8,128)(2,1)S(1)}, bf16[256,512]{1,0:T(8,128)(2,1)S(1)}, u32[]{:S(2)}, u32[]{:S(2)}) %collective-permute-start.16) | collective-permute-done | bytes 262176 | tf_op jit(solution)/shard_map/ppermute | solution.py:300
  48.2 1.8 %out.2.refs_8_ = f32[256,2048]{1,0:T(8,128)S(1)} custom-call(s32[3]{0:T(128)S(1)} %pad_add_fusion.place, bf16[256,512]{1,0:T(8,128)(2,1)S(1)} %get-tuple-element.47.refs_0_, bf16[256,512]{1,0:T(8,128)(2,1)S(1)} %collective-permute-done.16.refs_1_, bf16[512,2048]{1,0:T(8,128)(2,1)S(1)} %copy-done, bf16[512,2048]{1,0:T(8,128)(2,1)S(1)} %collective-permute-done.4.rest_1_.refs_3_), custom_call_target="tpu_custom_call" | custom-call | flops 1000 | bytes 1000 | tf_op jit(solution)/shard_map/out/pallas_call | solution.py:286
  50.0 3.8 %collective-permute-done.14.refs_1_ = bf16[256,512]{1,0:T(8,128)(2,1)S(1)} collective-permute-done((bf16[256,512]{1,0:T(8,128)(2,1)S(1)}, bf16[256,512]{1,0:T(8,128)(2,1)S(1)}, u32[]{:S(2)}, u32[]{:S(2)}) %collective-permute-start.14) | collective-permute-done | bytes 262176 | tf_op jit(solution)/shard_map/ppermute | solution.py:300
  53.8 5.9 %collective-permute-done.13.refs_0_ = bf16[256,512]{1,0:T(8,128)(2,1)S(1)} collective-permute-done((bf16[256,512]{1,0:T(8,128)(2,1)S(1)}, bf16[256,512]{1,0:T(8,128)(2,1)S(1)}, u32[]{:S(2)}, u32[]{:S(2)}) %collective-permute-start.13) | collective-permute-done | bytes 262176 | tf_op jit(solution)/shard_map/ppermute | solution.py:300
  59.7 2.6 %out.3 = bf16[256,2048]{1,0:T(8,128)(2,1)} custom-call(s32[3]{0:T(128)S(1)} %pad_add_fusion.place, bf16[256,512]{1,0:T(8,128)(2,1)S(1)} %collective-permute-done.13.refs_0_, bf16[256,512]{1,0:T(8,128)(2,1)S(1)} %collective-permute-done.14.refs_1_, bf16[112,2048]{1,0:T(8,128)(2,1)S(1)} %after.3.refs_2_, bf16[112,2048]{1,0:T(8,128)(2,1)S(1)} %after.4.refs_3_, ...), custom_call_target="tpu_custom_call" | custom-call | flops 1000 | bytes 1000 | tf_op jit(solution)/shard_map/out/pallas_call | solution.py:286
  (19 shorter events, 0.1 us)
Async XLA Ops:
  0.0 18.8 %collective-permute-start.4 = (bf16[512,2048]{1,0:T(8,128)(2,1)}, bf16[512,2048]{1,0:T(8,128)(2,1)S(1)}, u32[]{:S(2)}, u32[]{:S(2)}) collective-permute-start(bf16[512,2048]{1,0:T(8,128)(2,1)} %refs_2_.1), channel_id=1, source_target_pairs={{0,1},{1,0},{2,3},{3,2},{4,5},{5,4},{6,7},{7,6},{8,9},{9,8},{10,11... | collective-permute-start | bytes 6291464 | tf_op jit(solution)/shard_map/ppermute | solution.py:300
  2.1 16.7 %copy-start.1 = (f32[128,256]{1,0:T(8,128)S(1)}, f32[128,256]{1,0:T(8,128)}, u32[]{:S(2)}) copy-start(f32[128,256]{1,0:T(8,128)} %omega.5) | copy-start | bytes 393220
  2.1 16.7 %collective-permute-start.3 = (bf16[112,2048]{1,0:T(8,128)(2,1)S(1)}, bf16[112,2048]{1,0:T(8,128)(2,1)S(1)}, u32[]{:S(2)}, u32[]{:S(2)}) collective-permute-start(bf16[112,2048]{1,0:T(8,128)(2,1)S(1)} %cut.1._), channel_id=1, source_target_pairs={{0,2},{1,3},{2,0},{3,1},{4,6},{5,7},{6,4},{7,5},{8,10},{9,11},{10,... | collective-permute-start | bytes 1376264 | tf_op jit(solution)/shard_map/ppermute | solution.py:300
  15.1 28.2 %collective-permute-start.11 = (bf16[288,2048]{1,0:T(8,128)(2,1)S(1)}, bf16[288,2048]{1,0:T(8,128)(2,1)S(1)}, u32[]{:S(2)}, u32[]{:S(2)}) collective-permute-start(bf16[288,2048]{1,0:T(8,128)(2,1)S(1)} %get-tuple-element.44), channel_id=1, source_target_pairs={{0,2},{1,3},{2,0},{3,1},{4,6},{5,7},{6,4},{7,5},{8,10},{9,11},{10,... | collective-permute-start | bytes 3538952 | tf_op jit(solution)/shard_map/ppermute | solution.py:300
  15.2 7.0 %collective-permute-start = (bf16[1,144,256]{2,1,0:T(8,128)(2,1)S(1)}, bf16[1,144,256]{2,1,0:T(8,128)(2,1)S(1)}, u32[]{:S(2)}, u32[]{:S(2)}) collective-permute-start(bf16[1,144,256]{2,1,0:T(8,128)(2,1)S(1)} %get-tuple-element.28), channel_id=1, source_target_pairs={{0,4},{4,0},{8,12},{12,8},{16,20},{20,16},{24,28},{28,24},{1,5},{5... | collective-permute-start | bytes 221192 | tf_op jit(solution)/shard_map/ppermute | solution.py:300
  17.3 5.1 %collective-permute-start.1 = (bf16[1,144,256]{2,1,0:T(8,128)(2,1)S(1)}, bf16[1,144,256]{2,1,0:T(8,128)(2,1)S(1)}, u32[]{:S(2)}, u32[]{:S(2)}) collective-permute-start(bf16[1,144,256]{2,1,0:T(8,128)(2,1)S(1)} %get-tuple-element.29), channel_id=1, source_target_pairs={{0,8},{4,12},{8,0},{12,4},{16,24},{20,28},{24,16},{28,20},{1,9},{5... | collective-permute-start | bytes 221192 | tf_op jit(solution)/shard_map/ppermute | solution.py:300
  18.8 5.3 %collective-permute-start.2 = (bf16[1,144,256]{2,1,0:T(8,128)(2,1)S(1)}, bf16[1,144,256]{2,1,0:T(8,128)(2,1)S(1)}, u32[]{:S(2)}, u32[]{:S(2)}) collective-permute-start(bf16[1,144,256]{2,1,0:T(8,128)(2,1)S(1)} %get-tuple-element.30), channel_id=1, source_target_pairs={{0,12},{4,8},{8,4},{12,0},{16,28},{20,24},{24,20},{28,16},{1,13},{... | collective-permute-start | bytes 221192 | tf_op jit(solution)/shard_map/ppermute | solution.py:300
  24.1 10.7 %collective-permute-start.7 = (bf16[112,2048]{1,0:T(8,128)(2,1)S(1)}, bf16[112,2048]{1,0:T(8,128)(2,1)S(1)}, u32[]{:S(2)}, u32[]{:S(2)}) collective-permute-start(bf16[112,2048]{1,0:T(8,128)(2,1)S(1)} %after.3.refs_2_), channel_id=1, source_target_pairs={{0,4},{4,0},{8,12},{12,8},{16,20},{20,16},{24,28},{28,24},{1,5},{5... | collective-permute-start | bytes 1376264 | tf_op jit(solution)/shard_map/ppermute | solution.py:300
  24.7 10.2 %collective-permute-start.6 = (bf16[112,2048]{1,0:T(8,128)(2,1)S(1)}, bf16[112,2048]{1,0:T(8,128)(2,1)S(1)}, u32[]{:S(2)}, u32[]{:S(2)}) collective-permute-start(bf16[112,2048]{1,0:T(8,128)(2,1)S(1)} %after.3.refs_2_), channel_id=1, source_target_pairs={{0,1},{1,0},{2,3},{3,2},{4,5},{5,4},{6,7},{7,6},{8,9},{9,8},{10,11... | collective-permute-start | bytes 1376264 | tf_op jit(solution)/shard_map/ppermute | solution.py:300
  24.7 8.1 %collective-permute-start.5 = (bf16[1,144,256]{2,1,0:T(8,128)(2,1)S(1)}, bf16[1,144,256]{2,1,0:T(8,128)(2,1)S(1)}, u32[]{:S(2)}, u32[]{:S(2)}) collective-permute-start(bf16[1,144,256]{2,1,0:T(8,128)(2,1)S(1)} %group.1.rest_0_.__1_), channel_id=1, source_target_pairs={{0,16},{4,20},{8,24},{12,28},{1,17},{5,21},{9,25},{13,29},{2,18},{... | collective-permute-start | bytes 221192 | tf_op jit(solution)/shard_map/ppermute | solution.py:343
  35.6 7.9 %collective-permute-start.12 = (bf16[112,2048]{1,0:T(8,128)(2,1)S(1)}, bf16[112,2048]{1,0:T(8,128)(2,1)S(1)}, u32[]{:S(2)}, u32[]{:S(2)}) collective-permute-start(bf16[112,2048]{1,0:T(8,128)(2,1)S(1)} %after.4.refs_3_), channel_id=1, source_target_pairs={{0,1},{1,0},{2,3},{3,2},{4,5},{5,4},{6,7},{7,6},{8,9},{9,8},{10,11... | collective-permute-start | bytes 1376264 | tf_op jit(solution)/shard_map/ppermute | solution.py:300
  35.7 7.6 %collective-permute-start.8 = (bf16[1,144,256]{2,1,0:T(8,128)(2,1)S(1)}, bf16[1,144,256]{2,1,0:T(8,128)(2,1)S(1)}, u32[]{:S(2)}, u32[]{:S(2)}) collective-permute-start(bf16[1,144,256]{2,1,0:T(8,128)(2,1)S(1)} %get-tuple-element.39), channel_id=1, source_target_pairs={{0,4},{4,0},{8,12},{12,8},{16,20},{20,16},{24,28},{28,24},{1,5},{5... | collective-permute-start | bytes 221192 | tf_op jit(solution)/shard_map/ppermute | solution.py:300
  37.0 6.3 %collective-permute-start.9 = (bf16[1,144,256]{2,1,0:T(8,128)(2,1)S(1)}, bf16[1,144,256]{2,1,0:T(8,128)(2,1)S(1)}, u32[]{:S(2)}, u32[]{:S(2)}) collective-permute-start(bf16[1,144,256]{2,1,0:T(8,128)(2,1)S(1)} %get-tuple-element.40), channel_id=1, source_target_pairs={{0,8},{4,12},{8,0},{12,4},{16,24},{20,28},{24,16},{28,20},{1,9},{5... | collective-permute-start | bytes 221192 | tf_op jit(solution)/shard_map/ppermute | solution.py:300
  38.3 5.3 %collective-permute-start.10 = (bf16[1,144,256]{2,1,0:T(8,128)(2,1)S(1)}, bf16[1,144,256]{2,1,0:T(8,128)(2,1)S(1)}, u32[]{:S(2)}, u32[]{:S(2)}) collective-permute-start(bf16[1,144,256]{2,1,0:T(8,128)(2,1)S(1)} %get-tuple-element.41), channel_id=1, source_target_pairs={{0,12},{4,8},{8,4},{12,0},{16,28},{20,24},{24,20},{28,16},{1,13},{... | collective-permute-start | bytes 221192 | tf_op jit(solution)/shard_map/ppermute | solution.py:300
  44.9 3.3 %copy-start = (bf16[512,2048]{1,0:T(8,128)(2,1)S(1)}, bf16[512,2048]{1,0:T(8,128)(2,1)}, u32[]{:S(2)}) copy-start(bf16[512,2048]{1,0:T(8,128)(2,1)} %refs_2_.1) | copy-start | bytes 6291460
  44.9 14.8 %collective-permute-start.15 = (bf16[288,2048]{1,0:T(8,128)(2,1)S(1)}, bf16[288,2048]{1,0:T(8,128)(2,1)S(1)}, u32[]{:S(2)}, u32[]{:S(2)}) collective-permute-start(bf16[288,2048]{1,0:T(8,128)(2,1)S(1)} %after.5.refs_4_), channel_id=1, source_target_pairs={{0,1},{1,0},{2,3},{3,2},{4,5},{5,4},{6,7},{7,6},{8,9},{9,8},{10,11... | collective-permute-start | bytes 3538952 | tf_op jit(solution)/shard_map/ppermute | solution.py:300
  45.0 3.2 %collective-permute-start.16 = (bf16[256,512]{1,0:T(8,128)(2,1)S(1)}, bf16[256,512]{1,0:T(8,128)(2,1)S(1)}, u32[]{:S(2)}, u32[]{:S(2)}) collective-permute-start(bf16[256,512]{1,0:T(8,128)(2,1)S(1)} %get-tuple-element.48), channel_id=1, source_target_pairs={{0,1},{1,0},{2,3},{3,2},{4,5},{5,4},{6,7},{7,6},{8,9},{9,8},{10,11... | collective-permute-start | bytes 786440 | tf_op jit(solution)/shard_map/ppermute | solution.py:300
  45.5 8.3 %collective-permute-start.14 = (bf16[256,512]{1,0:T(8,128)(2,1)S(1)}, bf16[256,512]{1,0:T(8,128)(2,1)S(1)}, u32[]{:S(2)}, u32[]{:S(2)}) collective-permute-start(bf16[256,512]{1,0:T(8,128)(2,1)S(1)} %get-tuple-element.46), channel_id=1, source_target_pairs={{0,3},{1,2},{2,1},{3,0},{4,7},{5,6},{6,5},{7,4},{8,11},{9,10},{10,... | collective-permute-start | bytes 786440 | tf_op jit(solution)/shard_map/ppermute | solution.py:300
  46.7 13.1 %collective-permute-start.13 = (bf16[256,512]{1,0:T(8,128)(2,1)S(1)}, bf16[256,512]{1,0:T(8,128)(2,1)S(1)}, u32[]{:S(2)}, u32[]{:S(2)}) collective-permute-start(bf16[256,512]{1,0:T(8,128)(2,1)S(1)} %get-tuple-element.45.__1_), channel_id=1, source_target_pairs={{0,2},{1,3},{2,0},{3,1},{4,6},{5,7},{6,4},{7,5},{8,10},{9,11},{10,... | collective-permute-start | bytes 786440 | tf_op jit(solution)/shard_map/ppermute | solution.py:300

commit v3 on v2

--- a/solution.py
+++ b/solution.py
@@ -43,16 +43,18 @@
 def feature_weights(omega):
     size, features = omega.shape
     high, low = halves(omega * size ** (-0.25))
-    minus = jnp.full((2 * size, features), -1.0, BF16)
-    return jnp.concatenate([high, high, low, low, minus], axis=0)
+    return jnp.concatenate([high, high, low, jnp.full((size, features), -1.0, BF16)], axis=0)
 
 
 def features(rows, weights):
     size = rows.shape[1]
     high, low = halves(rows)
-    square_high, square_low = halves(rows * rows * (0.5 * size ** (-0.5)))
-    left = jnp.concatenate([high, low, high, low, square_high, square_low], axis=1)
-    exponent = dot(left, weights)
+    squares = rows * rows * (0.5 * size ** (-0.5))
+    squares = squares + pltpu.roll(squares, size // 2, 1)
+    square_high, square_low = halves(squares)
+    first = lax.broadcasted_iota(jnp.int32, rows.shape, 1) < size // 2
+    square = jnp.where(first, square_high.astype(F32), square_low.astype(F32)).astype(BF16)
+    exponent = dot(jnp.concatenate([high, low, high, square], axis=1), weights)
     return ((jnp.exp(exponent) + STABILIZER) * (1.0 / math.sqrt(weights.shape[1]))).astype(BF16)
 
 
@@ -243,9 +245,17 @@
             out[:, h * size : (h + 1) * size] = (r[:, :size] / r[:, size:]).astype(BF16)
 
 
-def out_kernel(count, place, *refs):
+def join_kernel(place, near, far, rest, _, out):
+    depth = near.shape[0]
+    even = place[0] == 0
+    out[:depth] = jnp.where(even, near[...], far[...])
+    out[depth : 2 * depth] = jnp.where(even, far[...], near[...])
+    out[2 * depth :] = rest[...]
+
+
+def out_kernel(*refs):
     lefts = refs[: 2]
-    rights, others = refs[2 : 2 + 2 * count], refs[2 + 2 * count :]
+    rights, others = refs[2:4], refs[4:]
     streamed = len(others) > 2
     if streamed:
         before, out, tiles, sem = others
@@ -258,12 +268,7 @@
         here = slice(tile * width, (tile + 1) * width)
         total = before[:, here] if streamed else None
         for i, left in enumerate(lefts):
-            if count == 1:
-                right = rights[i][:, here]
-            else:
-                near, far, rest = [ref[:, here] for ref in rights[3 * i : 3 * i + 3]]
-                even = place[0] == 0
-                right = jnp.concatenate([jnp.where(even, near, far), jnp.where(even, far, near), rest], axis=0)
+            right = rights[i][:, here]
             term = dot(left[...], right)
             total = term if total is None else total + term
         if streamed:
@@ -277,15 +282,15 @@
         copy.wait()
 
 
-def out_product(place, lefts, rights, partial, dtype):
+def out_product(lefts, rights, partial, dtype):
     rows, width = lefts[0].shape[0], rights[0].shape[1]
-    operands = [place] + list(lefts) + [pltpu.with_memory_space_constraint(w, pltpu.VMEM) for w in rights]
+    operands = list(lefts) + [pltpu.with_memory_space_constraint(w, pltpu.VMEM) for w in rights]
     if partial is not None:
         operands.append(partial)
     streamed = dtype == BF16
     return pl.pallas_call(
-        functools.partial(out_kernel, len(rights) // 2),
-        in_specs=[SMEM] + [VMEM] * (len(operands) - 1),
+        out_kernel,
+        in_specs=[VMEM] * len(operands),
         out_specs=HBM if streamed else VMEM,
         out_shape=jax.ShapeDtypeStruct((rows, width), dtype) if streamed else pltpu.VMEM((rows, width), dtype),
         scratch_shapes=[pltpu.VMEM((rows, width), dtype), pltpu.SemaphoreType.DMA((width // TILE,))] if streamed else [],
@@ -330,8 +335,8 @@
     )(*operands)
 
 
-FLOPS = dict(keys=10**10, queries=10**9)
-VMEM_MIB = dict(cut=4, keys=12, queries=12, group=8, scan=8, last=8, finish=8)
+FLOPS = dict(keys=10**10, queries=3 * 10**8)
+VMEM_MIB = dict(join=4, cut=4, keys=12, queries=12, group=8, scan=8, last=8, finish=8)
 
 
 def prefix(place, own, received, message, others):
@@ -370,7 +375,7 @@
     head_at = lax.axis_index("head")
     place = jnp.stack([seq_side, head_at, lax.axis_index("seq") % QUAD]).astype(jnp.int32)
 
-    depth = w_out.shape[0] * 7 // 32
+    depth = w_out.shape[0] // 4
     (part,) = local_call(
         cut_kernel,
         "cut",
@@ -428,20 +433,16 @@
         group_kernel, "group", [own] + received + [partials[0]], [VMEM] * QUAD + [ANY], [(sent[0].shape, BF16)]
     )
     near_part = after(near_part, message)
-    core_part = swap(near_part, "head", 1)
     partials = list(partials) + list(queries(count, [message]))
     far_part = swap(near_part, "seq", 1)
-    kept, *handed = prefix(place, own, received, message, [partials[2], core_part, far_part])
+    kept, *handed = prefix(place, own, received, message, [partials[2]])
     prefixes = [kept] + [swap(v, "seq", k) for k, v in enumerate(handed, 1)]
-    far_part = after(far_part, kept)
-    core_far = swap(far_part, "head", 1)
-
     share = rows // lax.axis_size("head")
     bits = (2, 3, 1, 0)
     to_x, to_diagonal, to_core, mine = local_call(
         functools.partial(finish_kernel, bits, count),
         "finish",
-        [place] + prefixes + partials + [near_rest, core_far],
+        [place] + prefixes + partials + [near_rest, far_part],
         [SMEM] + [VMEM] * (QUAD + len(partials)) + [ANY] * 2,
         [((share, heads * size), BF16)] * len(bits),
     )
@@ -449,11 +450,16 @@
     from_diagonal = swap(to_diagonal, "head", 3)
     from_core = swap(to_core, "head", 1)
 
-    total = out_product(place, [mine, from_core], [w_out, w_core], None, F32)
-    near_rest = after(near_rest, to_x)
-    core_rest = swap(near_rest, "head", 1)
-    rights = [near_part, far_part, near_rest, core_part, core_far, core_rest]
-    return out_product(place, [from_x, from_diagonal], rights, total, BF16)
+    total = out_product([mine, from_core], [w_out, w_core], None, F32)
+    (w_across,) = local_call(
+        join_kernel,
+        "join",
+        [place, near_part, far_part, near_rest, to_x],
+        [SMEM] + [VMEM] * 3 + [ANY],
+        [(w_out.shape, BF16)],
+    )
+    w_diagonal = swap(w_across, "head", 1)
+    return out_product([from_x, from_diagonal], [w_across, w_diagonal], total, BF16)
 
 
 def solution(mesh):

time: 62.6 us -> 59.9 us (0.957)
  waiting for transfers between devices: 18.9 us -> 15.6 us
  starting transfers between devices: 17.9 us -> 19.3 us
  Pallas kernels: 25.3 us -> 24.4 us
    ppermute x16 -> x14, waiting for transfers between devices: 18.9 us -> 15.6 us  [swap(): return lax.ppermute(value, axis, [(i, i ^ bit) for i in range(count)])]
    ppermute x16 -> x14, starting transfers between devices: 13.2 us -> 14.6 us  [swap(): return lax.ppermute(value, axis, [(i, i ^ bit) for i in range(count)])]
    pallas_call x2, Pallas kernels: 4.37 us -> 3.35 us  [out_product(): pl.pallas_call(out_kernel, in_specs=[VMEM] * len(operands), out_specs=HBM...]
    pallas_call x7 -> x8, Pallas kernels: 20.9 us -> 21.1 us  [local_call(): pl.pallas_call(kernel, in_specs=specs, out_specs=[VMEM] * len(outs), out_...]
  transfers between devices with their start and end apart: 17 -> 15, of which waited for: 8 -> 6; matrix products, arithmetic and copies ran while one was open for 0% -> 0% of each run, Pallas kernels for 34% -> 34%
where the time goes in v3:
time: 59.9 us; the launch traced here: 59.7 us
  Pallas kernels  24.4 us (41%)
  starting transfers between devices  19.3 us (32%)
  waiting for transfers between devices  15.6 us (26%)
    pallas_call x8, Pallas kernels, local_call(): pl.pallas_call(kernel, in_specs=specs, out_specs=[VMEM] * len(outs), out_...  21.1 us
    ppermute x14, waiting for transfers between devices, swap(): return lax.ppermute(value, axis, [(i, i ^ bit) for i in range(count)])  15.6 us
    ppermute x14, starting transfers between devices, swap(): return lax.ppermute(value, axis, [(i, i ^ bit) for i in range(count)])  14.6 us
    ppermute x1, starting transfers between devices, prefix(): lax.ppermute(message, 'seq', [(i, i + step) for i in range(count - step)])  4.67 us
    pallas_call x2, Pallas kernels, out_product(): pl.pallas_call(out_kernel, in_specs=[VMEM] * len(operands), out_specs=HBM...  3.35 us
  transfers between devices with their start and end apart: 15, of which 6 were waited for; matrix products, arithmetic and copies ran while one was open for 0% of the time, Pallas kernels for 34%

profile of v3, /device:TPU:0, one launch (start us, length us, event | category | flops | bytes accessed | tf_op | source)
XLA Modules:
  0.0 59.7 jit_solution(6942550696302990220)
XLA Ops:
  0.0 0.5 collective-permute-start.4
  0.5 0.1 pad_add_fusion.place
  0.5 1.6 %cut.1._ = bf16[128,2048]{1,0:T(8,128)(2,1)S(1)} custom-call(s32[3]{0:T(128)S(1)} %pad_add_fusion.place, bf16[512,2048]{1,0:T(8,128)(2,1)} %refs_2_.1), custom_call_target="tpu_custom_call" | custom-call | flops 1000 | bytes 1000 | tf_op jit(solution)/shard_map/cut/pallas_call | solution.py:326
  2.1 0.0 copy-start.1
  2.1 2.6 %collective-permute-start.3 = (bf16[128,2048]{1,0:T(8,128)(2,1)S(1)}, bf16[128,2048]{1,0:T(8,128)(2,1)S(1)}, u32[]{:S(2)}, u32[]{:S(2)}) collective-permute-start(bf16[128,2048]{1,0:T(8,128)(2,1)S(1)} %cut.1._), channel_id=1, source_target_pairs={{0,2},{1,3},{2,0},{3,1},{4,6},{5,7},{6,4},{7,5},{8,10},{9,11},{10,... | collective-permute-start | bytes 1572872 | tf_op jit(solution)/shard_map/ppermute | solution.py:305
  4.7 10.2 %keys.1 = (bf16[1024,2048]{1,0:T(8,128)(2,1)S(1)}, bf16[2048,512]{1,0:T(8,128)(2,1)S(1)}, bf16[4,1024,256]{2,1,0:T(8,128)(2,1)S(1)}, bf16[1024,512]{1,0:T(8,128)...) custom-call(s32[3]{0:T(128)S(1)} %pad_add_fusion.place, ...), custom_call_target="tpu_custom_call" | custom-call | flops 10000000000 | bytes 1000 | tf_op jit(solution)/shard_map/keys/pallas_call | solution.py:326
  15.0 0.1 collective-permute-start.9
  15.0 2.0 %collective-permute-start = (bf16[1,144,256]{2,1,0:T(8,128)(2,1)S(1)}, bf16[1,144,256]{2,1,0:T(8,128)(2,1)S(1)}, u32[]{:S(2)}, u32[]{:S(2)}) collective-permute-start(bf16[1,144,256]{2,1,0:T(8,128)(2,1)S(1)} %get-tuple-element.28), channel_id=1, source_target_pairs={{0,4},{4,0},{8,12},{12,8},{16,20},{20,16},{24,28},{28,24},{1,5},{5... | collective-permute-start | bytes 221192 | tf_op jit(solution)/shard_map/ppermute | solution.py:305
  17.1 1.6 %collective-permute-start.1 = (bf16[1,144,256]{2,1,0:T(8,128)(2,1)S(1)}, bf16[1,144,256]{2,1,0:T(8,128)(2,1)S(1)}, u32[]{:S(2)}, u32[]{:S(2)}) collective-permute-start(bf16[1,144,256]{2,1,0:T(8,128)(2,1)S(1)} %get-tuple-element.29), channel_id=1, source_target_pairs={{0,8},{4,12},{8,0},{12,4},{16,24},{20,28},{24,16},{28,20},{1,9},{5... | collective-permute-start | bytes 221192 | tf_op jit(solution)/shard_map/ppermute | solution.py:305
  18.7 1.4 %collective-permute-start.2 = (bf16[1,144,256]{2,1,0:T(8,128)(2,1)S(1)}, bf16[1,144,256]{2,1,0:T(8,128)(2,1)S(1)}, u32[]{:S(2)}, u32[]{:S(2)}) collective-permute-start(bf16[1,144,256]{2,1,0:T(8,128)(2,1)S(1)} %get-tuple-element.30), channel_id=1, source_target_pairs={{0,12},{4,8},{8,4},{12,0},{16,28},{20,24},{24,20},{28,16},{1,13},{... | collective-permute-start | bytes 221192 | tf_op jit(solution)/shard_map/ppermute | solution.py:305
  20.1 3.2 %queries.2 = (bf16[2,1024,256]{2,1,0:T(8,128)(2,1)S(1)}, f32[1024,512]{1,0:T(8,128)S(1)}) custom-call(bf16[1024,2048]{1,0:T(8,128)(2,1)S(1)} %get-tuple-element.31.tok, bf16[2048,512]{1,0:T(8,128)(2,1)S(1)} %get-tuple-element.32.wq, f32[128,256]{1,0:T(8,128)S(1)} %copy-done.1, bf16[4,1024,256]{2,1,0:T(8,128)(2,1)S(1)} %get-tuple-element.33.feat, ...), custom_call_target="tpu_custom_call" | custom-call | flops 300000000 | bytes 1000 | tf_op jit(solution)/shard_map/queries/pallas_call | solution.py:326
  23.3 0.6 %collective-permute-done.2.three = bf16[1,144,256]{2,1,0:T(8,128)(2,1)S(1)} collective-permute-done((bf16[1,144,256]{2,1,0:T(8,128)(2,1)S(1)}, bf16[1,144,256]{2,1,0:T(8,128)(2,1)S(1)}, u32[]{:S(2)}, u32[]{:S(2)}) %collective-permute-start.2) | collective-permute-done | bytes 73760 | tf_op jit(solution)/shard_map/ppermute | solution.py:305
  24.0 0.6 %collective-permute-start.10 = (bf16[128,2048]{1,0:T(8,128)(2,1)S(1)}, bf16[128,2048]{1,0:T(8,128)(2,1)S(1)}, u32[]{:S(2)}, u32[]{:S(2)}) collective-permute-start(bf16[128,2048]{1,0:T(8,128)(2,1)S(1)} %after.1.near), channel_id=1, source_target_pairs={{0,4},{4,0},{8,12},{12,8},{16,20},{20,16},{24,28},{28,24},{1,5},{5... | collective-permute-start | bytes 1572872 | tf_op jit(solution)/shard_map/ppermute | solution.py:305
  24.6 4.7 %collective-permute-start.5 = (bf16[1,144,256]{2,1,0:T(8,128)(2,1)S(1)}, bf16[1,144,256]{2,1,0:T(8,128)(2,1)S(1)}, u32[]{:S(2)}, u32[]{:S(2)}) collective-permute-start(bf16[1,144,256]{2,1,0:T(8,128)(2,1)S(1)} %group.1.rest_0_.__1_), channel_id=1, source_target_pairs={{0,16},{4,20},{8,24},{12,28},{1,17},{5,21},{9,25},{13,29},{2,18},{... | collective-permute-start | bytes 221192 | tf_op jit(solution)/shard_map/ppermute | solution.py:348
  29.3 3.2 %queries.3 = (bf16[2,1024,256]{2,1,0:T(8,128)(2,1)S(1)}, f32[1024,512]{1,0:T(8,128)S(1)}) custom-call(bf16[1024,2048]{1,0:T(8,128)(2,1)S(1)} %get-tuple-element.31.tok, bf16[2048,512]{1,0:T(8,128)(2,1)S(1)} %get-tuple-element.32.wq, f32[128,256]{1,0:T(8,128)S(1)} %copy-done.1, bf16[4,1024,256]{2,1,0:T(8,128)(2,1)S(1)} %get-tuple-element.33.feat, ...), custom_call_target="tpu_custom_call" | custom-call | flops 300000000 | bytes 1000 | tf_op jit(solution)/shard_map/queries/pallas_call | solution.py:326
  32.5 0.7 %last.1 = (bf16[1,144,256]{2,1,0:T(8,128)(2,1)S(1)}, bf16[1,144,256]{2,1,0:T(8,128)(2,1)S(1)}, bf16[1,144,256]{2,1,0:T(8,128)(2,1)S(1)}, bf16[1,144,256]{2,1,0:T(8,128)(2,1)S(1)}) custom-call(s32[3]{0:T(128)S(1)} %pad_add_fusion.place, f32[1,136,256]{2,1,0:T(8,128)S(1)} %get-tuple-element.27.own, bf16[1,144,256]{2,1,0:T(8,128)(2,1)S(1)} %collective-permute-done.one, ...), custom_call_target="tpu_custom_call" | custom-call | flops 1000 | bytes 1000 | tf_op jit(solution)/shard_map/last/pallas_call | solution.py:326
  33.2 1.5 %collective-permute-start.6 = (bf16[1,144,256]{2,1,0:T(8,128)(2,1)S(1)}, bf16[1,144,256]{2,1,0:T(8,128)(2,1)S(1)}, u32[]{:S(2)}, u32[]{:S(2)}) collective-permute-start(bf16[1,144,256]{2,1,0:T(8,128)(2,1)S(1)} %get-tuple-element.39), channel_id=1, source_target_pairs={{0,4},{4,0},{8,12},{12,8},{16,20},{20,16},{24,28},{28,24},{1,5},{5... | collective-permute-start | bytes 221192 | tf_op jit(solution)/shard_map/ppermute | solution.py:305
  34.7 0.6 %collective-permute-start.7 = (bf16[1,144,256]{2,1,0:T(8,128)(2,1)S(1)}, bf16[1,144,256]{2,1,0:T(8,128)(2,1)S(1)}, u32[]{:S(2)}, u32[]{:S(2)}) collective-permute-start(bf16[1,144,256]{2,1,0:T(8,128)(2,1)S(1)} %get-tuple-element.40), channel_id=1, source_target_pairs={{0,8},{4,12},{8,0},{12,4},{16,24},{20,28},{24,16},{28,20},{1,9},{5... | collective-permute-start | bytes 221192 | tf_op jit(solution)/shard_map/ppermute | solution.py:305
  35.4 1.4 %collective-permute-start.8 = (bf16[1,144,256]{2,1,0:T(8,128)(2,1)S(1)}, bf16[1,144,256]{2,1,0:T(8,128)(2,1)S(1)}, u32[]{:S(2)}, u32[]{:S(2)}) collective-permute-start(bf16[1,144,256]{2,1,0:T(8,128)(2,1)S(1)} %get-tuple-element.41), channel_id=1, source_target_pairs={{0,12},{4,8},{8,4},{12,0},{16,28},{20,24},{24,20},{28,16},{1,13},{... | collective-permute-start | bytes 221192 | tf_op jit(solution)/shard_map/ppermute | solution.py:305
  36.8 3.5 %collective-permute-done.9.refs_8_.rest = bf16[256,2048]{1,0:T(8,128)(2,1)S(1)} collective-permute-done((bf16[256,2048]{1,0:T(8,128)(2,1)S(1)}, bf16[256,2048]{1,0:T(8,128)(2,1)S(1)}, u32[]{:S(2)}, u32[]{:S(2)}) %collective-permute-start.9) | collective-permute-done | bytes 1048608 | tf_op jit(solution)/shard_map/ppermute | solution.py:305
  40.3 0.3 collective-permute-done.8.refs_3_
  40.6 1.3 %finish.1 = (bf16[256,512]{1,0:T(8,128)(2,1)S(1)}, bf16[256,512]{1,0:T(8,128)(2,1)S(1)}, bf16[256,512]{1,0:T(8,128)(2,1)S(1)}, bf16[256,512]{1,0:T(8,128)(2,1)S(1)}) custom-call(s32[3]{0:T(128)S(1)} %pad_add_fusion.place, bf16[1,144,256]{2,1,0:T(8,128)(2,1)S(1)} %get-tuple-element.38.refs_0_, bf16[1,144,256]{2,1,0:T(8,128)(2,1)S(1)} %collective-permute-done.6.refs_1_, ...), custom_call_target="tpu_custom_call" | custom-call | flops 1000 | bytes 1000 | tf_op jit(solution)/shard_map/finish/pallas_call | solution.py:326
  42.0 0.7 %join.1.refs_2_ = bf16[512,2048]{1,0:T(8,128)(2,1)S(1)} custom-call(s32[3]{0:T(128)S(1)} %pad_add_fusion.place, bf16[128,2048]{1,0:T(8,128)(2,1)S(1)} %after.1.near, bf16[128,2048]{1,0:T(8,128)(2,1)S(1)} %collective-permute-done.10.refs_9_.far, bf16[256,2048]{1,0:T(8,128)(2,1)S(1)} %collective-permute-done.9.refs_8_.rest, ...), custom_call_target="tpu_custom_call" | custom-call | flops 1000 | bytes 1000 | tf_op jit(solution)/shard_map/join/pallas_call | solution.py:326
  42.7 0.1 collective-permute-start.13
  42.8 0.5 collective-permute-start.14
  43.3 1.4 %collective-permute-start.12 = (bf16[256,512]{1,0:T(8,128)(2,1)S(1)}, bf16[256,512]{1,0:T(8,128)(2,1)S(1)}, u32[]{:S(2)}, u32[]{:S(2)}) collective-permute-start(bf16[256,512]{1,0:T(8,128)(2,1)S(1)} %get-tuple-element.46), channel_id=1, source_target_pairs={{0,3},{1,2},{2,1},{3,0},{4,7},{5,6},{6,5},{7,4},{8,11},{9,10},{10,... | collective-permute-start | bytes 786440 | tf_op jit(solution)/shard_map/ppermute | solution.py:305
  44.7 0.3 collective-permute-start.11
  45.0 2.3 %collective-permute-done.14.refs_1_ = bf16[256,512]{1,0:T(8,128)(2,1)S(1)} collective-permute-done((bf16[256,512]{1,0:T(8,128)(2,1)S(1)}, bf16[256,512]{1,0:T(8,128)(2,1)S(1)}, u32[]{:S(2)}, u32[]{:S(2)}) %collective-permute-start.14) | collective-permute-done | bytes 262176 | tf_op jit(solution)/shard_map/ppermute | solution.py:305
  47.3 1.3 %out.2.refs_4_ = f32[256,2048]{1,0:T(8,128)S(1)} custom-call(bf16[256,512]{1,0:T(8,128)(2,1)S(1)} %get-tuple-element.47.refs_0_, bf16[256,512]{1,0:T(8,128)(2,1)S(1)} %collective-permute-done.14.refs_1_, bf16[512,2048]{1,0:T(8,128)(2,1)S(1)} %copy-done, bf16[512,2048]{1,0:T(8,128)(2,1)S(1)} %collective-permute-done.4.rest_1_.refs_3_), custom_call_target="tpu_custom_call" | custom-call | flops 1000 | bytes 1000 | tf_op jit(solution)/shard_map/out/pallas_call | solution.py:291
  48.6 3.0 %collective-permute-done.12.refs_1_ = bf16[256,512]{1,0:T(8,128)(2,1)S(1)} collective-permute-done((bf16[256,512]{1,0:T(8,128)(2,1)S(1)}, bf16[256,512]{1,0:T(8,128)(2,1)S(1)}, u32[]{:S(2)}, u32[]{:S(2)}) %collective-permute-start.12) | collective-permute-done | bytes 262176 | tf_op jit(solution)/shard_map/ppermute | solution.py:305
  51.6 5.9 %collective-permute-done.11.refs_0_ = bf16[256,512]{1,0:T(8,128)(2,1)S(1)} collective-permute-done((bf16[256,512]{1,0:T(8,128)(2,1)S(1)}, bf16[256,512]{1,0:T(8,128)(2,1)S(1)}, u32[]{:S(2)}, u32[]{:S(2)}) %collective-permute-start.11) | collective-permute-done | bytes 262176 | tf_op jit(solution)/shard_map/ppermute | solution.py:305
  57.5 2.1 %out.3 = bf16[256,2048]{1,0:T(8,128)(2,1)} custom-call(bf16[256,512]{1,0:T(8,128)(2,1)S(1)} %collective-permute-done.11.refs_0_, bf16[256,512]{1,0:T(8,128)(2,1)S(1)} %collective-permute-done.12.refs_1_, bf16[512,2048]{1,0:T(8,128)(2,1)S(1)} %join.1.refs_2_, bf16[512,2048]{1,0:T(8,128)(2,1)S(1)} %collective-permute-done.13.refs_3_, f32[256,2048]{1,0:T(8,128)S(1)} %out.2.refs_4_), custom_call_target="tpu_custom_call" | custom-call | flops 1000 | bytes 1000 | tf_op jit(solution)/shard_map/out/pallas_call | solution.py:291
  (14 shorter events, 0.1 us)
Async XLA Ops:
  0.0 20.1 %collective-permute-start.4 = (bf16[512,2048]{1,0:T(8,128)(2,1)}, bf16[512,2048]{1,0:T(8,128)(2,1)S(1)}, u32[]{:S(2)}, u32[]{:S(2)}) collective-permute-start(bf16[512,2048]{1,0:T(8,128)(2,1)} %refs_2_.1), channel_id=1, source_target_pairs={{0,1},{1,0},{2,3},{3,2},{4,5},{5,4},{6,7},{7,6},{8,9},{9,8},{10,11... | collective-permute-start | bytes 6291464 | tf_op jit(solution)/shard_map/ppermute | solution.py:305
  2.1 17.9 %copy-start.1 = (f32[128,256]{1,0:T(8,128)S(1)}, f32[128,256]{1,0:T(8,128)}, u32[]{:S(2)}) copy-start(f32[128,256]{1,0:T(8,128)} %omega.5) | copy-start | bytes 393220
  2.1 16.5 %collective-permute-start.3 = (bf16[128,2048]{1,0:T(8,128)(2,1)S(1)}, bf16[128,2048]{1,0:T(8,128)(2,1)S(1)}, u32[]{:S(2)}, u32[]{:S(2)}) collective-permute-start(bf16[128,2048]{1,0:T(8,128)(2,1)S(1)} %cut.1._), channel_id=1, source_target_pairs={{0,2},{1,3},{2,0},{3,1},{4,6},{5,7},{6,4},{7,5},{8,10},{9,11},{10,... | collective-permute-start | bytes 1572872 | tf_op jit(solution)/shard_map/ppermute | solution.py:305
  15.0 25.4 %collective-permute-start.9 = (bf16[256,2048]{1,0:T(8,128)(2,1)S(1)}, bf16[256,2048]{1,0:T(8,128)(2,1)S(1)}, u32[]{:S(2)}, u32[]{:S(2)}) collective-permute-start(bf16[256,2048]{1,0:T(8,128)(2,1)S(1)} %get-tuple-element.44), channel_id=1, source_target_pairs={{0,2},{1,3},{2,0},{3,1},{4,6},{5,7},{6,4},{7,5},{8,10},{9,11},{10,... | collective-permute-start | bytes 3145736 | tf_op jit(solution)/shard_map/ppermute | solution.py:305
  15.0 8.2 %collective-permute-start = (bf16[1,144,256]{2,1,0:T(8,128)(2,1)S(1)}, bf16[1,144,256]{2,1,0:T(8,128)(2,1)S(1)}, u32[]{:S(2)}, u32[]{:S(2)}) collective-permute-start(bf16[1,144,256]{2,1,0:T(8,128)(2,1)S(1)} %get-tuple-element.28), channel_id=1, source_target_pairs={{0,4},{4,0},{8,12},{12,8},{16,20},{20,16},{24,28},{28,24},{1,5},{5... | collective-permute-start | bytes 221192 | tf_op jit(solution)/shard_map/ppermute | solution.py:305
  17.1 6.2 %collective-permute-start.1 = (bf16[1,144,256]{2,1,0:T(8,128)(2,1)S(1)}, bf16[1,144,256]{2,1,0:T(8,128)(2,1)S(1)}, u32[]{:S(2)}, u32[]{:S(2)}) collective-permute-start(bf16[1,144,256]{2,1,0:T(8,128)(2,1)S(1)} %get-tuple-element.29), channel_id=1, source_target_pairs={{0,8},{4,12},{8,0},{12,4},{16,24},{20,28},{24,16},{28,20},{1,9},{5... | collective-permute-start | bytes 221192 | tf_op jit(solution)/shard_map/ppermute | solution.py:305
  18.7 5.3 %collective-permute-start.2 = (bf16[1,144,256]{2,1,0:T(8,128)(2,1)S(1)}, bf16[1,144,256]{2,1,0:T(8,128)(2,1)S(1)}, u32[]{:S(2)}, u32[]{:S(2)}) collective-permute-start(bf16[1,144,256]{2,1,0:T(8,128)(2,1)S(1)} %get-tuple-element.30), channel_id=1, source_target_pairs={{0,12},{4,8},{8,4},{12,0},{16,28},{20,24},{24,20},{28,16},{1,13},{... | collective-permute-start | bytes 221192 | tf_op jit(solution)/shard_map/ppermute | solution.py:305
  24.0 16.6 %collective-permute-start.10 = (bf16[128,2048]{1,0:T(8,128)(2,1)S(1)}, bf16[128,2048]{1,0:T(8,128)(2,1)S(1)}, u32[]{:S(2)}, u32[]{:S(2)}) collective-permute-start(bf16[128,2048]{1,0:T(8,128)(2,1)S(1)} %after.1.near), channel_id=1, source_target_pairs={{0,4},{4,0},{8,12},{12,8},{16,20},{20,16},{24,28},{28,24},{1,5},{5... | collective-permute-start | bytes 1572872 | tf_op jit(solution)/shard_map/ppermute | solution.py:305
  24.6 7.9 %collective-permute-start.5 = (bf16[1,144,256]{2,1,0:T(8,128)(2,1)S(1)}, bf16[1,144,256]{2,1,0:T(8,128)(2,1)S(1)}, u32[]{:S(2)}, u32[]{:S(2)}) collective-permute-start(bf16[1,144,256]{2,1,0:T(8,128)(2,1)S(1)} %group.1.rest_0_.__1_), channel_id=1, source_target_pairs={{0,16},{4,20},{8,24},{12,28},{1,17},{5,21},{9,25},{13,29},{2,18},{... | collective-permute-start | bytes 221192 | tf_op jit(solution)/shard_map/ppermute | solution.py:348
  33.2 7.1 %collective-permute-start.6 = (bf16[1,144,256]{2,1,0:T(8,128)(2,1)S(1)}, bf16[1,144,256]{2,1,0:T(8,128)(2,1)S(1)}, u32[]{:S(2)}, u32[]{:S(2)}) collective-permute-start(bf16[1,144,256]{2,1,0:T(8,128)(2,1)S(1)} %get-tuple-element.39), channel_id=1, source_target_pairs={{0,4},{4,0},{8,12},{12,8},{16,20},{20,16},{24,28},{28,24},{1,5},{5... | collective-permute-start | bytes 221192 | tf_op jit(solution)/shard_map/ppermute | solution.py:305
  34.7 5.6 %collective-permute-start.7 = (bf16[1,144,256]{2,1,0:T(8,128)(2,1)S(1)}, bf16[1,144,256]{2,1,0:T(8,128)(2,1)S(1)}, u32[]{:S(2)}, u32[]{:S(2)}) collective-permute-start(bf16[1,144,256]{2,1,0:T(8,128)(2,1)S(1)} %get-tuple-element.40), channel_id=1, source_target_pairs={{0,8},{4,12},{8,0},{12,4},{16,24},{20,28},{24,16},{28,20},{1,9},{5... | collective-permute-start | bytes 221192 | tf_op jit(solution)/shard_map/ppermute | solution.py:305
  35.4 5.3 %collective-permute-start.8 = (bf16[1,144,256]{2,1,0:T(8,128)(2,1)S(1)}, bf16[1,144,256]{2,1,0:T(8,128)(2,1)S(1)}, u32[]{:S(2)}, u32[]{:S(2)}) collective-permute-start(bf16[1,144,256]{2,1,0:T(8,128)(2,1)S(1)} %get-tuple-element.41), channel_id=1, source_target_pairs={{0,12},{4,8},{8,4},{12,0},{16,28},{20,24},{24,20},{28,16},{1,13},{... | collective-permute-start | bytes 221192 | tf_op jit(solution)/shard_map/ppermute | solution.py:305
  42.0 5.3 %copy-start = (bf16[512,2048]{1,0:T(8,128)(2,1)S(1)}, bf16[512,2048]{1,0:T(8,128)(2,1)}, u32[]{:S(2)}) copy-start(bf16[512,2048]{1,0:T(8,128)(2,1)} %refs_2_.1) | copy-start | bytes 6291460
  42.7 14.8 %collective-permute-start.13 = (bf16[512,2048]{1,0:T(8,128)(2,1)S(1)}, bf16[512,2048]{1,0:T(8,128)(2,1)S(1)}, u32[]{:S(2)}, u32[]{:S(2)}) collective-permute-start(bf16[512,2048]{1,0:T(8,128)(2,1)S(1)} %join.1.refs_2_), channel_id=1, source_target_pairs={{0,1},{1,0},{2,3},{3,2},{4,5},{5,4},{6,7},{7,6},{8,9},{9,8},{10,11... | collective-permute-start | bytes 6291464 | tf_op jit(solution)/shard_map/ppermute | solution.py:305
  42.8 4.5 %collective-permute-start.14 = (bf16[256,512]{1,0:T(8,128)(2,1)S(1)}, bf16[256,512]{1,0:T(8,128)(2,1)S(1)}, u32[]{:S(2)}, u32[]{:S(2)}) collective-permute-start(bf16[256,512]{1,0:T(8,128)(2,1)S(1)} %get-tuple-element.48), channel_id=1, source_target_pairs={{0,1},{1,0},{2,3},{3,2},{4,5},{5,4},{6,7},{7,6},{8,9},{9,8},{10,11... | collective-permute-start | bytes 786440 | tf_op jit(solution)/shard_map/ppermute | solution.py:305
  43.3 8.3 %collective-permute-start.12 = (bf16[256,512]{1,0:T(8,128)(2,1)S(1)}, bf16[256,512]{1,0:T(8,128)(2,1)S(1)}, u32[]{:S(2)}, u32[]{:S(2)}) collective-permute-start(bf16[256,512]{1,0:T(8,128)(2,1)S(1)} %get-tuple-element.46), channel_id=1, source_target_pairs={{0,3},{1,2},{2,1},{3,0},{4,7},{5,6},{6,5},{7,4},{8,11},{9,10},{10,... | collective-permute-start | bytes 786440 | tf_op jit(solution)/shard_map/ppermute | solution.py:305
  44.7 12.8 %collective-permute-start.11 = (bf16[256,512]{1,0:T(8,128)(2,1)S(1)}, bf16[256,512]{1,0:T(8,128)(2,1)S(1)}, u32[]{:S(2)}, u32[]{:S(2)}) collective-permute-start(bf16[256,512]{1,0:T(8,128)(2,1)S(1)} %get-tuple-element.45._), channel_id=1, source_target_pairs={{0,2},{1,3},{2,0},{3,1},{4,6},{5,7},{6,4},{7,5},{8,10},{9,11},{10,... | collective-permute-start | bytes 786440 | tf_op jit(solution)/shard_map/ppermute | solution.py:305

commit v4 on v3

--- a/solution.py
+++ b/solution.py
@@ -87,7 +87,7 @@
 
 
 def key_kernel(
-    place, tok, wk, wv, omega, wq, wo, _, tok_out, wq_out, feat, value, own, sent_1, sent_2, sent_3, local, rest, wk_in, wv_in, om_in, keys, sem
+    place, tok, wk, wv, omega, wq, wo, _, tok_out, wq_out, feat, value, own, sent_1, sent_2, sent_3, local, rest, wv_in, om_in, keys, sem
 ):
     rows = tok.shape[0]
     size = omega.shape[0]
@@ -105,7 +105,6 @@
         part = pl.ds(i * chunk, chunk)
         return fetch(tok.at[part], tok_out.at[part])
 
-    wk_copy = fetch(wk, wk_in)
     token_copies = [token_chunk(0), token_chunk(1)]
     om_copy = fetch(omega, om_in)
     token_copies += [token_chunk(2), token_chunk(3)]
@@ -113,11 +112,10 @@
     wq_copy = fetch(wq, wq_out)
     rest_copy = fetch(wo.at[pl.ds(wo.shape[0] - rest.shape[0], rest.shape[0])], rest)
 
-    wk_copy.wait()
     for i, copy in enumerate(token_copies):
         copy.wait()
         part = slice(i * chunk, (i + 1) * chunk)
-        keys[part] = dot(tok_out[part], wk_in[...])
+        keys[part] = dot(tok_out[part], wk[...])
     wv_copy.wait()
     for start in range(0, rows, BLOCK):
         part = slice(start, start + BLOCK)
@@ -194,7 +192,7 @@
             result[part, h * 2 * size : (h + 1) * 2 * size] = out
 
 
-def group_kernel(own, one, two, three, _, sent):
+def group_kernel(own, one, two, three, _, _2, sent):
     for j in range(own.shape[0]):
         sent[j] = narrow(own[j] + widen(one[j]) + widen(two[j]) + widen(three[j]))
 
@@ -245,17 +243,15 @@
             out[:, h * size : (h + 1) * size] = (r[:, :size] / r[:, size:]).astype(BF16)
 
 
-def join_kernel(place, near, far, rest, _, out):
+def join_kernel(place, near, far, out):
     depth = near.shape[0]
     even = place[0] == 0
     out[:depth] = jnp.where(even, near[...], far[...])
-    out[depth : 2 * depth] = jnp.where(even, far[...], near[...])
-    out[2 * depth :] = rest[...]
-
-
-def out_kernel(*refs):
-    lefts = refs[: 2]
-    rights, others = refs[2:4], refs[4:]
+    out[depth:] = jnp.where(even, far[...], near[...])
+
+
+def out_kernel(count, *refs):
+    lefts, rights, others = refs[:2], refs[2 : 2 + 2 * count], refs[2 + 2 * count :]
     streamed = len(others) > 2
     if streamed:
         before, out, tiles, sem = others
@@ -268,8 +264,8 @@
         here = slice(tile * width, (tile + 1) * width)
         total = before[:, here] if streamed else None
         for i, left in enumerate(lefts):
-            right = rights[i][:, here]
-            term = dot(left[...], right)
+            parts = [ref[:, here] for ref in rights[count * i : count * (i + 1)]]
+            term = dot(left[...], jnp.concatenate(parts, axis=0) if count > 1 else parts[0])
             total = term if total is None else total + term
         if streamed:
             tiles[:, here] = total.astype(out.dtype)
@@ -283,13 +279,13 @@
 
 
 def out_product(lefts, rights, partial, dtype):
-    rows, width = lefts[0].shape[0], rights[0].shape[1]
-    operands = list(lefts) + [pltpu.with_memory_space_constraint(w, pltpu.VMEM) for w in rights]
+    rows, width = lefts[0].shape[0], rights[0][0].shape[1]
+    operands = list(lefts) + [pltpu.with_memory_space_constraint(w, pltpu.VMEM) for group in rights for w in group]
     if partial is not None:
         operands.append(partial)
     streamed = dtype == BF16
     return pl.pallas_call(
-        out_kernel,
+        functools.partial(out_kernel, len(rights[0])),
         in_specs=[VMEM] * len(operands),
         out_specs=HBM if streamed else VMEM,
         out_shape=jax.ShapeDtypeStruct((rows, width), dtype) if streamed else pltpu.VMEM((rows, width), dtype),
@@ -391,8 +387,10 @@
     tok, wq, key_feat, value, own, *sent, local, rest = local_call(
         key_kernel,
         "keys",
-        [place] + [pltpu.with_memory_space_constraint(v, pltpu.HBM) for v in (tokens, w_key, w_value, omega, w_query, w_out)] + [part],
-        [SMEM] + [HBM] * 6 + [ANY],
+        [place, pltpu.with_memory_space_constraint(tokens, pltpu.HBM), pltpu.with_memory_space_constraint(w_key, pltpu.VMEM)]
+        + [pltpu.with_memory_space_constraint(v, pltpu.HBM) for v in (w_value, omega, w_query, w_out)]
+        + [part],
+        [SMEM, HBM, VMEM] + [HBM] * 4 + [ANY],
         [
             ((rows, width), BF16),
             (w_query.shape, BF16),
@@ -406,7 +404,6 @@
             ((w_out.shape[0] - 2 * depth, w_out.shape[1]), BF16),
         ],
         scratch_shapes=[
-            pltpu.VMEM(w_key.shape, BF16),
             pltpu.VMEM(w_value.shape, BF16),
             pltpu.VMEM(omega.shape, F32),
             pltpu.VMEM((rows, heads * size), F32),
@@ -428,21 +425,29 @@
 
     received = [swap(v, "seq", k) for k, v in enumerate(sent, 1)]
     near_rest = swap(rest, "head", 2)
-    partials = queries(0, [near_part, w_core])
+    partials = queries(0, [w_core])
     (message,) = local_call(
-        group_kernel, "group", [own] + received + [partials[0]], [VMEM] * QUAD + [ANY], [(sent[0].shape, BF16)]
+        group_kernel, "group", [own] + received + [partials[0], near_part], [VMEM] * QUAD + [ANY] * 2, [(sent[0].shape, BF16)]
     )
     near_part = after(near_part, message)
     partials = list(partials) + list(queries(count, [message]))
     far_part = swap(near_part, "seq", 1)
     kept, *handed = prefix(place, own, received, message, [partials[2]])
     prefixes = [kept] + [swap(v, "seq", k) for k, v in enumerate(handed, 1)]
+    (joined,) = local_call(
+        join_kernel,
+        "join",
+        [place, near_part, far_part],
+        [SMEM] + [VMEM] * 2,
+        [((2 * depth, w_out.shape[1]), BF16)],
+    )
+
     share = rows // lax.axis_size("head")
     bits = (2, 3, 1, 0)
     to_x, to_diagonal, to_core, mine = local_call(
         functools.partial(finish_kernel, bits, count),
         "finish",
-        [place] + prefixes + partials + [near_rest, far_part],
+        [place] + prefixes + partials + [near_rest, joined],
         [SMEM] + [VMEM] * (QUAD + len(partials)) + [ANY] * 2,
         [((share, heads * size), BF16)] * len(bits),
     )
@@ -450,16 +455,10 @@
     from_diagonal = swap(to_diagonal, "head", 3)
     from_core = swap(to_core, "head", 1)
 
-    total = out_product([mine, from_core], [w_out, w_core], None, F32)
-    (w_across,) = local_call(
-        join_kernel,
-        "join",
-        [place, near_part, far_part, near_rest, to_x],
-        [SMEM] + [VMEM] * 3 + [ANY],
-        [(w_out.shape, BF16)],
-    )
-    w_diagonal = swap(w_across, "head", 1)
-    return out_product([from_x, from_diagonal], [w_across, w_diagonal], total, BF16)
+    total = out_product([mine, from_core], [[w_out], [w_core]], None, F32)
+    pieces = [after(v, to_x) for v in (joined, near_rest)]
+    core_pieces = [swap(v, "head", 1) for v in pieces]
+    return out_product([from_x, from_diagonal], [pieces, core_pieces], total, BF16)
 
 
 def solution(mesh):

time: 59.9 us -> 58.5 us (0.977)
  starting transfers between devices: 19.3 us -> 18.2 us
  Pallas kernels: 24.4 us -> 23.7 us
    ppermute x14 -> x15, starting transfers between devices: 14.6 us -> 13.5 us  [swap(): return lax.ppermute(value, axis, [(i, i ^ bit) for i in range(count)])]
    pallas_call x8, Pallas kernels: 21.1 us -> 20.4 us  [local_call(): pl.pallas_call(kernel, in_specs=specs, out_specs=[VMEM] * len(outs), out_...]
    ppermute x14 -> x15, waiting for transfers between devices: 15.6 us -> 16 us  [swap(): return lax.ppermute(value, axis, [(i, i ^ bit) for i in range(count)])]
  transfers between devices with their start and end apart: 15 -> 16, of which waited for: 6 -> 7; matrix products, arithmetic and copies ran while one was open for 0% -> 0% of each run, Pallas kernels for 34% -> 35%
where the time goes in v4:
time: 58.5 us; the launch traced here: 58.3 us
  Pallas kernels  23.7 us (41%)
  starting transfers between devices  18.2 us (31%)
  waiting for transfers between devices  16 us (27%)
    pallas_call x8, Pallas kernels, local_call(): pl.pallas_call(kernel, in_specs=specs, out_specs=[VMEM] * len(outs), out_...  20.4 us
    ppermute x15, waiting for transfers between devices, swap(): return lax.ppermute(value, axis, [(i, i ^ bit) for i in range(count)])  16 us
    ppermute x15, starting transfers between devices, swap(): return lax.ppermute(value, axis, [(i, i ^ bit) for i in range(count)])  13.5 us
    ppermute x1, starting transfers between devices, prefix(): lax.ppermute(message, 'seq', [(i, i + step) for i in range(count - step)])  4.67 us
    pallas_call x2, Pallas kernels, out_product(): pl.pallas_call(functools.partial(out_kernel, len(rights[0])), in_specs=[V...  3.26 us
  transfers between devices with their start and end apart: 16, of which 7 were waited for; matrix products, arithmetic and copies ran while one was open for 0% of the time, Pallas kernels for 35%

profile of v4, /device:TPU:0, one launch (start us, length us, event | category | flops | bytes accessed | tf_op | source)
XLA Modules:
  0.0 58.3 jit_solution(13730220461332856915)
XLA Ops:
  0.0 0.5 collective-permute-start.3
  0.5 0.1 pad_add_fusion.place
  0.5 1.6 %cut.1._ = bf16[128,2048]{1,0:T(8,128)(2,1)S(1)} custom-call(s32[3]{0:T(128)S(1)} %pad_add_fusion.place, bf16[512,2048]{1,0:T(8,128)(2,1)} %refs_2_.1), custom_call_target="tpu_custom_call" | custom-call | flops 1000 | bytes 1000 | tf_op jit(solution)/shard_map/cut/pallas_call | solution.py:322
  2.2 2.6 %collective-permute-start.4 = (bf16[128,2048]{1,0:T(8,128)(2,1)S(1)}, bf16[128,2048]{1,0:T(8,128)(2,1)S(1)}, u32[]{:S(2)}, u32[]{:S(2)}) collective-permute-start(bf16[128,2048]{1,0:T(8,128)(2,1)S(1)} %cut.1._), channel_id=1, source_target_pairs={{0,2},{1,3},{2,0},{3,1},{4,6},{5,7},{6,4},{7,5},{8,10},{9,11},{10,... | collective-permute-start | bytes 1572872 | tf_op jit(solution)/shard_map/ppermute | solution.py:301
  4.7 9.7 %keys.1 = (bf16[1024,2048]{1,0:T(8,128)(2,1)S(1)}, bf16[2048,512]{1,0:T(8,128)(2,1)S(1)}, bf16[4,1024,256]{2,1,0:T(8,128)(2,1)S(1)}, bf16[1024,512]{1,0:T(8,128)...) custom-call(s32[3]{0:T(128)S(1)} %pad_add_fusion.place, ...), custom_call_target="tpu_custom_call" | custom-call | flops 10000000000 | bytes 1000 | tf_op jit(solution)/shard_map/keys/pallas_call | solution.py:322
  14.4 0.1 collective-permute-start.9
  14.5 2.0 %collective-permute-start = (bf16[1,144,256]{2,1,0:T(8,128)(2,1)S(1)}, bf16[1,144,256]{2,1,0:T(8,128)(2,1)S(1)}, u32[]{:S(2)}, u32[]{:S(2)}) collective-permute-start(bf16[1,144,256]{2,1,0:T(8,128)(2,1)S(1)} %get-tuple-element.28), channel_id=1, source_target_pairs={{0,4},{4,0},{8,12},{12,8},{16,20},{20,16},{24,28},{28,24},{1,5},{5... | collective-permute-start | bytes 221192 | tf_op jit(solution)/shard_map/ppermute | solution.py:301
  16.5 1.6 %collective-permute-start.1 = (bf16[1,144,256]{2,1,0:T(8,128)(2,1)S(1)}, bf16[1,144,256]{2,1,0:T(8,128)(2,1)S(1)}, u32[]{:S(2)}, u32[]{:S(2)}) collective-permute-start(bf16[1,144,256]{2,1,0:T(8,128)(2,1)S(1)} %get-tuple-element.29), channel_id=1, source_target_pairs={{0,8},{4,12},{8,0},{12,4},{16,24},{20,28},{24,16},{28,20},{1,9},{5... | collective-permute-start | bytes 221192 | tf_op jit(solution)/shard_map/ppermute | solution.py:301
  18.1 3.2 %queries.2 = (bf16[2,1024,256]{2,1,0:T(8,128)(2,1)S(1)}, f32[1024,512]{1,0:T(8,128)S(1)}) custom-call(bf16[1024,2048]{1,0:T(8,128)(2,1)S(1)} %get-tuple-element.31.tok, bf16[2048,512]{1,0:T(8,128)(2,1)S(1)} %get-tuple-element.32.wq, f32[128,256]{1,0:T(8,128)S(1)} %copy-done.1, bf16[4,1024,256]{2,1,0:T(8,128)(2,1)S(1)} %get-tuple-element.33.feat, ...), custom_call_target="tpu_custom_call" | custom-call | flops 300000000 | bytes 1000 | tf_op jit(solution)/shard_map/queries/pallas_call | solution.py:322
  21.3 0.3 collective-permute-done.1.two
  21.6 1.8 %collective-permute-done.2.three = bf16[1,144,256]{2,1,0:T(8,128)(2,1)S(1)} collective-permute-done((bf16[1,144,256]{2,1,0:T(8,128)(2,1)S(1)}, bf16[1,144,256]{2,1,0:T(8,128)(2,1)S(1)}, u32[]{:S(2)}, u32[]{:S(2)}) %collective-permute-start.2) | collective-permute-done | bytes 73760 | tf_op jit(solution)/shard_map/ppermute | solution.py:301
  23.4 0.6 collective-permute-start.10
  24.0 4.7 %collective-permute-start.5 = (bf16[1,144,256]{2,1,0:T(8,128)(2,1)S(1)}, bf16[1,144,256]{2,1,0:T(8,128)(2,1)S(1)}, u32[]{:S(2)}, u32[]{:S(2)}) collective-permute-start(bf16[1,144,256]{2,1,0:T(8,128)(2,1)S(1)} %group.1.rest_0_.__1_), channel_id=1, source_target_pairs={{0,16},{4,20},{8,24},{12,28},{1,17},{5,21},{9,25},{13,29},{2,18},{... | collective-permute-start | bytes 221192 | tf_op jit(solution)/shard_map/ppermute | solution.py:344
  28.7 3.2 %queries.3 = (bf16[2,1024,256]{2,1,0:T(8,128)(2,1)S(1)}, f32[1024,512]{1,0:T(8,128)S(1)}) custom-call(bf16[1024,2048]{1,0:T(8,128)(2,1)S(1)} %get-tuple-element.31.tok, bf16[2048,512]{1,0:T(8,128)(2,1)S(1)} %get-tuple-element.32.wq, f32[128,256]{1,0:T(8,128)S(1)} %copy-done.1, bf16[4,1024,256]{2,1,0:T(8,128)(2,1)S(1)} %get-tuple-element.33.feat, ...), custom_call_target="tpu_custom_call" | custom-call | flops 300000000 | bytes 1000 | tf_op jit(solution)/shard_map/queries/pallas_call | solution.py:322
  31.9 0.7 %last.1 = (bf16[1,144,256]{2,1,0:T(8,128)(2,1)S(1)}, bf16[1,144,256]{2,1,0:T(8,128)(2,1)S(1)}, bf16[1,144,256]{2,1,0:T(8,128)(2,1)S(1)}, bf16[1,144,256]{2,1,0:T(8,128)(2,1)S(1)}) custom-call(s32[3]{0:T(128)S(1)} %pad_add_fusion.place, f32[1,136,256]{2,1,0:T(8,128)S(1)} %get-tuple-element.27.own, bf16[1,144,256]{2,1,0:T(8,128)(2,1)S(1)} %collective-permute-done.one, ...), custom_call_target="tpu_custom_call" | custom-call | flops 1000 | bytes 1000 | tf_op jit(solution)/shard_map/last/pallas_call | solution.py:322
  32.6 1.6 %collective-permute-start.6 = (bf16[1,144,256]{2,1,0:T(8,128)(2,1)S(1)}, bf16[1,144,256]{2,1,0:T(8,128)(2,1)S(1)}, u32[]{:S(2)}, u32[]{:S(2)}) collective-permute-start(bf16[1,144,256]{2,1,0:T(8,128)(2,1)S(1)} %get-tuple-element.39), channel_id=1, source_target_pairs={{0,4},{4,0},{8,12},{12,8},{16,20},{20,16},{24,28},{28,24},{1,5},{5... | collective-permute-start | bytes 221192 | tf_op jit(solution)/shard_map/ppermute | solution.py:301
  34.1 0.4 collective-permute-start.7
  34.6 1.5 %collective-permute-start.8 = (bf16[1,144,256]{2,1,0:T(8,128)(2,1)S(1)}, bf16[1,144,256]{2,1,0:T(8,128)(2,1)S(1)}, u32[]{:S(2)}, u32[]{:S(2)}) collective-permute-start(bf16[1,144,256]{2,1,0:T(8,128)(2,1)S(1)} %get-tuple-element.41), channel_id=1, source_target_pairs={{0,12},{4,8},{8,4},{12,0},{16,28},{20,24},{24,20},{28,16},{1,13},{... | collective-permute-start | bytes 221192 | tf_op jit(solution)/shard_map/ppermute | solution.py:301
  36.1 1.0 %collective-permute-done.10.far = bf16[128,2048]{1,0:T(8,128)(2,1)S(1)} collective-permute-done((bf16[128,2048]{1,0:T(8,128)(2,1)S(1)}, bf16[128,2048]{1,0:T(8,128)(2,1)S(1)}, u32[]{:S(2)}, u32[]{:S(2)}) %collective-permute-start.10) | collective-permute-done | bytes 524320 | tf_op jit(solution)/shard_map/ppermute | solution.py:301
  37.1 0.7 %join.1.refs_9_.__0_ = bf16[256,2048]{1,0:T(8,128)(2,1)S(1)} custom-call(s32[3]{0:T(128)S(1)} %pad_add_fusion.place, bf16[128,2048]{1,0:T(8,128)(2,1)S(1)} %after.3.near, bf16[128,2048]{1,0:T(8,128)(2,1)S(1)} %collective-permute-done.10.far), custom_call_target="tpu_custom_call" | custom-call | flops 1000 | bytes 1000 | tf_op jit(solution)/shard_map/join/pallas_call | solution.py:322
  37.8 2.0 %collective-permute-done.9.refs_8_.__0_ = bf16[256,2048]{1,0:T(8,128)(2,1)S(1)} collective-permute-done((bf16[256,2048]{1,0:T(8,128)(2,1)S(1)}, bf16[256,2048]{1,0:T(8,128)(2,1)S(1)}, u32[]{:S(2)}, u32[]{:S(2)}) %collective-permute-start.9) | collective-permute-done | bytes 1048608 | tf_op jit(solution)/shard_map/ppermute | solution.py:301
  39.8 1.4 %finish.1 = (bf16[256,512]{1,0:T(8,128)(2,1)S(1)}, bf16[256,512]{1,0:T(8,128)(2,1)S(1)}, bf16[256,512]{1,0:T(8,128)(2,1)S(1)}, bf16[256,512]{1,0:T(8,128)(2,1)S(1)}) custom-call(s32[3]{0:T(128)S(1)} %pad_add_fusion.place, bf16[1,144,256]{2,1,0:T(8,128)(2,1)S(1)} %get-tuple-element.38.refs_0_, bf16[1,144,256]{2,1,0:T(8,128)(2,1)S(1)} %collective-permute-done.6.refs_1_, ...), custom_call_target="tpu_custom_call" | custom-call | flops 1000 | bytes 1000 | tf_op jit(solution)/shard_map/finish/pallas_call | solution.py:322
  41.2 0.1 collective-permute-start.13
  41.3 0.5 collective-permute-start.14
  41.8 0.1 collective-permute-start.15
  41.9 1.7 %collective-permute-start.12 = (bf16[256,512]{1,0:T(8,128)(2,1)S(1)}, bf16[256,512]{1,0:T(8,128)(2,1)S(1)}, u32[]{:S(2)}, u32[]{:S(2)}) collective-permute-start(bf16[256,512]{1,0:T(8,128)(2,1)S(1)} %get-tuple-element.46), channel_id=1, source_target_pairs={{0,3},{1,2},{2,1},{3,0},{4,7},{5,6},{6,5},{7,4},{8,11},{9,10},{10,... | collective-permute-start | bytes 786440 | tf_op jit(solution)/shard_map/ppermute | solution.py:301
  43.6 0.3 collective-permute-start.11
  44.0 1.9 %collective-permute-done.15.refs_1_ = bf16[256,512]{1,0:T(8,128)(2,1)S(1)} collective-permute-done((bf16[256,512]{1,0:T(8,128)(2,1)S(1)}, bf16[256,512]{1,0:T(8,128)(2,1)S(1)}, u32[]{:S(2)}, u32[]{:S(2)}) %collective-permute-start.15) | collective-permute-done | bytes 262176 | tf_op jit(solution)/shard_map/ppermute | solution.py:301
  45.8 1.2 %out.2.refs_6_ = f32[256,2048]{1,0:T(8,128)S(1)} custom-call(bf16[256,512]{1,0:T(8,128)(2,1)S(1)} %get-tuple-element.47.refs_0_, bf16[256,512]{1,0:T(8,128)(2,1)S(1)} %collective-permute-done.15.refs_1_, bf16[512,2048]{1,0:T(8,128)(2,1)S(1)} %copy-done, bf16[512,2048]{1,0:T(8,128)(2,1)S(1)} %collective-permute-done.3.rest_0_.refs_3_), custom_call_target="tpu_custom_call" | custom-call | flops 1000 | bytes 1000 | tf_op jit(solution)/shard_map/out/pallas_call | solution.py:287
  47.1 3.2 %collective-permute-done.12.refs_1_ = bf16[256,512]{1,0:T(8,128)(2,1)S(1)} collective-permute-done((bf16[256,512]{1,0:T(8,128)(2,1)S(1)}, bf16[256,512]{1,0:T(8,128)(2,1)S(1)}, u32[]{:S(2)}, u32[]{:S(2)}) %collective-permute-start.12) | collective-permute-done | bytes 262176 | tf_op jit(solution)/shard_map/ppermute | solution.py:301
  50.3 5.8 %collective-permute-done.11.refs_0_ = bf16[256,512]{1,0:T(8,128)(2,1)S(1)} collective-permute-done((bf16[256,512]{1,0:T(8,128)(2,1)S(1)}, bf16[256,512]{1,0:T(8,128)(2,1)S(1)}, u32[]{:S(2)}, u32[]{:S(2)}) %collective-permute-start.11) | collective-permute-done | bytes 262176 | tf_op jit(solution)/shard_map/ppermute | solution.py:301
  56.1 2.0 %out.3 = bf16[256,2048]{1,0:T(8,128)(2,1)} custom-call(bf16[256,512]{1,0:T(8,128)(2,1)S(1)} %collective-permute-done.11.refs_0_, bf16[256,512]{1,0:T(8,128)(2,1)S(1)} %collective-permute-done.12.refs_1_, bf16[256,2048]{1,0:T(8,128)(2,1)S(1)} %after.4.refs_2_, bf16[256,2048]{1,0:T(8,128)(2,1)S(1)} %after.5.refs_3_, ...), custom_call_target="tpu_custom_call" | custom-call | flops 1000 | bytes 1000 | tf_op jit(solution)/shard_map/out/pallas_call | solution.py:287
  (20 shorter events, 0.1 us)
Async XLA Ops:
  0.0 18.1 %collective-permute-start.3 = (bf16[512,2048]{1,0:T(8,128)(2,1)}, bf16[512,2048]{1,0:T(8,128)(2,1)S(1)}, u32[]{:S(2)}, u32[]{:S(2)}) collective-permute-start(bf16[512,2048]{1,0:T(8,128)(2,1)} %refs_2_.1), channel_id=1, source_target_pairs={{0,1},{1,0},{2,3},{3,2},{4,5},{5,4},{6,7},{7,6},{8,9},{9,8},{10,11... | collective-permute-start | bytes 6291464 | tf_op jit(solution)/shard_map/ppermute | solution.py:301
  0.5 4.3 %copy-start.2 = (bf16[2048,512]{1,0:T(8,128)(2,1)S(1)}, bf16[2048,512]{1,0:T(8,128)(2,1)}, u32[]{:S(2)}) copy-start(bf16[2048,512]{1,0:T(8,128)(2,1)} %wk.1) | copy-start | bytes 6291460
  2.2 15.9 %copy-start.1 = (f32[128,256]{1,0:T(8,128)S(1)}, f32[128,256]{1,0:T(8,128)}, u32[]{:S(2)}) copy-start(f32[128,256]{1,0:T(8,128)} %omega.5) | copy-start | bytes 393220
  2.2 21.2 %collective-permute-start.4 = (bf16[128,2048]{1,0:T(8,128)(2,1)S(1)}, bf16[128,2048]{1,0:T(8,128)(2,1)S(1)}, u32[]{:S(2)}, u32[]{:S(2)}) collective-permute-start(bf16[128,2048]{1,0:T(8,128)(2,1)S(1)} %cut.1._), channel_id=1, source_target_pairs={{0,2},{1,3},{2,0},{3,1},{4,6},{5,7},{6,4},{7,5},{8,10},{9,11},{10,... | collective-permute-start | bytes 1572872 | tf_op jit(solution)/shard_map/ppermute | solution.py:301
  14.4 25.4 %collective-permute-start.9 = (bf16[256,2048]{1,0:T(8,128)(2,1)S(1)}, bf16[256,2048]{1,0:T(8,128)(2,1)S(1)}, u32[]{:S(2)}, u32[]{:S(2)}) collective-permute-start(bf16[256,2048]{1,0:T(8,128)(2,1)S(1)} %get-tuple-element.44), channel_id=1, source_target_pairs={{0,2},{1,3},{2,0},{3,1},{4,6},{5,7},{6,4},{7,5},{8,10},{9,11},{10,... | collective-permute-start | bytes 3145736 | tf_op jit(solution)/shard_map/ppermute | solution.py:301
  14.5 6.8 %collective-permute-start = (bf16[1,144,256]{2,1,0:T(8,128)(2,1)S(1)}, bf16[1,144,256]{2,1,0:T(8,128)(2,1)S(1)}, u32[]{:S(2)}, u32[]{:S(2)}) collective-permute-start(bf16[1,144,256]{2,1,0:T(8,128)(2,1)S(1)} %get-tuple-element.28), channel_id=1, source_target_pairs={{0,4},{4,0},{8,12},{12,8},{16,20},{20,16},{24,28},{28,24},{1,5},{5... | collective-permute-start | bytes 221192 | tf_op jit(solution)/shard_map/ppermute | solution.py:301
  16.5 5.1 %collective-permute-start.1 = (bf16[1,144,256]{2,1,0:T(8,128)(2,1)S(1)}, bf16[1,144,256]{2,1,0:T(8,128)(2,1)S(1)}, u32[]{:S(2)}, u32[]{:S(2)}) collective-permute-start(bf16[1,144,256]{2,1,0:T(8,128)(2,1)S(1)} %get-tuple-element.29), channel_id=1, source_target_pairs={{0,8},{4,12},{8,0},{12,4},{16,24},{20,28},{24,16},{28,20},{1,9},{5... | collective-permute-start | bytes 221192 | tf_op jit(solution)/shard_map/ppermute | solution.py:301
  18.1 5.3 %collective-permute-start.2 = (bf16[1,144,256]{2,1,0:T(8,128)(2,1)S(1)}, bf16[1,144,256]{2,1,0:T(8,128)(2,1)S(1)}, u32[]{:S(2)}, u32[]{:S(2)}) collective-permute-start(bf16[1,144,256]{2,1,0:T(8,128)(2,1)S(1)} %get-tuple-element.30), channel_id=1, source_target_pairs={{0,12},{4,8},{8,4},{12,0},{16,28},{20,24},{24,20},{28,16},{1,13},{... | collective-permute-start | bytes 221192 | tf_op jit(solution)/shard_map/ppermute | solution.py:301
  23.4 13.7 %collective-permute-start.10 = (bf16[128,2048]{1,0:T(8,128)(2,1)S(1)}, bf16[128,2048]{1,0:T(8,128)(2,1)S(1)}, u32[]{:S(2)}, u32[]{:S(2)}) collective-permute-start(bf16[128,2048]{1,0:T(8,128)(2,1)S(1)} %after.3.near), channel_id=1, source_target_pairs={{0,4},{4,0},{8,12},{12,8},{16,20},{20,16},{24,28},{28,24},{1,5},{5... | collective-permute-start | bytes 1572872 | tf_op jit(solution)/shard_map/ppermute | solution.py:301
  24.0 7.9 %collective-permute-start.5 = (bf16[1,144,256]{2,1,0:T(8,128)(2,1)S(1)}, bf16[1,144,256]{2,1,0:T(8,128)(2,1)S(1)}, u32[]{:S(2)}, u32[]{:S(2)}) collective-permute-start(bf16[1,144,256]{2,1,0:T(8,128)(2,1)S(1)} %group.1.rest_0_.__1_), channel_id=1, source_target_pairs={{0,16},{4,20},{8,24},{12,28},{1,17},{5,21},{9,25},{13,29},{2,18},{... | collective-permute-start | bytes 221192 | tf_op jit(solution)/shard_map/ppermute | solution.py:344
  32.6 7.2 %collective-permute-start.6 = (bf16[1,144,256]{2,1,0:T(8,128)(2,1)S(1)}, bf16[1,144,256]{2,1,0:T(8,128)(2,1)S(1)}, u32[]{:S(2)}, u32[]{:S(2)}) collective-permute-start(bf16[1,144,256]{2,1,0:T(8,128)(2,1)S(1)} %get-tuple-element.39), channel_id=1, source_target_pairs={{0,4},{4,0},{8,12},{12,8},{16,20},{20,16},{24,28},{28,24},{1,5},{5... | collective-permute-start | bytes 221192 | tf_op jit(solution)/shard_map/ppermute | solution.py:301
  34.1 5.7 %collective-permute-start.7 = (bf16[1,144,256]{2,1,0:T(8,128)(2,1)S(1)}, bf16[1,144,256]{2,1,0:T(8,128)(2,1)S(1)}, u32[]{:S(2)}, u32[]{:S(2)}) collective-permute-start(bf16[1,144,256]{2,1,0:T(8,128)(2,1)S(1)} %get-tuple-element.40), channel_id=1, source_target_pairs={{0,8},{4,12},{8,0},{12,4},{16,24},{20,28},{24,16},{28,20},{1,9},{5... | collective-permute-start | bytes 221192 | tf_op jit(solution)/shard_map/ppermute | solution.py:301
  34.6 5.3 %collective-permute-start.8 = (bf16[1,144,256]{2,1,0:T(8,128)(2,1)S(1)}, bf16[1,144,256]{2,1,0:T(8,128)(2,1)S(1)}, u32[]{:S(2)}, u32[]{:S(2)}) collective-permute-start(bf16[1,144,256]{2,1,0:T(8,128)(2,1)S(1)} %get-tuple-element.41), channel_id=1, source_target_pairs={{0,12},{4,8},{8,4},{12,0},{16,28},{20,24},{24,20},{28,16},{1,13},{... | collective-permute-start | bytes 221192 | tf_op jit(solution)/shard_map/ppermute | solution.py:301
  41.2 4.6 %copy-start = (bf16[512,2048]{1,0:T(8,128)(2,1)S(1)}, bf16[512,2048]{1,0:T(8,128)(2,1)}, u32[]{:S(2)}) copy-start(bf16[512,2048]{1,0:T(8,128)(2,1)} %refs_2_.1) | copy-start | bytes 6291460
  41.2 14.9 %collective-permute-start.13 = (bf16[256,2048]{1,0:T(8,128)(2,1)S(1)}, bf16[256,2048]{1,0:T(8,128)(2,1)S(1)}, u32[]{:S(2)}, u32[]{:S(2)}) collective-permute-start(bf16[256,2048]{1,0:T(8,128)(2,1)S(1)} %after.4.refs_2_), channel_id=1, source_target_pairs={{0,1},{1,0},{2,3},{3,2},{4,5},{5,4},{6,7},{7,6},{8,9},{9,8},{10,11... | collective-permute-start | bytes 3145736 | tf_op jit(solution)/shard_map/ppermute | solution.py:301
  41.3 14.8 %collective-permute-start.14 = (bf16[256,2048]{1,0:T(8,128)(2,1)S(1)}, bf16[256,2048]{1,0:T(8,128)(2,1)S(1)}, u32[]{:S(2)}, u32[]{:S(2)}) collective-permute-start(bf16[256,2048]{1,0:T(8,128)(2,1)S(1)} %after.5.refs_3_), channel_id=1, source_target_pairs={{0,1},{1,0},{2,3},{3,2},{4,5},{5,4},{6,7},{7,6},{8,9},{9,8},{10,11... | collective-permute-start | bytes 3145736 | tf_op jit(solution)/shard_map/ppermute | solution.py:301
  41.8 4.0 %collective-permute-start.15 = (bf16[256,512]{1,0:T(8,128)(2,1)S(1)}, bf16[256,512]{1,0:T(8,128)(2,1)S(1)}, u32[]{:S(2)}, u32[]{:S(2)}) collective-permute-start(bf16[256,512]{1,0:T(8,128)(2,1)S(1)} %get-tuple-element.48), channel_id=1, source_target_pairs={{0,1},{1,0},{2,3},{3,2},{4,5},{5,4},{6,7},{7,6},{8,9},{9,8},{10,11... | collective-permute-start | bytes 786440 | tf_op jit(solution)/shard_map/ppermute | solution.py:301
  41.9 8.4 %collective-permute-start.12 = (bf16[256,512]{1,0:T(8,128)(2,1)S(1)}, bf16[256,512]{1,0:T(8,128)(2,1)S(1)}, u32[]{:S(2)}, u32[]{:S(2)}) collective-permute-start(bf16[256,512]{1,0:T(8,128)(2,1)S(1)} %get-tuple-element.46), channel_id=1, source_target_pairs={{0,3},{1,2},{2,1},{3,0},{4,7},{5,6},{6,5},{7,4},{8,11},{9,10},{10,... | collective-permute-start | bytes 786440 | tf_op jit(solution)/shard_map/ppermute | solution.py:301
  43.6 12.5 %collective-permute-start.11 = (bf16[256,512]{1,0:T(8,128)(2,1)S(1)}, bf16[256,512]{1,0:T(8,128)(2,1)S(1)}, u32[]{:S(2)}, u32[]{:S(2)}) collective-permute-start(bf16[256,512]{1,0:T(8,128)(2,1)S(1)} %get-tuple-element.45.__1_), channel_id=1, source_target_pairs={{0,2},{1,3},{2,0},{3,1},{4,6},{5,7},{6,4},{7,5},{8,10},{9,11},{10,... | collective-permute-start | bytes 786440 | tf_op jit(solution)/shard_map/ppermute | solution.py:301

commit v5 on v4

--- a/solution.py
+++ b/solution.py
@@ -447,8 +447,8 @@
     to_x, to_diagonal, to_core, mine = local_call(
         functools.partial(finish_kernel, bits, count),
         "finish",
-        [place] + prefixes + partials + [near_rest, joined],
-        [SMEM] + [VMEM] * (QUAD + len(partials)) + [ANY] * 2,
+        [place] + prefixes + partials + [joined],
+        [SMEM] + [VMEM] * (QUAD + len(partials)) + [ANY],
         [((share, heads * size), BF16)] * len(bits),
     )
     from_x = swap(to_x, "head", 2)

time: 58.5 us -> 58.5 us (level)
  transfers between devices with their start and end apart: 16 -> 16, of which waited for: 7 -> 9; matrix products, arithmetic and copies ran while one was open for 0% -> 0% of each run, Pallas kernels for 35% -> 37%
where the time goes in v5:
time: 58.5 us; the launch traced here: 58.4 us
  Pallas kernels  23.7 us (41%)
  starting transfers between devices  18.2 us (31%)
  waiting for transfers between devices  16 us (27%)
    pallas_call x8, Pallas kernels, local_call(): pl.pallas_call(kernel, in_specs=specs, out_specs=[VMEM] * len(outs), out_...  20.4 us
    ppermute x15, waiting for transfers between devices, swap(): return lax.ppermute(value, axis, [(i, i ^ bit) for i in range(count)])  16 us
    ppermute x15, starting transfers between devices, swap(): return lax.ppermute(value, axis, [(i, i ^ bit) for i in range(count)])  13.5 us
    ppermute x1, starting transfers between devices, prefix(): lax.ppermute(message, 'seq', [(i, i + step) for i in range(count - step)])  4.67 us
    pallas_call x2, Pallas kernels, out_product(): pl.pallas_call(functools.partial(out_kernel, len(rights[0])), in_specs=[V...  3.33 us
  transfers between devices with their start and end apart: 16, of which 9 were waited for; matrix products, arithmetic and copies ran while one was open for 0% of the time, Pallas kernels for 37%

profile of v5, /device:TPU:0, one launch (start us, length us, event | category | flops | bytes accessed | tf_op | source)
XLA Modules:
  0.0 58.4 jit_solution(7556712391387080523)
XLA Ops:
  0.0 0.5 collective-permute-start.3
  0.5 1.6 %cut.1._ = bf16[128,2048]{1,0:T(8,128)(2,1)S(1)} custom-call(s32[3]{0:T(128)S(1)} %pad_add_fusion.place, bf16[512,2048]{1,0:T(8,128)(2,1)} %refs_2_.1), custom_call_target="tpu_custom_call" | custom-call | flops 1000 | bytes 1000 | tf_op jit(solution)/shard_map/cut/pallas_call | solution.py:322
  2.2 2.6 %collective-permute-start.4 = (bf16[128,2048]{1,0:T(8,128)(2,1)S(1)}, bf16[128,2048]{1,0:T(8,128)(2,1)S(1)}, u32[]{:S(2)}, u32[]{:S(2)}) collective-permute-start(bf16[128,2048]{1,0:T(8,128)(2,1)S(1)} %cut.1._), channel_id=1, source_target_pairs={{0,2},{1,3},{2,0},{3,1},{4,6},{5,7},{6,4},{7,5},{8,10},{9,11},{10,... | collective-permute-start | bytes 1572872 | tf_op jit(solution)/shard_map/ppermute | solution.py:301
  4.7 9.7 %keys.1 = (bf16[1024,2048]{1,0:T(8,128)(2,1)S(1)}, bf16[2048,512]{1,0:T(8,128)(2,1)S(1)}, bf16[4,1024,256]{2,1,0:T(8,128)(2,1)S(1)}, bf16[1024,512]{1,0:T(8,128)...) custom-call(s32[3]{0:T(128)S(1)} %pad_add_fusion.place, ...), custom_call_target="tpu_custom_call" | custom-call | flops 10000000000 | bytes 1000 | tf_op jit(solution)/shard_map/keys/pallas_call | solution.py:322
  14.4 0.1 collective-permute-start.12
  14.5 2.0 %collective-permute-start = (bf16[1,144,256]{2,1,0:T(8,128)(2,1)S(1)}, bf16[1,144,256]{2,1,0:T(8,128)(2,1)S(1)}, u32[]{:S(2)}, u32[]{:S(2)}) collective-permute-start(bf16[1,144,256]{2,1,0:T(8,128)(2,1)S(1)} %get-tuple-element.28), channel_id=1, source_target_pairs={{0,4},{4,0},{8,12},{12,8},{16,20},{20,16},{24,28},{28,24},{1,5},{5... | collective-permute-start | bytes 221192 | tf_op jit(solution)/shard_map/ppermute | solution.py:301
  16.5 1.6 %collective-permute-start.1 = (bf16[1,144,256]{2,1,0:T(8,128)(2,1)S(1)}, bf16[1,144,256]{2,1,0:T(8,128)(2,1)S(1)}, u32[]{:S(2)}, u32[]{:S(2)}) collective-permute-start(bf16[1,144,256]{2,1,0:T(8,128)(2,1)S(1)} %get-tuple-element.29), channel_id=1, source_target_pairs={{0,8},{4,12},{8,0},{12,4},{16,24},{20,28},{24,16},{28,20},{1,9},{5... | collective-permute-start | bytes 221192 | tf_op jit(solution)/shard_map/ppermute | solution.py:301
  18.1 3.2 %queries.2 = (bf16[2,1024,256]{2,1,0:T(8,128)(2,1)S(1)}, f32[1024,512]{1,0:T(8,128)S(1)}) custom-call(bf16[1024,2048]{1,0:T(8,128)(2,1)S(1)} %get-tuple-element.31.tok, bf16[2048,512]{1,0:T(8,128)(2,1)S(1)} %get-tuple-element.32.wq, f32[128,256]{1,0:T(8,128)S(1)} %copy-done.1, bf16[4,1024,256]{2,1,0:T(8,128)(2,1)S(1)} %get-tuple-element.33.feat, ...), custom_call_target="tpu_custom_call" | custom-call | flops 300000000 | bytes 1000 | tf_op jit(solution)/shard_map/queries/pallas_call | solution.py:322
  21.3 0.3 collective-permute-done.1.two
  21.6 1.8 %collective-permute-done.2.three = bf16[1,144,256]{2,1,0:T(8,128)(2,1)S(1)} collective-permute-done((bf16[1,144,256]{2,1,0:T(8,128)(2,1)S(1)}, bf16[1,144,256]{2,1,0:T(8,128)(2,1)S(1)}, u32[]{:S(2)}, u32[]{:S(2)}) %collective-permute-start.2) | collective-permute-done | bytes 73760 | tf_op jit(solution)/shard_map/ppermute | solution.py:301
  23.4 0.6 collective-permute-start.9
  24.0 4.7 %collective-permute-start.5 = (bf16[1,144,256]{2,1,0:T(8,128)(2,1)S(1)}, bf16[1,144,256]{2,1,0:T(8,128)(2,1)S(1)}, u32[]{:S(2)}, u32[]{:S(2)}) collective-permute-start(bf16[1,144,256]{2,1,0:T(8,128)(2,1)S(1)} %group.1.rest_0_.__1_), channel_id=1, source_target_pairs={{0,16},{4,20},{8,24},{12,28},{1,17},{5,21},{9,25},{13,29},{2,18},{... | collective-permute-start | bytes 221192 | tf_op jit(solution)/shard_map/ppermute | solution.py:344
  28.7 3.2 %queries.3 = (bf16[2,1024,256]{2,1,0:T(8,128)(2,1)S(1)}, f32[1024,512]{1,0:T(8,128)S(1)}) custom-call(bf16[1024,2048]{1,0:T(8,128)(2,1)S(1)} %get-tuple-element.31.tok, bf16[2048,512]{1,0:T(8,128)(2,1)S(1)} %get-tuple-element.32.wq, f32[128,256]{1,0:T(8,128)S(1)} %copy-done.1, bf16[4,1024,256]{2,1,0:T(8,128)(2,1)S(1)} %get-tuple-element.33.feat, ...), custom_call_target="tpu_custom_call" | custom-call | flops 300000000 | bytes 1000 | tf_op jit(solution)/shard_map/queries/pallas_call | solution.py:322
  31.9 0.7 %last.1 = (bf16[1,144,256]{2,1,0:T(8,128)(2,1)S(1)}, bf16[1,144,256]{2,1,0:T(8,128)(2,1)S(1)}, bf16[1,144,256]{2,1,0:T(8,128)(2,1)S(1)}, bf16[1,144,256]{2,1,0:T(8,128)(2,1)S(1)}) custom-call(s32[3]{0:T(128)S(1)} %pad_add_fusion.place, f32[1,136,256]{2,1,0:T(8,128)S(1)} %get-tuple-element.27.own, bf16[1,144,256]{2,1,0:T(8,128)(2,1)S(1)} %collective-permute-done.one, ...), custom_call_target="tpu_custom_call" | custom-call | flops 1000 | bytes 1000 | tf_op jit(solution)/shard_map/last/pallas_call | solution.py:322
  32.6 1.6 %collective-permute-start.6 = (bf16[1,144,256]{2,1,0:T(8,128)(2,1)S(1)}, bf16[1,144,256]{2,1,0:T(8,128)(2,1)S(1)}, u32[]{:S(2)}, u32[]{:S(2)}) collective-permute-start(bf16[1,144,256]{2,1,0:T(8,128)(2,1)S(1)} %get-tuple-element.39), channel_id=1, source_target_pairs={{0,4},{4,0},{8,12},{12,8},{16,20},{20,16},{24,28},{28,24},{1,5},{5... | collective-permute-start | bytes 221192 | tf_op jit(solution)/shard_map/ppermute | solution.py:301
  34.1 0.5 collective-permute-start.7
  34.6 1.5 %collective-permute-start.8 = (bf16[1,144,256]{2,1,0:T(8,128)(2,1)S(1)}, bf16[1,144,256]{2,1,0:T(8,128)(2,1)S(1)}, u32[]{:S(2)}, u32[]{:S(2)}) collective-permute-start(bf16[1,144,256]{2,1,0:T(8,128)(2,1)S(1)} %get-tuple-element.41), channel_id=1, source_target_pairs={{0,12},{4,8},{8,4},{12,0},{16,28},{20,24},{24,20},{28,16},{1,13},{... | collective-permute-start | bytes 221192 | tf_op jit(solution)/shard_map/ppermute | solution.py:301
  36.1 1.0 %collective-permute-done.9.far = bf16[128,2048]{1,0:T(8,128)(2,1)S(1)} collective-permute-done((bf16[128,2048]{1,0:T(8,128)(2,1)S(1)}, bf16[128,2048]{1,0:T(8,128)(2,1)S(1)}, u32[]{:S(2)}, u32[]{:S(2)}) %collective-permute-start.9) | collective-permute-done | bytes 524320 | tf_op jit(solution)/shard_map/ppermute | solution.py:301
  37.1 0.7 %join.1.refs_8_.__0_ = bf16[256,2048]{1,0:T(8,128)(2,1)S(1)} custom-call(s32[3]{0:T(128)S(1)} %pad_add_fusion.place, bf16[128,2048]{1,0:T(8,128)(2,1)S(1)} %after.3.near, bf16[128,2048]{1,0:T(8,128)(2,1)S(1)} %collective-permute-done.9.far), custom_call_target="tpu_custom_call" | custom-call | flops 1000 | bytes 1000 | tf_op jit(solution)/shard_map/join/pallas_call | solution.py:322
  37.8 0.1 collective-permute-done.6.refs_1_
  37.9 0.6 collective-permute-done.7.refs_2_
  38.5 1.4 %collective-permute-done.8.refs_3_ = bf16[1,144,256]{2,1,0:T(8,128)(2,1)S(1)} collective-permute-done((bf16[1,144,256]{2,1,0:T(8,128)(2,1)S(1)}, bf16[1,144,256]{2,1,0:T(8,128)(2,1)S(1)}, u32[]{:S(2)}, u32[]{:S(2)}) %collective-permute-start.8) | collective-permute-done | bytes 73760 | tf_op jit(solution)/shard_map/ppermute | solution.py:301
  39.8 1.4 %finish.1 = (bf16[256,512]{1,0:T(8,128)(2,1)S(1)}, bf16[256,512]{1,0:T(8,128)(2,1)S(1)}, bf16[256,512]{1,0:T(8,128)(2,1)S(1)}, bf16[256,512]{1,0:T(8,128)(2,1)S(1)}) custom-call(s32[3]{0:T(128)S(1)} %pad_add_fusion.place, bf16[1,144,256]{2,1,0:T(8,128)(2,1)S(1)} %get-tuple-element.38.refs_0_, bf16[1,144,256]{2,1,0:T(8,128)(2,1)S(1)} %collective-permute-done.6.refs_1_, ...), custom_call_target="tpu_custom_call" | custom-call | flops 1000 | bytes 1000 | tf_op jit(solution)/shard_map/finish/pallas_call | solution.py:322
  41.3 0.5 collective-permute-start.14
  41.8 0.1 collective-permute-start.15
  41.9 1.5 %collective-permute-start.11 = (bf16[256,512]{1,0:T(8,128)(2,1)S(1)}, bf16[256,512]{1,0:T(8,128)(2,1)S(1)}, u32[]{:S(2)}, u32[]{:S(2)}) collective-permute-start(bf16[256,512]{1,0:T(8,128)(2,1)S(1)} %get-tuple-element.45), channel_id=1, source_target_pairs={{0,3},{1,2},{2,1},{3,0},{4,7},{5,6},{6,5},{7,4},{8,11},{9,10},{10,... | collective-permute-start | bytes 786440 | tf_op jit(solution)/shard_map/ppermute | solution.py:301
  43.4 0.5 collective-permute-start.10
  44.0 1.9 %collective-permute-done.15.refs_1_ = bf16[256,512]{1,0:T(8,128)(2,1)S(1)} collective-permute-done((bf16[256,512]{1,0:T(8,128)(2,1)S(1)}, bf16[256,512]{1,0:T(8,128)(2,1)S(1)}, u32[]{:S(2)}, u32[]{:S(2)}) %collective-permute-start.15) | collective-permute-done | bytes 262176 | tf_op jit(solution)/shard_map/ppermute | solution.py:301
  45.8 1.3 %out.2.refs_6_ = f32[256,2048]{1,0:T(8,128)S(1)} custom-call(bf16[256,512]{1,0:T(8,128)(2,1)S(1)} %get-tuple-element.47.refs_0_, bf16[256,512]{1,0:T(8,128)(2,1)S(1)} %collective-permute-done.15.refs_1_, bf16[512,2048]{1,0:T(8,128)(2,1)S(1)} %copy-done, bf16[512,2048]{1,0:T(8,128)(2,1)S(1)} %collective-permute-done.3.rest_0_.refs_3_), custom_call_target="tpu_custom_call" | custom-call | flops 1000 | bytes 1000 | tf_op jit(solution)/shard_map/out/pallas_call | solution.py:287
  47.1 3.0 %collective-permute-done.11.refs_1_ = bf16[256,512]{1,0:T(8,128)(2,1)S(1)} collective-permute-done((bf16[256,512]{1,0:T(8,128)(2,1)S(1)}, bf16[256,512]{1,0:T(8,128)(2,1)S(1)}, u32[]{:S(2)}, u32[]{:S(2)}) %collective-permute-start.11) | collective-permute-done | bytes 262176 | tf_op jit(solution)/shard_map/ppermute | solution.py:301
  50.1 6.0 %collective-permute-done.10.refs_0_ = bf16[256,512]{1,0:T(8,128)(2,1)S(1)} collective-permute-done((bf16[256,512]{1,0:T(8,128)(2,1)S(1)}, bf16[256,512]{1,0:T(8,128)(2,1)S(1)}, u32[]{:S(2)}, u32[]{:S(2)}) %collective-permute-start.10) | collective-permute-done | bytes 262176 | tf_op jit(solution)/shard_map/ppermute | solution.py:301
  56.1 2.1 %out.3 = bf16[256,2048]{1,0:T(8,128)(2,1)} custom-call(bf16[256,512]{1,0:T(8,128)(2,1)S(1)} %collective-permute-done.10.refs_0_, bf16[256,512]{1,0:T(8,128)(2,1)S(1)} %collective-permute-done.11.refs_1_, bf16[256,2048]{1,0:T(8,128)(2,1)S(1)} %after.4.refs_2_, bf16[256,2048]{1,0:T(8,128)(2,1)S(1)} %after.5.refs_3_, ...), custom_call_target="tpu_custom_call" | custom-call | flops 1000 | bytes 1000 | tf_op jit(solution)/shard_map/out/pallas_call | solution.py:287
  (20 shorter events, 0.2 us)
Async XLA Ops:
  0.0 18.1 %collective-permute-start.3 = (bf16[512,2048]{1,0:T(8,128)(2,1)}, bf16[512,2048]{1,0:T(8,128)(2,1)S(1)}, u32[]{:S(2)}, u32[]{:S(2)}) collective-permute-start(bf16[512,2048]{1,0:T(8,128)(2,1)} %refs_2_.1), channel_id=1, source_target_pairs={{0,1},{1,0},{2,3},{3,2},{4,5},{5,4},{6,7},{7,6},{8,9},{9,8},{10,11... | collective-permute-start | bytes 6291464 | tf_op jit(solution)/shard_map/ppermute | solution.py:301
  0.5 4.3 %copy-start.2 = (bf16[2048,512]{1,0:T(8,128)(2,1)S(1)}, bf16[2048,512]{1,0:T(8,128)(2,1)}, u32[]{:S(2)}) copy-start(bf16[2048,512]{1,0:T(8,128)(2,1)} %wk.1) | copy-start | bytes 6291460
  2.2 15.9 %copy-start.1 = (f32[128,256]{1,0:T(8,128)S(1)}, f32[128,256]{1,0:T(8,128)}, u32[]{:S(2)}) copy-start(f32[128,256]{1,0:T(8,128)} %omega.5) | copy-start | bytes 393220
  2.2 21.2 %collective-permute-start.4 = (bf16[128,2048]{1,0:T(8,128)(2,1)S(1)}, bf16[128,2048]{1,0:T(8,128)(2,1)S(1)}, u32[]{:S(2)}, u32[]{:S(2)}) collective-permute-start(bf16[128,2048]{1,0:T(8,128)(2,1)S(1)} %cut.1._), channel_id=1, source_target_pairs={{0,2},{1,3},{2,0},{3,1},{4,6},{5,7},{6,4},{7,5},{8,10},{9,11},{10,... | collective-permute-start | bytes 1572872 | tf_op jit(solution)/shard_map/ppermute | solution.py:301
  14.4 26.9 %collective-permute-start.12 = (bf16[256,2048]{1,0:T(8,128)(2,1)S(1)}, bf16[256,2048]{1,0:T(8,128)(2,1)S(1)}, u32[]{:S(2)}, u32[]{:S(2)}) collective-permute-start(bf16[256,2048]{1,0:T(8,128)(2,1)S(1)} %get-tuple-element.46), channel_id=1, source_target_pairs={{0,2},{1,3},{2,0},{3,1},{4,6},{5,7},{6,4},{7,5},{8,10},{9,11},{10,... | collective-permute-start | bytes 3145736 | tf_op jit(solution)/shard_map/ppermute | solution.py:301
  14.5 6.8 %collective-permute-start = (bf16[1,144,256]{2,1,0:T(8,128)(2,1)S(1)}, bf16[1,144,256]{2,1,0:T(8,128)(2,1)S(1)}, u32[]{:S(2)}, u32[]{:S(2)}) collective-permute-start(bf16[1,144,256]{2,1,0:T(8,128)(2,1)S(1)} %get-tuple-element.28), channel_id=1, source_target_pairs={{0,4},{4,0},{8,12},{12,8},{16,20},{20,16},{24,28},{28,24},{1,5},{5... | collective-permute-start | bytes 221192 | tf_op jit(solution)/shard_map/ppermute | solution.py:301
  16.5 5.1 %collective-permute-start.1 = (bf16[1,144,256]{2,1,0:T(8,128)(2,1)S(1)}, bf16[1,144,256]{2,1,0:T(8,128)(2,1)S(1)}, u32[]{:S(2)}, u32[]{:S(2)}) collective-permute-start(bf16[1,144,256]{2,1,0:T(8,128)(2,1)S(1)} %get-tuple-element.29), channel_id=1, source_target_pairs={{0,8},{4,12},{8,0},{12,4},{16,24},{20,28},{24,16},{28,20},{1,9},{5... | collective-permute-start | bytes 221192 | tf_op jit(solution)/shard_map/ppermute | solution.py:301
  18.1 5.3 %collective-permute-start.2 = (bf16[1,144,256]{2,1,0:T(8,128)(2,1)S(1)}, bf16[1,144,256]{2,1,0:T(8,128)(2,1)S(1)}, u32[]{:S(2)}, u32[]{:S(2)}) collective-permute-start(bf16[1,144,256]{2,1,0:T(8,128)(2,1)S(1)} %get-tuple-element.30), channel_id=1, source_target_pairs={{0,12},{4,8},{8,4},{12,0},{16,28},{20,24},{24,20},{28,16},{1,13},{... | collective-permute-start | bytes 221192 | tf_op jit(solution)/shard_map/ppermute | solution.py:301
  23.4 13.7 %collective-permute-start.9 = (bf16[128,2048]{1,0:T(8,128)(2,1)S(1)}, bf16[128,2048]{1,0:T(8,128)(2,1)S(1)}, u32[]{:S(2)}, u32[]{:S(2)}) collective-permute-start(bf16[128,2048]{1,0:T(8,128)(2,1)S(1)} %after.3.near), channel_id=1, source_target_pairs={{0,4},{4,0},{8,12},{12,8},{16,20},{20,16},{24,28},{28,24},{1,5},{5... | collective-permute-start | bytes 1572872 | tf_op jit(solution)/shard_map/ppermute | solution.py:301
  24.0 7.9 %collective-permute-start.5 = (bf16[1,144,256]{2,1,0:T(8,128)(2,1)S(1)}, bf16[1,144,256]{2,1,0:T(8,128)(2,1)S(1)}, u32[]{:S(2)}, u32[]{:S(2)}) collective-permute-start(bf16[1,144,256]{2,1,0:T(8,128)(2,1)S(1)} %group.1.rest_0_.__1_), channel_id=1, source_target_pairs={{0,16},{4,20},{8,24},{12,28},{1,17},{5,21},{9,25},{13,29},{2,18},{... | collective-permute-start | bytes 221192 | tf_op jit(solution)/shard_map/ppermute | solution.py:344
  32.6 5.4 %collective-permute-start.6 = (bf16[1,144,256]{2,1,0:T(8,128)(2,1)S(1)}, bf16[1,144,256]{2,1,0:T(8,128)(2,1)S(1)}, u32[]{:S(2)}, u32[]{:S(2)}) collective-permute-start(bf16[1,144,256]{2,1,0:T(8,128)(2,1)S(1)} %get-tuple-element.39), channel_id=1, source_target_pairs={{0,4},{4,0},{8,12},{12,8},{16,20},{20,16},{24,28},{28,24},{1,5},{5... | collective-permute-start | bytes 221192 | tf_op jit(solution)/shard_map/ppermute | solution.py:301
  34.1 4.4 %collective-permute-start.7 = (bf16[1,144,256]{2,1,0:T(8,128)(2,1)S(1)}, bf16[1,144,256]{2,1,0:T(8,128)(2,1)S(1)}, u32[]{:S(2)}, u32[]{:S(2)}) collective-permute-start(bf16[1,144,256]{2,1,0:T(8,128)(2,1)S(1)} %get-tuple-element.40), channel_id=1, source_target_pairs={{0,8},{4,12},{8,0},{12,4},{16,24},{20,28},{24,16},{28,20},{1,9},{5... | collective-permute-start | bytes 221192 | tf_op jit(solution)/shard_map/ppermute | solution.py:301
  34.6 5.3 %collective-permute-start.8 = (bf16[1,144,256]{2,1,0:T(8,128)(2,1)S(1)}, bf16[1,144,256]{2,1,0:T(8,128)(2,1)S(1)}, u32[]{:S(2)}, u32[]{:S(2)}) collective-permute-start(bf16[1,144,256]{2,1,0:T(8,128)(2,1)S(1)} %get-tuple-element.41), channel_id=1, source_target_pairs={{0,12},{4,8},{8,4},{12,0},{16,28},{20,24},{24,20},{28,16},{1,13},{... | collective-permute-start | bytes 221192 | tf_op jit(solution)/shard_map/ppermute | solution.py:301
  41.2 4.6 %copy-start = (bf16[512,2048]{1,0:T(8,128)(2,1)S(1)}, bf16[512,2048]{1,0:T(8,128)(2,1)}, u32[]{:S(2)}) copy-start(bf16[512,2048]{1,0:T(8,128)(2,1)} %refs_2_.1) | copy-start | bytes 6291460
  41.2 14.9 %collective-permute-start.13 = (bf16[256,2048]{1,0:T(8,128)(2,1)S(1)}, bf16[256,2048]{1,0:T(8,128)(2,1)S(1)}, u32[]{:S(2)}, u32[]{:S(2)}) collective-permute-start(bf16[256,2048]{1,0:T(8,128)(2,1)S(1)} %after.4.refs_2_), channel_id=1, source_target_pairs={{0,1},{1,0},{2,3},{3,2},{4,5},{5,4},{6,7},{7,6},{8,9},{9,8},{10,11... | collective-permute-start | bytes 3145736 | tf_op jit(solution)/shard_map/ppermute | solution.py:301
  41.3 14.8 %collective-permute-start.14 = (bf16[256,2048]{1,0:T(8,128)(2,1)S(1)}, bf16[256,2048]{1,0:T(8,128)(2,1)S(1)}, u32[]{:S(2)}, u32[]{:S(2)}) collective-permute-start(bf16[256,2048]{1,0:T(8,128)(2,1)S(1)} %after.5.refs_3_), channel_id=1, source_target_pairs={{0,1},{1,0},{2,3},{3,2},{4,5},{5,4},{6,7},{7,6},{8,9},{9,8},{10,11... | collective-permute-start | bytes 3145736 | tf_op jit(solution)/shard_map/ppermute | solution.py:301
  41.8 4.0 %collective-permute-start.15 = (bf16[256,512]{1,0:T(8,128)(2,1)S(1)}, bf16[256,512]{1,0:T(8,128)(2,1)S(1)}, u32[]{:S(2)}, u32[]{:S(2)}) collective-permute-start(bf16[256,512]{1,0:T(8,128)(2,1)S(1)} %get-tuple-element.48), channel_id=1, source_target_pairs={{0,1},{1,0},{2,3},{3,2},{4,5},{5,4},{6,7},{7,6},{8,9},{9,8},{10,11... | collective-permute-start | bytes 786440 | tf_op jit(solution)/shard_map/ppermute | solution.py:301
  41.9 8.2 %collective-permute-start.11 = (bf16[256,512]{1,0:T(8,128)(2,1)S(1)}, bf16[256,512]{1,0:T(8,128)(2,1)S(1)}, u32[]{:S(2)}, u32[]{:S(2)}) collective-permute-start(bf16[256,512]{1,0:T(8,128)(2,1)S(1)} %get-tuple-element.45), channel_id=1, source_target_pairs={{0,3},{1,2},{2,1},{3,0},{4,7},{5,6},{6,5},{7,4},{8,11},{9,10},{10,... | collective-permute-start | bytes 786440 | tf_op jit(solution)/shard_map/ppermute | solution.py:301
  43.4 12.7 %collective-permute-start.10 = (bf16[256,512]{1,0:T(8,128)(2,1)S(1)}, bf16[256,512]{1,0:T(8,128)(2,1)S(1)}, u32[]{:S(2)}, u32[]{:S(2)}) collective-permute-start(bf16[256,512]{1,0:T(8,128)(2,1)S(1)} %get-tuple-element.44.__1_), channel_id=1, source_target_pairs={{0,2},{1,3},{2,0},{3,1},{4,6},{5,7},{6,4},{7,5},{8,10},{9,11},{10,... | collective-permute-start | bytes 786440 | tf_op jit(solution)/shard_map/ppermute | solution.py:301

commit v6 on v5

--- a/solution.py
+++ b/solution.py
@@ -371,7 +371,7 @@
     head_at = lax.axis_index("head")
     place = jnp.stack([seq_side, head_at, lax.axis_index("seq") % QUAD]).astype(jnp.int32)
 
-    depth = w_out.shape[0] // 4
+    depth = w_out.shape[0] * 7 // 32
     (part,) = local_call(
         cut_kernel,
         "cut",

time: 58.5 us -> 87.4 us (1.49)
  waiting for transfers between devices: 16 us -> 43.8 us
  starting transfers between devices: 18.2 us -> 19.4 us
    ppermute x15, waiting for transfers between devices: 16 us -> 43.7 us  [swap(): return lax.ppermute(value, axis, [(i, i ^ bit) for i in range(count)])]
    ppermute x15, starting transfers between devices: 13.5 us -> 14.7 us  [swap(): return lax.ppermute(value, axis, [(i, i ^ bit) for i in range(count)])]
  transfers between devices with their start and end apart: 16 -> 16, of which waited for: 9 -> 9; matrix products, arithmetic and copies ran while one was open for 0% -> 0% of each run, Pallas kernels for 37% -> 25%
where the time goes in v6:
time: 87.4 us; the launch traced here: 87.3 us
  waiting for transfers between devices  43.8 us (50%)
  Pallas kernels  23.7 us (27%)
  starting transfers between devices  19.4 us (22%)
    ppermute x15, waiting for transfers between devices, swap(): return lax.ppermute(value, axis, [(i, i ^ bit) for i in range(count)])  43.7 us
    pallas_call x8, Pallas kernels, local_call(): pl.pallas_call(kernel, in_specs=specs, out_specs=[VMEM] * len(outs), out_...  20.4 us
    ppermute x15, starting transfers between devices, swap(): return lax.ppermute(value, axis, [(i, i ^ bit) for i in range(count)])  14.7 us
    ppermute x1, starting transfers between devices, prefix(): lax.ppermute(message, 'seq', [(i, i + step) for i in range(count - step)])  4.67 us
    pallas_call x2, Pallas kernels, out_product(): pl.pallas_call(functools.partial(out_kernel, len(rights[0])), in_specs=[V...  3.29 us
  transfers between devices with their start and end apart: 16, of which 9 were waited for; matrix products, arithmetic and copies ran while one was open for 0% of the time, Pallas kernels for 25%

profile of v6, /device:TPU:0, one launch (start us, length us, event | category | flops | bytes accessed | tf_op | source)
XLA Modules:
  0.0 87.3 jit_solution(4050081622025266720)
XLA Ops:
  0.0 0.5 collective-permute-start.3
  0.5 1.6 %cut.1._ = bf16[112,2048]{1,0:T(8,128)(2,1)S(1)} custom-call(s32[3]{0:T(128)S(1)} %pad_add_fusion.place, bf16[512,2048]{1,0:T(8,128)(2,1)} %refs_2_.1), custom_call_target="tpu_custom_call" | custom-call | flops 1000 | bytes 1000 | tf_op jit(solution)/shard_map/cut/pallas_call | solution.py:322
  2.2 9.7 %keys.1 = (bf16[1024,2048]{1,0:T(8,128)(2,1)S(1)}, bf16[2048,512]{1,0:T(8,128)(2,1)S(1)}, bf16[4,1024,256]{2,1,0:T(8,128)(2,1)S(1)}, bf16[1024,512]{1,0:T(8,128)...) custom-call(s32[3]{0:T(128)S(1)} %pad_add_fusion.place, ...), custom_call_target="tpu_custom_call" | custom-call | flops 10000000000 | bytes 1000 | tf_op jit(solution)/shard_map/keys/pallas_call | solution.py:322
  11.8 2.6 %collective-permute-start.12 = (bf16[288,2048]{1,0:T(8,128)(2,1)S(1)}, bf16[288,2048]{1,0:T(8,128)(2,1)S(1)}, u32[]{:S(2)}, u32[]{:S(2)}) collective-permute-start(bf16[288,2048]{1,0:T(8,128)(2,1)S(1)} %get-tuple-element.46), channel_id=1, source_target_pairs={{0,2},{1,3},{2,0},{3,1},{4,6},{5,7},{6,4},{7,5},{8,10},{9,11},{10,... | collective-permute-start | bytes 3538952 | tf_op jit(solution)/shard_map/ppermute | solution.py:301
  14.4 0.1 collective-permute-start.4
  14.5 2.0 %collective-permute-start = (bf16[1,144,256]{2,1,0:T(8,128)(2,1)S(1)}, bf16[1,144,256]{2,1,0:T(8,128)(2,1)S(1)}, u32[]{:S(2)}, u32[]{:S(2)}) collective-permute-start(bf16[1,144,256]{2,1,0:T(8,128)(2,1)S(1)} %get-tuple-element.28), channel_id=1, source_target_pairs={{0,4},{4,0},{8,12},{12,8},{16,20},{20,16},{24,28},{28,24},{1,5},{5... | collective-permute-start | bytes 221192 | tf_op jit(solution)/shard_map/ppermute | solution.py:301
  16.4 1.6 %collective-permute-start.1 = (bf16[1,144,256]{2,1,0:T(8,128)(2,1)S(1)}, bf16[1,144,256]{2,1,0:T(8,128)(2,1)S(1)}, u32[]{:S(2)}, u32[]{:S(2)}) collective-permute-start(bf16[1,144,256]{2,1,0:T(8,128)(2,1)S(1)} %get-tuple-element.29), channel_id=1, source_target_pairs={{0,8},{4,12},{8,0},{12,4},{16,24},{20,28},{24,16},{28,20},{1,9},{5... | collective-permute-start | bytes 221192 | tf_op jit(solution)/shard_map/ppermute | solution.py:301
  18.0 3.2 %queries.2 = (bf16[2,1024,256]{2,1,0:T(8,128)(2,1)S(1)}, f32[1024,512]{1,0:T(8,128)S(1)}) custom-call(bf16[1024,2048]{1,0:T(8,128)(2,1)S(1)} %get-tuple-element.31.tok, bf16[2048,512]{1,0:T(8,128)(2,1)S(1)} %get-tuple-element.32.wq, f32[128,256]{1,0:T(8,128)S(1)} %copy-done.1, bf16[4,1024,256]{2,1,0:T(8,128)(2,1)S(1)} %get-tuple-element.33.feat, ...), custom_call_target="tpu_custom_call" | custom-call | flops 300000000 | bytes 1000 | tf_op jit(solution)/shard_map/queries/pallas_call | solution.py:322
  21.2 0.3 collective-permute-done.1.two
  21.5 1.7 %collective-permute-done.2.three = bf16[1,144,256]{2,1,0:T(8,128)(2,1)S(1)} collective-permute-done((bf16[1,144,256]{2,1,0:T(8,128)(2,1)S(1)}, bf16[1,144,256]{2,1,0:T(8,128)(2,1)S(1)}, u32[]{:S(2)}, u32[]{:S(2)}) %collective-permute-start.2) | collective-permute-done | bytes 73760 | tf_op jit(solution)/shard_map/ppermute | solution.py:301
  23.3 27.6 %collective-permute-done.4._2.__0_ = bf16[112,2048]{1,0:T(8,128)(2,1)S(1)} collective-permute-done((bf16[112,2048]{1,0:T(8,128)(2,1)S(1)}, bf16[112,2048]{1,0:T(8,128)(2,1)S(1)}, u32[]{:S(2)}, u32[]{:S(2)}) %collective-permute-start.4) | collective-permute-done | bytes 458784 | tf_op jit(solution)/shard_map/ppermute | solution.py:301
  50.9 1.8 %collective-permute-start.9 = (bf16[112,2048]{1,0:T(8,128)(2,1)S(1)}, bf16[112,2048]{1,0:T(8,128)(2,1)S(1)}, u32[]{:S(2)}, u32[]{:S(2)}) collective-permute-start(bf16[112,2048]{1,0:T(8,128)(2,1)S(1)} %after.3.near), channel_id=1, source_target_pairs={{0,4},{4,0},{8,12},{12,8},{16,20},{20,16},{24,28},{28,24},{1,5},{5... | collective-permute-start | bytes 1376264 | tf_op jit(solution)/shard_map/ppermute | solution.py:301
  52.8 4.7 %collective-permute-start.5 = (bf16[1,144,256]{2,1,0:T(8,128)(2,1)S(1)}, bf16[1,144,256]{2,1,0:T(8,128)(2,1)S(1)}, u32[]{:S(2)}, u32[]{:S(2)}) collective-permute-start(bf16[1,144,256]{2,1,0:T(8,128)(2,1)S(1)} %group.1.rest_0_.__1_), channel_id=1, source_target_pairs={{0,16},{4,20},{8,24},{12,28},{1,17},{5,21},{9,25},{13,29},{2,18},{... | collective-permute-start | bytes 221192 | tf_op jit(solution)/shard_map/ppermute | solution.py:344
  57.4 3.2 %queries.3 = (bf16[2,1024,256]{2,1,0:T(8,128)(2,1)S(1)}, f32[1024,512]{1,0:T(8,128)S(1)}) custom-call(bf16[1024,2048]{1,0:T(8,128)(2,1)S(1)} %get-tuple-element.31.tok, bf16[2048,512]{1,0:T(8,128)(2,1)S(1)} %get-tuple-element.32.wq, f32[128,256]{1,0:T(8,128)S(1)} %copy-done.1, bf16[4,1024,256]{2,1,0:T(8,128)(2,1)S(1)} %get-tuple-element.33.feat, ...), custom_call_target="tpu_custom_call" | custom-call | flops 300000000 | bytes 1000 | tf_op jit(solution)/shard_map/queries/pallas_call | solution.py:322
  60.6 0.7 last.1
  61.3 0.6 collective-permute-start.6
  61.9 1.6 %collective-permute-start.7 = (bf16[1,144,256]{2,1,0:T(8,128)(2,1)S(1)}, bf16[1,144,256]{2,1,0:T(8,128)(2,1)S(1)}, u32[]{:S(2)}, u32[]{:S(2)}) collective-permute-start(bf16[1,144,256]{2,1,0:T(8,128)(2,1)S(1)} %get-tuple-element.40), channel_id=1, source_target_pairs={{0,8},{4,12},{8,0},{12,4},{16,24},{20,28},{24,16},{28,20},{1,9},{5... | collective-permute-start | bytes 221192 | tf_op jit(solution)/shard_map/ppermute | solution.py:301
  63.5 1.4 %collective-permute-start.8 = (bf16[1,144,256]{2,1,0:T(8,128)(2,1)S(1)}, bf16[1,144,256]{2,1,0:T(8,128)(2,1)S(1)}, u32[]{:S(2)}, u32[]{:S(2)}) collective-permute-start(bf16[1,144,256]{2,1,0:T(8,128)(2,1)S(1)} %get-tuple-element.41), channel_id=1, source_target_pairs={{0,12},{4,8},{8,4},{12,0},{16,28},{20,24},{24,20},{28,16},{1,13},{... | collective-permute-start | bytes 221192 | tf_op jit(solution)/shard_map/ppermute | solution.py:301
  64.9 0.7 join.1.refs_8_.__0_
  65.5 1.0 %collective-permute-done.6.refs_1_ = bf16[1,144,256]{2,1,0:T(8,128)(2,1)S(1)} collective-permute-done((bf16[1,144,256]{2,1,0:T(8,128)(2,1)S(1)}, bf16[1,144,256]{2,1,0:T(8,128)(2,1)S(1)}, u32[]{:S(2)}, u32[]{:S(2)}) %collective-permute-start.6) | collective-permute-done | bytes 73760 | tf_op jit(solution)/shard_map/ppermute | solution.py:301
  66.5 0.3 collective-permute-done.7.refs_2_
  66.9 1.9 %collective-permute-done.8.refs_3_ = bf16[1,144,256]{2,1,0:T(8,128)(2,1)S(1)} collective-permute-done((bf16[1,144,256]{2,1,0:T(8,128)(2,1)S(1)}, bf16[1,144,256]{2,1,0:T(8,128)(2,1)S(1)}, u32[]{:S(2)}, u32[]{:S(2)}) %collective-permute-start.8) | collective-permute-done | bytes 73760 | tf_op jit(solution)/shard_map/ppermute | solution.py:301
  68.7 1.4 %finish.1 = (bf16[256,512]{1,0:T(8,128)(2,1)S(1)}, bf16[256,512]{1,0:T(8,128)(2,1)S(1)}, bf16[256,512]{1,0:T(8,128)(2,1)S(1)}, bf16[256,512]{1,0:T(8,128)(2,1)S(1)}) custom-call(s32[3]{0:T(128)S(1)} %pad_add_fusion.place, bf16[1,144,256]{2,1,0:T(8,128)(2,1)S(1)} %get-tuple-element.38.refs_0_, bf16[1,144,256]{2,1,0:T(8,128)(2,1)S(1)} %collective-permute-done.6.refs_1_, ...), custom_call_target="tpu_custom_call" | custom-call | flops 1000 | bytes 1000 | tf_op jit(solution)/shard_map/finish/pallas_call | solution.py:322
  70.2 0.5 collective-permute-start.13
  70.7 0.1 collective-permute-start.15
  70.8 1.5 %collective-permute-start.11 = (bf16[256,512]{1,0:T(8,128)(2,1)S(1)}, bf16[256,512]{1,0:T(8,128)(2,1)S(1)}, u32[]{:S(2)}, u32[]{:S(2)}) collective-permute-start(bf16[256,512]{1,0:T(8,128)(2,1)S(1)} %get-tuple-element.45), channel_id=1, source_target_pairs={{0,3},{1,2},{2,1},{3,0},{4,7},{5,6},{6,5},{7,4},{8,11},{9,10},{10,... | collective-permute-start | bytes 786440 | tf_op jit(solution)/shard_map/ppermute | solution.py:301
  72.4 0.5 collective-permute-start.10
  72.9 1.9 %collective-permute-done.15.refs_1_ = bf16[256,512]{1,0:T(8,128)(2,1)S(1)} collective-permute-done((bf16[256,512]{1,0:T(8,128)(2,1)S(1)}, bf16[256,512]{1,0:T(8,128)(2,1)S(1)}, u32[]{:S(2)}, u32[]{:S(2)}) %collective-permute-start.15) | collective-permute-done | bytes 262176 | tf_op jit(solution)/shard_map/ppermute | solution.py:301
  74.8 1.2 %out.2.refs_6_ = f32[256,2048]{1,0:T(8,128)S(1)} custom-call(bf16[256,512]{1,0:T(8,128)(2,1)S(1)} %get-tuple-element.47.refs_0_, bf16[256,512]{1,0:T(8,128)(2,1)S(1)} %collective-permute-done.15.refs_1_, bf16[512,2048]{1,0:T(8,128)(2,1)S(1)} %copy-done, bf16[512,2048]{1,0:T(8,128)(2,1)S(1)} %collective-permute-done.3.rest_0_.refs_3_), custom_call_target="tpu_custom_call" | custom-call | flops 1000 | bytes 1000 | tf_op jit(solution)/shard_map/out/pallas_call | solution.py:287
  76.0 3.0 %collective-permute-done.11.refs_1_ = bf16[256,512]{1,0:T(8,128)(2,1)S(1)} collective-permute-done((bf16[256,512]{1,0:T(8,128)(2,1)S(1)}, bf16[256,512]{1,0:T(8,128)(2,1)S(1)}, u32[]{:S(2)}, u32[]{:S(2)}) %collective-permute-start.11) | collective-permute-done | bytes 262176 | tf_op jit(solution)/shard_map/ppermute | solution.py:301
  79.0 6.0 %collective-permute-done.10.refs_0_ = bf16[256,512]{1,0:T(8,128)(2,1)S(1)} collective-permute-done((bf16[256,512]{1,0:T(8,128)(2,1)S(1)}, bf16[256,512]{1,0:T(8,128)(2,1)S(1)}, u32[]{:S(2)}, u32[]{:S(2)}) %collective-permute-start.10) | collective-permute-done | bytes 262176 | tf_op jit(solution)/shard_map/ppermute | solution.py:301
  85.1 2.1 %out.3 = bf16[256,2048]{1,0:T(8,128)(2,1)} custom-call(bf16[256,512]{1,0:T(8,128)(2,1)S(1)} %collective-permute-done.10.refs_0_, bf16[256,512]{1,0:T(8,128)(2,1)S(1)} %collective-permute-done.11.refs_1_, bf16[224,2048]{1,0:T(8,128)(2,1)S(1)} %after.4.refs_2_, bf16[288,2048]{1,0:T(8,128)(2,1)S(1)} %after.5.refs_3_, ...), custom_call_target="tpu_custom_call" | custom-call | flops 1000 | bytes 1000 | tf_op jit(solution)/shard_map/out/pallas_call | solution.py:287
  (20 shorter events, 0.2 us)
Async XLA Ops:
  0.0 18.0 %collective-permute-start.3 = (bf16[512,2048]{1,0:T(8,128)(2,1)}, bf16[512,2048]{1,0:T(8,128)(2,1)S(1)}, u32[]{:S(2)}, u32[]{:S(2)}) collective-permute-start(bf16[512,2048]{1,0:T(8,128)(2,1)} %refs_2_.1), channel_id=1, source_target_pairs={{0,1},{1,0},{2,3},{3,2},{4,5},{5,4},{6,7},{7,6},{8,9},{9,8},{10,11... | collective-permute-start | bytes 6291464 | tf_op jit(solution)/shard_map/ppermute | solution.py:301
  0.5 1.7 %copy-start.2 = (bf16[2048,512]{1,0:T(8,128)(2,1)S(1)}, bf16[2048,512]{1,0:T(8,128)(2,1)}, u32[]{:S(2)}) copy-start(bf16[2048,512]{1,0:T(8,128)(2,1)} %wk.1) | copy-start | bytes 6291460
  2.2 15.9 %copy-start.1 = (f32[128,256]{1,0:T(8,128)S(1)}, f32[128,256]{1,0:T(8,128)}, u32[]{:S(2)}) copy-start(f32[128,256]{1,0:T(8,128)} %omega.5) | copy-start | bytes 393220
  11.8 58.3 %collective-permute-start.12 = (bf16[288,2048]{1,0:T(8,128)(2,1)S(1)}, bf16[288,2048]{1,0:T(8,128)(2,1)S(1)}, u32[]{:S(2)}, u32[]{:S(2)}) collective-permute-start(bf16[288,2048]{1,0:T(8,128)(2,1)S(1)} %get-tuple-element.46), channel_id=1, source_target_pairs={{0,2},{1,3},{2,0},{3,1},{4,6},{5,7},{6,4},{7,5},{8,10},{9,11},{10,... | collective-permute-start | bytes 3538952 | tf_op jit(solution)/shard_map/ppermute | solution.py:301
  14.4 36.5 %collective-permute-start.4 = (bf16[112,2048]{1,0:T(8,128)(2,1)S(1)}, bf16[112,2048]{1,0:T(8,128)(2,1)S(1)}, u32[]{:S(2)}, u32[]{:S(2)}) collective-permute-start(bf16[112,2048]{1,0:T(8,128)(2,1)S(1)} %cut.1._), channel_id=1, source_target_pairs={{0,2},{1,3},{2,0},{3,1},{4,6},{5,7},{6,4},{7,5},{8,10},{9,11},{10,... | collective-permute-start | bytes 1376264 | tf_op jit(solution)/shard_map/ppermute | solution.py:301
  14.5 6.7 %collective-permute-start = (bf16[1,144,256]{2,1,0:T(8,128)(2,1)S(1)}, bf16[1,144,256]{2,1,0:T(8,128)(2,1)S(1)}, u32[]{:S(2)}, u32[]{:S(2)}) collective-permute-start(bf16[1,144,256]{2,1,0:T(8,128)(2,1)S(1)} %get-tuple-element.28), channel_id=1, source_target_pairs={{0,4},{4,0},{8,12},{12,8},{16,20},{20,16},{24,28},{28,24},{1,5},{5... | collective-permute-start | bytes 221192 | tf_op jit(solution)/shard_map/ppermute | solution.py:301
  16.4 5.1 %collective-permute-start.1 = (bf16[1,144,256]{2,1,0:T(8,128)(2,1)S(1)}, bf16[1,144,256]{2,1,0:T(8,128)(2,1)S(1)}, u32[]{:S(2)}, u32[]{:S(2)}) collective-permute-start(bf16[1,144,256]{2,1,0:T(8,128)(2,1)S(1)} %get-tuple-element.29), channel_id=1, source_target_pairs={{0,8},{4,12},{8,0},{12,4},{16,24},{20,28},{24,16},{28,20},{1,9},{5... | collective-permute-start | bytes 221192 | tf_op jit(solution)/shard_map/ppermute | solution.py:301
  18.0 5.3 %collective-permute-start.2 = (bf16[1,144,256]{2,1,0:T(8,128)(2,1)S(1)}, bf16[1,144,256]{2,1,0:T(8,128)(2,1)S(1)}, u32[]{:S(2)}, u32[]{:S(2)}) collective-permute-start(bf16[1,144,256]{2,1,0:T(8,128)(2,1)S(1)} %get-tuple-element.30), channel_id=1, source_target_pairs={{0,12},{4,8},{8,4},{12,0},{16,28},{20,24},{24,20},{28,16},{1,13},{... | collective-permute-start | bytes 221192 | tf_op jit(solution)/shard_map/ppermute | solution.py:301
  50.9 14.0 %collective-permute-start.9 = (bf16[112,2048]{1,0:T(8,128)(2,1)S(1)}, bf16[112,2048]{1,0:T(8,128)(2,1)S(1)}, u32[]{:S(2)}, u32[]{:S(2)}) collective-permute-start(bf16[112,2048]{1,0:T(8,128)(2,1)S(1)} %after.3.near), channel_id=1, source_target_pairs={{0,4},{4,0},{8,12},{12,8},{16,20},{20,16},{24,28},{28,24},{1,5},{5... | collective-permute-start | bytes 1376264 | tf_op jit(solution)/shard_map/ppermute | solution.py:301
  52.8 7.9 %collective-permute-start.5 = (bf16[1,144,256]{2,1,0:T(8,128)(2,1)S(1)}, bf16[1,144,256]{2,1,0:T(8,128)(2,1)S(1)}, u32[]{:S(2)}, u32[]{:S(2)}) collective-permute-start(bf16[1,144,256]{2,1,0:T(8,128)(2,1)S(1)} %group.1.rest_0_.__1_), channel_id=1, source_target_pairs={{0,16},{4,20},{8,24},{12,28},{1,17},{5,21},{9,25},{13,29},{2,18},{... | collective-permute-start | bytes 221192 | tf_op jit(solution)/shard_map/ppermute | solution.py:344
  61.3 5.2 %collective-permute-start.6 = (bf16[1,144,256]{2,1,0:T(8,128)(2,1)S(1)}, bf16[1,144,256]{2,1,0:T(8,128)(2,1)S(1)}, u32[]{:S(2)}, u32[]{:S(2)}) collective-permute-start(bf16[1,144,256]{2,1,0:T(8,128)(2,1)S(1)} %get-tuple-element.39), channel_id=1, source_target_pairs={{0,4},{4,0},{8,12},{12,8},{16,20},{20,16},{24,28},{28,24},{1,5},{5... | collective-permute-start | bytes 221192 | tf_op jit(solution)/shard_map/ppermute | solution.py:301
  61.9 5.0 %collective-permute-start.7 = (bf16[1,144,256]{2,1,0:T(8,128)(2,1)S(1)}, bf16[1,144,256]{2,1,0:T(8,128)(2,1)S(1)}, u32[]{:S(2)}, u32[]{:S(2)}) collective-permute-start(bf16[1,144,256]{2,1,0:T(8,128)(2,1)S(1)} %get-tuple-element.40), channel_id=1, source_target_pairs={{0,8},{4,12},{8,0},{12,4},{16,24},{20,28},{24,16},{28,20},{1,9},{5... | collective-permute-start | bytes 221192 | tf_op jit(solution)/shard_map/ppermute | solution.py:301
  63.5 5.3 %collective-permute-start.8 = (bf16[1,144,256]{2,1,0:T(8,128)(2,1)S(1)}, bf16[1,144,256]{2,1,0:T(8,128)(2,1)S(1)}, u32[]{:S(2)}, u32[]{:S(2)}) collective-permute-start(bf16[1,144,256]{2,1,0:T(8,128)(2,1)S(1)} %get-tuple-element.41), channel_id=1, source_target_pairs={{0,12},{4,8},{8,4},{12,0},{16,28},{20,24},{24,20},{28,16},{1,13},{... | collective-permute-start | bytes 221192 | tf_op jit(solution)/shard_map/ppermute | solution.py:301
  70.1 4.6 %copy-start = (bf16[512,2048]{1,0:T(8,128)(2,1)S(1)}, bf16[512,2048]{1,0:T(8,128)(2,1)}, u32[]{:S(2)}) copy-start(bf16[512,2048]{1,0:T(8,128)(2,1)} %refs_2_.1) | copy-start | bytes 6291460
  70.2 14.9 %collective-permute-start.14 = (bf16[288,2048]{1,0:T(8,128)(2,1)S(1)}, bf16[288,2048]{1,0:T(8,128)(2,1)S(1)}, u32[]{:S(2)}, u32[]{:S(2)}) collective-permute-start(bf16[288,2048]{1,0:T(8,128)(2,1)S(1)} %after.5.refs_3_), channel_id=1, source_target_pairs={{0,1},{1,0},{2,3},{3,2},{4,5},{5,4},{6,7},{7,6},{8,9},{9,8},{10,11... | collective-permute-start | bytes 3538952 | tf_op jit(solution)/shard_map/ppermute | solution.py:301
  70.2 14.8 %collective-permute-start.13 = (bf16[224,2048]{1,0:T(8,128)(2,1)S(1)}, bf16[224,2048]{1,0:T(8,128)(2,1)S(1)}, u32[]{:S(2)}, u32[]{:S(2)}) collective-permute-start(bf16[224,2048]{1,0:T(8,128)(2,1)S(1)} %after.4.refs_2_), channel_id=1, source_target_pairs={{0,1},{1,0},{2,3},{3,2},{4,5},{5,4},{6,7},{7,6},{8,9},{9,8},{10,11... | collective-permute-start | bytes 2752520 | tf_op jit(solution)/shard_map/ppermute | solution.py:301
  70.7 4.0 %collective-permute-start.15 = (bf16[256,512]{1,0:T(8,128)(2,1)S(1)}, bf16[256,512]{1,0:T(8,128)(2,1)S(1)}, u32[]{:S(2)}, u32[]{:S(2)}) collective-permute-start(bf16[256,512]{1,0:T(8,128)(2,1)S(1)} %get-tuple-element.48), channel_id=1, source_target_pairs={{0,1},{1,0},{2,3},{3,2},{4,5},{5,4},{6,7},{7,6},{8,9},{9,8},{10,11... | collective-permute-start | bytes 786440 | tf_op jit(solution)/shard_map/ppermute | solution.py:301
  70.8 8.2 %collective-permute-start.11 = (bf16[256,512]{1,0:T(8,128)(2,1)S(1)}, bf16[256,512]{1,0:T(8,128)(2,1)S(1)}, u32[]{:S(2)}, u32[]{:S(2)}) collective-permute-start(bf16[256,512]{1,0:T(8,128)(2,1)S(1)} %get-tuple-element.45), channel_id=1, source_target_pairs={{0,3},{1,2},{2,1},{3,0},{4,7},{5,6},{6,5},{7,4},{8,11},{9,10},{10,... | collective-permute-start | bytes 786440 | tf_op jit(solution)/shard_map/ppermute | solution.py:301
  72.4 12.7 %collective-permute-start.10 = (bf16[256,512]{1,0:T(8,128)(2,1)S(1)}, bf16[256,512]{1,0:T(8,128)(2,1)S(1)}, u32[]{:S(2)}, u32[]{:S(2)}) collective-permute-start(bf16[256,512]{1,0:T(8,128)(2,1)S(1)} %get-tuple-element.44.__1_), channel_id=1, source_target_pairs={{0,2},{1,3},{2,0},{3,1},{4,6},{5,7},{6,4},{7,5},{8,10},{9,11},{10,... | collective-permute-start | bytes 786440 | tf_op jit(solution)/shard_map/ppermute | solution.py:301
